TPU v7x, 256 devices: a whole 4x4x8 slice. The times are simulated.
256 devices in a mesh: seq: 64 (over z, x, core), head: 4 (over y).
Axes of the slice: x: 4, y: 4, z: 8, core: 2. Of those that a mesh axis runs over, the one named last changes fastest.
Arguments:
- tokens: bfloat16 [32768, 1024], P('seq'), may hold values from -40 to 40
- query_weight: bfloat16 [1024, 1024], P(None, 'head'), may hold values from -0.1875 to 0.1875
- key_weight: bfloat16 [1024, 1024], P(None, 'head'), may hold values from -0.1875 to 0.1875
- value_weight: bfloat16 [1024, 1024], P(None, 'head'), may hold values from -0.1875 to 0.1875
- out_weight: bfloat16 [1024, 1024], P('head'), may hold values from -0.1875 to 0.1875
- level_gate: int32 [256, 16], P('seq'), may hold values 0 or 1
Outputs:
- mixed: bfloat16 [32768, 1024], P('seq', 'head')
All inputs are finite; a program needn't handle non-finite values. No bound on the sum of `level_gate` on one device may be relied on, other than what follows from the above.
Results may differ from a plain program's by a relative error of at most 0.012.
The roundings to bfloat16 on the way count: a program that leaves them out, or rounds other values in their place, can miss the bound.
Values may be sent and summed in bfloat16 or wider, within the bound.
No kernel may reach another device: no remote copies, remote signals or barrier semaphores. Data moves between devices by JAX's collectives and lax.ppermute only.
A program may use at most 128 MiB of HBM per device.

v0:
```python
import math

import jax
import jax.numpy as jnp
import numpy as np
from jax import lax
from jax.sharding import PartitionSpec as P

HEAD_DIM = 64
BLOCK = 128


LOG_TWO = math.log(2.0)
NEG_FILL = -1e30


def pool_pair(paired, level):
    count = paired.shape[1] >> level
    shaped = paired.reshape(2, count, 1 << level, paired.shape[2])
    return jnp.mean(shaped, axis=2, dtype=jnp.float32).astype(jnp.bfloat16)


def shards(tokens, query_weight, key_weight, value_weight, out_weight, level_gate):
    query = jnp.dot(tokens, query_weight, preferred_element_type=jnp.float32).astype(jnp.bfloat16)
    keys = jnp.dot(tokens, key_weight, preferred_element_type=jnp.float32).astype(jnp.bfloat16)
    values = jnp.dot(tokens, value_weight, preferred_element_type=jnp.float32).astype(jnp.bfloat16)
    rows_dev, width = query.shape
    blocks_dev = rows_dev // BLOCK
    local_levels = blocks_dev.bit_length() - 1
    seq_count = lax.axis_size("seq")
    cross_levels = seq_count.bit_length() - 1
    device = lax.axis_index("seq")
    paired = jnp.stack([keys, values])
    block_ids = np.arange(blocks_dev)
    gate_live = level_gate == 1
    pieces = [paired.reshape(2, blocks_dev, BLOCK, width)]
    live_cols = []
    for level in range(local_levels):
        pooled = pool_pair(paired, level).reshape(2, blocks_dev >> level, BLOCK, width)
        sibling = np.maximum((block_ids >> level) - 1, 0)
        pieces.append(pooled[:, sibling])
        upper_bits = block_ids >> level & 1 == 1
        live_cols.append(jnp.logical_and(jnp.asarray(upper_bits), gate_live[:, level]))
    own_top = [pool_pair(paired, local_levels + step) for step in range(cross_levels)]
    siblings = []
    sizes = [piece.shape[1] for piece in own_top]
    stacked = jnp.concatenate(own_top, axis=1)
    gathered = lax.all_gather(stacked, "seq", axis=1, tiled=True)
    whole = gathered.reshape(2, seq_count, stacked.shape[1], width)
    offset = 0
    for step in range(cross_levels):
        part_rows = whole[:, :, offset : offset + sizes[step]]
        start = jnp.maximum((device >> step) - 1 << step, 0)
        chosen = lax.dynamic_slice_in_dim(part_rows, start, 1 << step, 1)
        siblings.append(chosen.reshape(2, BLOCK, width))
        offset += sizes[step]
    for step in range(cross_levels):
        pieces.append(jnp.broadcast_to(siblings[step][:, None], (2, blocks_dev, BLOCK, width)))
        bit_set = device >> step & 1 == 1
        live_cols.append(jnp.logical_and(bit_set, gate_live[:, local_levels + step]))
    levels_all = local_levels + cross_levels
    key_sets = jnp.concatenate(pieces, axis=2)
    key_total = key_sets.shape[2]
    level_bias = jnp.stack(
        [
            jnp.where(live_cols[level], level * LOG_TWO, NEG_FILL).astype(jnp.float32)
            for level in range(levels_all)
        ],
        axis=1,
    )
    positions = jnp.arange(BLOCK, dtype=jnp.int32)
    causal = jnp.where(positions[None, :] <= positions[:, None], 0.0, NEG_FILL).astype(jnp.float32)
    group = min(4, blocks_dev)
    heads_dev = width // HEAD_DIM
    query_blocks = query.reshape(blocks_dev // group, group, BLOCK, heads_dev, HEAD_DIM)
    split_sets = key_sets.reshape(2, blocks_dev // group, group, key_total, heads_dev, HEAD_DIM)
    bias_blocks = level_bias.reshape(blocks_dev // group, group, levels_all)

    def attend(inputs):
        rows, key_rows, value_rows, biases = inputs
        scores = (
            jnp.einsum("gqhd,gkhd->ghqk", rows, key_rows, preferred_element_type=jnp.float32)
            * 0.125
        )
        spread = jnp.repeat(biases, BLOCK, axis=1)
        full_bias = jnp.concatenate(
            [
                jnp.broadcast_to(causal, (group, BLOCK, BLOCK)),
                jnp.broadcast_to(spread[:, None, :], (group, BLOCK, levels_all * BLOCK)),
            ],
            axis=2,
        )
        scores = scores + full_bias[:, None]
        top = jnp.max(scores, axis=-1, keepdims=True)
        expo = jnp.exp(scores - top)
        total = jnp.sum(expo, axis=-1, keepdims=True)
        weights = (expo / total).astype(jnp.bfloat16)
        result = jnp.einsum(
            "ghqk,gkhd->gqhd", weights, value_rows, preferred_element_type=jnp.float32
        )
        return result.astype(jnp.bfloat16).reshape(group * BLOCK, width)

    attended = lax.map(attend, (query_blocks, split_sets[0], split_sets[1], bias_blocks)).reshape(
        rows_dev, width
    )
    partial_value = jnp.dot(attended, out_weight, preferred_element_type=jnp.float32)
    return lax.psum_scatter(partial_value, "head", scatter_dimension=1, tiled=True).astype(
        jnp.bfloat16
    )


def solution(mesh):
    placed = (
        P("seq", None),
        P(None, "head"),
        P(None, "head"),
        P(None, "head"),
        P("head", None),
        P("seq", None),
    )
    return jax.shard_map(
        shards, mesh=mesh, in_specs=placed, out_specs=P("seq", "head"), check_vma=False
    )
```

profile of v0, /device:TPU:32, one launch (start us, length us, event | category | flops | bytes accessed | tf_op | source)
XLA Modules:
  0.0 203.6 jit_solution(9132994075747899889)
XLA Ops:
  6.5 1.2 copy-done
  7.8 1.5 convolution_convert_fusion.2
  9.3 1.5 convolution_convert_fusion.1
  12.6 1.0 copy.37
  15.8 1.1 reshape.120
  17.5 1.4 convert_reduce_fusion.6
  21.6 1.6 pad_maximum_fusion
  23.1 90.7 %all-gather.2.cloned.1.call-done = bf16[2,16128,256]{2,0,1:T(2,128)(2,1)} async-done(((bf16[2,252,256]{2,0,1:T(2,128)(2,1)}), bf16[2,16128,256]{2,0,1:T(2,128)(2,1)}) %all-gather.2.cloned.1.call-update) | async-done | bytes 16515088 | tf_op jit(solution)/shard_map/all_gather | solution.py:48
  113.9 8.1 %slice.70 = bf16[2,64,128,256]{3,0,2,1:T(2,128)(2,1)} slice(bf16[2,64,252,256]{3,0,2,1:T(2,128)(2,1)} %bitcast.68), slice={[0:2], [0:64], [0:128], [0:256]} | slice | bytes 16777216 | tf_op jit(solution)/shard_map/slice | solution.py:52
  121.9 5.8 %slice.71 = bf16[2,64,64,256]{3,0,2,1:T(2,128)(2,1)S(1)} slice(bf16[2,64,252,256]{3,0,2,1:T(2,128)(2,1)} %bitcast.69), slice={[0:2], [0:64], [128:192], [0:256]} | slice | bytes 8388608 | tf_op jit(solution)/shard_map/slice | solution.py:52
  127.8 3.5 %slice.72 = bf16[2,64,32,256]{3,0,2,1:T(2,128)(2,1)S(1)} slice(bf16[2,64,252,256]{3,0,2,1:T(2,128)(2,1)} %bitcast.70), slice={[0:2], [0:64], [192:224], [0:256]} | slice | bytes 4194304 | tf_op jit(solution)/shard_map/slice | solution.py:52
  131.3 2.1 %slice.73 = bf16[2,64,16,256]{3,0,2,1:T(2,128)(2,1)S(1)} slice(bf16[2,64,252,256]{3,0,2,1:T(2,128)(2,1)} %bitcast.71), slice={[0:2], [0:64], [224:240], [0:256]} | slice | bytes 2097152 | tf_op jit(solution)/shard_map/slice | solution.py:52
  133.5 1.4 slice.74
  134.9 1.1 slice.75
  136.1 1.0 constant_dynamic-slice_fusion.5
  138.0 1.8 fusion.31
  139.8 4.3 %copy.41 = bf16[1,4,1152,256]{2,3,1,0:T(8,128)(2,1)} copy(bf16[1,4,1152,256]{3,2,0,1:T(8,128)(2,1)} %get-tuple-element.17) | data formatting | bytes 4718592 | tf_op jit(solution)/shard_map/slice | solution.py:103
  144.1 2.6 %copy.39 = bf16[1,4,1152,256]{2,3,1,0:T(8,128)(2,1)} copy(bf16[1,4,1152,256]{3,2,0,1:T(8,128)(2,1)S(1)} %get-tuple-element.18) | data formatting | bytes 4718592 | tf_op jit(solution)/shard_map/slice | solution.py:103
  146.7 5.5 %fusion.32 = f32[4,4,128]{2,1,0:T(4,128)S(1)} fusion(f32[4,128,1152]{2,1,0:T(8,128)} %pad_maximum_fusion, bf16[4,1152,4,64]{1,3,2,0:T(8,128)(2,1)} %bitcast.76, bf16[4,128,4,64]{3,2,1,0:T(4,128)(2,1)} %reshape.120), kind=kOutput, calls=%fused_computation.81 | convolution fusion | flops 311428224 | bytes 4988928 | tf_op jit(solution)/shard_map/while/body/eval_jaxpr/sub | solution.py:95
  152.2 7.5 %fusion.8 = bf16[4,128,4,64]{1,3,2,0:T(8,128)(2,1)} fusion(bf16[4,1152,4,64]{1,3,2,0:T(8,128)(2,1)} %bitcast.78, f32[4,4,128]{2,1,0:T(4,128)S(1)} %fusion.32, f32[4,128,1152]{2,1,0:T(8,128)} %pad_maximum_fusion, bf16[4,1152,4,64]{1,3,2,0:T(8,128)(2,1)S(1)} %bitcast.77, bf16[4,128,4,64]{3,2,1,0:T(4,128)(2,1)} %reshape.120), kind=kOutput, calls=%fused_computation.16 | convolution fusion | flops 615910528 | bytes 7610368 | tf_op jit(solution)/shard_map/while/body/eval_jaxpr/ghqk,gkhd->gqhd/dot_general | solution.py:98
  159.7 1.2 copy.43
  160.9 2.9 %fusion.15 = f32[512,1024]{1,0:T(8,128)} fusion(bf16[256,1024]{1,0:T(8,128)(2,1)} %param.16, bf16[32,8,4,128]{3,2,1,0:T(4,128)(2,1)S(1)} %bitcast.80), kind=kOutput, calls=%fused_computation.31 | convolution fusion | flops 268435456 | bytes 2883584 | tf_op jit(solution)/shard_map/dot_general | solution.py:106
  163.7 31.3 %reduce-scatter.2.cloned.1.call-done = f32[512,256]{1,0:T(8,128)} async-done(((f32[512,1024]{1,0:T(8,128)}), f32[512,256]{1,0:T(8,128)}) %reduce-scatter.2.cloned.1.call-update) | async-done | bytes 524304 | tf_op jit(solution)/shard_map/reduce_scatter | solution.py:107
  195.0 1.8 convert_element_type.97
  (73 shorter events, 7.9 us)
Async XLA Ops:
  6.5 1.2 copy-start
  6.5 107.3 %all-gather.2.cloned.1.call-start = ((), (), s32[]{:S(2)}) async-start(), calls=%async_computation.1 | async-start | bytes 16773120 | tf_op jit(solution)/shard_map/all_gather | solution.py:48
  10.8 4.3 %copy-start.2 = (s32[4,16]{1,0:T(4,128)S(1)}, s32[4,16]{1,0:T(4,128)}, u32[]{:S(2)}) copy-start(s32[4,16]{1,0:T(4,128)} %param.17) | copy-start | bytes 772
  10.8 4.3 %copy-start.4 = (pred[4,1]{1,0:T(4,128)(4,1)S(1)}, pred[4,1]{1,0:T(4,128)(4,1)}, u32[]{:S(2)}) copy-start(pred[4,1]{1,0:T(4,128)(4,1)} %constant.113) | copy-start | bytes 16
  10.8 4.3 %copy-start.5 = (pred[4,1]{1,0:T(4,128)(4,1)S(1)}, pred[4,1]{1,0:T(4,128)(4,1)}, u32[]{:S(2)}) copy-start(pred[4,1]{1,0:T(4,128)(4,1)} %constant.114) | copy-start | bytes 16
  10.8 4.6 %copy-start.6 = (bf16[1024,256]{1,0:T(8,128)(2,1)S(1)}, bf16[1024,256]{1,0:T(8,128)(2,1)}, u32[]{:S(2)}) copy-start(bf16[1024,256]{1,0:T(8,128)(2,1)} %param.13) | copy-start | bytes 1572868
  12.2 4.7 %copy-start.3 = (s32[4]{0:T(128)S(1)}, s32[4]{0:T(128)}, u32[]{:S(2)}) copy-start(s32[4]{0:T(128)} %constant.115) | copy-start | bytes 52
  13.6 181.4 %reduce-scatter.2.cloned.1.call-start = ((), (), s32[]{:S(2)}) async-start(), calls=%async_computation.2 | async-start | bytes 2621440 | tf_op jit(solution)/shard_map/reduce_scatter | solution.py:107
  121.9 15.8 %slice-start = ((s8[4718592]{0:T(1024)(128)(4,1)}), s8[524288]{0:T(1024)(128)(4,1)S(1)}, s32[]{:S(2)}) async-start(s8[4718592]{0:T(1024)(128)(4,1)} %bitcast.74), calls=%async_computation.3 | async-start | bytes 1048576
  127.8 10.0 %slice-start.1 = ((s8[4718592]{0:T(1024)(128)(4,1)}), s8[4194304]{0:T(1024)(128)(4,1)S(1)}, s32[]{:S(2)}) async-start(s8[4718592]{0:T(1024)(128)(4,1)} %bitcast.74), calls=%async_computation.4 | async-start | bytes 8388608
  146.7 5.5 %copy-start.1 = (bf16[1,4,1152,256]{2,3,1,0:T(8,128)(2,1)S(1)}, bf16[1,4,1152,256]{2,3,1,0:T(8,128)(2,1)}, u32[]{:S(2)}) copy-start(bf16[1,4,1152,256]{2,3,1,0:T(8,128)(2,1)} %copy.41) | copy-start | bytes 7077892
Sparse Core Ops, SparseCore 0:
  13.8 100.0 all-gather.1
  163.9 31.1 reduce-scatter.1
where the time goes:
time: 205 us; the launch traced here: 204 us
  waiting for transfers between devices  122 us (60%)
  local copies, waits for them, and re-layouts  40.7 us (20%)
  matrix products  19.2 us (9%)
  between operations  13.9 us (7%)
  other arithmetic  7.48 us (4%)
    all_gather x1, waiting for transfers between devices, shards(): gathered = lax.all_gather(stacked, 'seq', axis=1, tiled=True)  90.7 us
    reduce_scatter x1, waiting for transfers between devices, shards(): lax.psum_scatter(partial_value, 'head', scatter_dimension=1, tiled=True)  31.3 us
    slice x6, local copies, waits for them, and re-layouts, shards(): part_rows = whole[:, :, offset:offset + sizes[step]]  22.2 us
    dot_general x1, matrix products, attend(): jnp.einsum('ghqk,gkhd->gqhd', weights, value_rows, preferred_element_type...  7.51 us
    slice x2, local copies, waits for them, and re-layouts, shards(): split_sets[0]  6.1 us
    sub x1, matrix products, attend(): expo = jnp.exp(scores - top)  5.47 us
  transfers between devices with their start and end apart: 2, of which 2 were waited for; matrix products, arithmetic and copies ran while one was open for 4% of the time, Pallas kernels for 0%

commit v1 on v0

v1 whole, which is shorter than its diff:
```python
import functools
import math

import jax
import jax.numpy as jnp
from jax import lax
from jax.experimental import pallas as pl
from jax.experimental.pallas import tpu as pltpu
from jax.sharding import PartitionSpec as P

LOG_TWO = math.log(2.0)
NEG = -1e30
BLOCK = 128
WIDTH = 256
HEADS = 4
F32 = jnp.float32
BF16 = jnp.bfloat16

Z, X, C = 8, 4, 2


def index(z, x, c):
    return (z % Z) * 8 + (x % X) * 2 + c


CHIPS = [(z, x, c) for z in range(Z) for x in range(X) for c in range(C)]


def dot(a, b):
    return lax.dot_general(a, b, (((1,), (0,)), ((), ())), preferred_element_type=F32)


def pool_rows(rows, level):
    token = lax.broadcasted_iota(jnp.int32, (rows, 512), 1)
    row = lax.broadcasted_iota(jnp.int32, (rows, 512), 0)
    inverse = jnp.float32(0.0)
    for each in range(1, 8):
        inverse = jnp.where(level == each, jnp.float32(2.0**-each), inverse)
    hit = lax.shift_right_logical(token, jnp.full((rows, 512), level, jnp.int32)) == row
    return jnp.where(hit, inverse, 0.0).astype(BF16)


def blocks_kernel(tok, mean):
    mean[...] = jnp.zeros(mean.shape, F32)
    for b in range(4):
        part = tok[b * BLOCK : (b + 1) * BLOCK, :].astype(F32)
        mean[b : b + 1, :] = jnp.sum(part, axis=0, keepdims=True) * (1.0 / BLOCK)


def keys_kernel(tok, wk, wv, kv, l1, s0, e1, z3, z4):
    keys = dot(tok[...], wk[...]).astype(BF16)
    values = dot(tok[...], wv[...]).astype(BF16)
    both = jnp.concatenate([keys, values], axis=1)
    kv[...] = both
    parts = [pool_rows(n, level) for n, level in ((128, 2), (128, 1), (64, 3), (32, 4), (16, 5), (16, 6))]
    pooled = dot(jnp.concatenate(parts, axis=0), both)
    s0[...] = pooled[0:128].astype(BF16)
    l1[...] = pooled[128:256].astype(BF16)
    e1[...] = pooled[256:352].astype(BF16)
    z3[...] = pooled[352:368].astype(BF16)
    z4[...] = pooled[368:384].astype(BF16)


def far_rows_kernel(mean, wk, wv, z4, out):
    high = mean[...].astype(BF16)
    low = (mean[...] - high.astype(F32)).astype(BF16)
    both = jnp.concatenate([high.astype(F32), low.astype(F32)], axis=0).astype(BF16)
    for w, cols in ((wk, slice(0, WIDTH)), (wv, slice(WIDTH, 2 * WIDTH))):
        rows = dot(both, w[...])
        own = z4[:, cols].astype(F32)
        out[:, cols] = jnp.concatenate([own[:8], rows[:8] + rows[8:]], axis=0).astype(BF16)


def joint_kernel(z3, sent, got, out):
    sent, got = sent[...].astype(F32), got[...].astype(F32)
    last = jnp.concatenate([got[:8], sent[8:12], got[8:12]], axis=0).astype(BF16)
    out[0:16, :] = z3[...]
    out[16:32, :] = last


def far_join_kernel(sent, got, out):
    mine, other = sent[16:32, :].astype(F32), got[16:32, :].astype(F32)
    out[0:16, :] = got[0:16, :]
    out[16:32, :] = jnp.concatenate([mine[:8], other[:8]], axis=0).astype(BF16)
    out[32:48, :] = jnp.concatenate([mine[8:], other[8:]], axis=0).astype(BF16)


def near_join_kernel(sent, got, out):
    out[0:32, :] = sent[64:96, :]
    out[32:64, :] = got[64:96, :]


def plane_join_kernel(s0, first, second, out):
    out[0:128, :] = s0[...]
    out[128:192, :] = first[0:64, :]
    out[192:256, :] = second[...]


def row_join_kernel(a, b, c, d, out):
    for step, piece in enumerate((a, b, c, d)):
        out[step * 48 : (step + 1) * 48, :] = piece[...]


def stack_heads(query_t):
    head = lax.broadcasted_iota(jnp.int32, (WIDTH, BLOCK), 0) // 64
    zero = jnp.zeros_like(query_t)
    return jnp.concatenate([jnp.where(head == h, query_t, zero) for h in range(HEADS)], axis=1)


def pick_heads(stacked):
    return jnp.concatenate(
        [stacked[h * 64 : (h + 1) * 64, h * BLOCK : (h + 1) * BLOCK] for h in range(HEADS)], axis=0
    )


def spread_heads(row):
    return jnp.concatenate(
        [jnp.broadcast_to(row[:, h * BLOCK : (h + 1) * BLOCK], (64, BLOCK)) for h in range(HEADS)],
        axis=0,
    )


def turn(array):
    return array.astype(F32).T.astype(BF16)


def gate_bias(gate, block, level):
    return jnp.where(gate[block, level] == 1, jnp.float32(level * LOG_TWO), jnp.float32(NEG))


def four(array):
    return jnp.concatenate([array] * 4, axis=1)


def own_kernel(gate, tok, wq, kv, l1, qt, acc, ml):
    query = dot(tok[...], wq[...]).astype(BF16).astype(F32) * 0.125
    query_t = query.T.astype(BF16)
    qt[...] = query_t
    key = lax.broadcasted_iota(jnp.int32, (BLOCK, BLOCK), 0)
    row = lax.broadcasted_iota(jnp.int32, (BLOCK, BLOCK), 1)
    causal = jnp.where(key <= row, 0.0, NEG).astype(F32)
    values_t = turn(kv[:, WIDTH:])
    l1_t = turn(l1[:, WIDTH:])
    for b in range(4):
        rows = slice(b * BLOCK, (b + 1) * BLOCK)
        keys = [kv[rows, :WIDTH]]
        values = [values_t[:, rows]]
        bias = [causal]
        if b & 1:
            before = slice((b - 1) * BLOCK, b * BLOCK)
            keys.append(kv[before, :WIDTH])
            values.append(values_t[:, before])
            bias.append(jnp.full((BLOCK, BLOCK), gate_bias(gate, b, 0)))
        if b & 2:
            keys.append(l1[:, :WIDTH])
            values.append(l1_t)
            bias.append(jnp.full((BLOCK, BLOCK), gate_bias(gate, b, 1)))
        scores = dot(jnp.concatenate(keys, axis=0), stack_heads(query_t[:, rows]))
        scores = scores + four(jnp.concatenate(bias, axis=0))
        top = jnp.max(scores, axis=0, keepdims=True)
        expo = jnp.exp(scores - top)
        ml[b : b + 1, :] = top
        ml[4 + b : 5 + b, :] = jnp.sum(expo, axis=0, keepdims=True)
        acc[:, rows] = pick_heads(dot(jnp.concatenate(values, axis=1), expo.astype(BF16)))


def plane_levels():
    seq = lax.axis_index("seq")
    have = [jnp.where(lax.shift_right_logical(seq, bit) % 2 == 1, 2 + bit, -1) for bit in range(3)]
    spot = lax.broadcasted_iota(jnp.int32, (384, BLOCK), 0)
    return jnp.where(spot < 128, have[0], jnp.where(spot % 128 < 64, have[1], have[2]))


def far_levels():
    z = lax.axis_index("seq") // 8
    spot = lax.broadcasted_iota(jnp.int32, (384, BLOCK), 0) % 48
    have = [jnp.where(lax.shift_right_logical(z, bit) % 2 == 1, 5 + bit, -1) for bit in range(3)]
    return jnp.where(spot < 16, have[0], jnp.where(spot < 32, have[1], have[2]))


def bias_rows(gate, block, levels, used):
    bias = jnp.full(levels.shape, NEG, F32)
    for level in used:
        bias = jnp.where(levels == level, gate_bias(gate, block, level), bias)
    return four(bias)


def cross(b, qt, acc, ml, keys, values_t, bias):
    rows = slice(b * BLOCK, (b + 1) * BLOCK)
    old_top, old_total = ml[b : b + 1, :], ml[4 + b : 5 + b, :]
    scores = dot(keys, stack_heads(qt[:, rows])) + bias
    top = jnp.maximum(old_top, jnp.max(scores, axis=0, keepdims=True))
    expo = jnp.exp(scores - top)
    scale = jnp.exp(old_top - top)
    total = old_total * scale + jnp.sum(expo, axis=0, keepdims=True)
    out = pick_heads(dot(values_t, expo.astype(BF16)))
    return acc[:, rows] * spread_heads(scale) + out, top, total


def plane_kernel(gate, qt, acc, ml, first, second, other, acc_out, ml_out):
    pieces = [other[0:128, :], first[0:64, :], second[...], other[128:256, :]]
    keys = jnp.concatenate([piece[:, :WIDTH] for piece in pieces], axis=0)
    values_t = turn(jnp.concatenate([piece[:, WIDTH:] for piece in pieces], axis=0))
    levels = plane_levels()
    for b in range(4):
        bias = bias_rows(gate, b, levels, (2, 3, 4))
        out, top, total = cross(b, qt, acc, ml, keys, values_t, bias)
        acc_out[:, b * BLOCK : (b + 1) * BLOCK] = out
        ml_out[b : b + 1, :] = top
        ml_out[4 + b : 5 + b, :] = total


def far_kernel(half, gate, qt, acc, ml, mine, other, att):
    keys = jnp.concatenate([mine[:, :WIDTH], other[:, :WIDTH]], axis=0)
    values_t = turn(jnp.concatenate([mine[:, WIDTH:], other[:, WIDTH:]], axis=0))
    levels = far_levels()
    for step in range(2):
        b = half * 2 + step
        bias = bias_rows(gate, b, levels, (5, 6, 7))
        out, _, total = cross(b, qt, acc, ml, keys, values_t, bias)
        att[step * BLOCK : (step + 1) * BLOCK, :] = (out / spread_heads(total)).T.astype(BF16)


def project_kernel(half, mine_att, peer_att, mine_w, peer_w, keep, send):
    head = lax.axis_index("head")
    other = (3 - head) if half == 0 else (head + 1 - 2 * (head % 2))
    for where, ref in ((other, send), (head, keep)):
        cols = pl.ds(pl.multiple_of(where * WIDTH, WIDTH), WIDTH)
        total = dot(mine_att[...], mine_w[:, cols]) + dot(peer_att[...], peer_w[:, cols])
        ref[...] = total.astype(ref.dtype)


VMEM = pl.BlockSpec(memory_space=pltpu.VMEM)
SMEM = pl.BlockSpec(memory_space=pltpu.SMEM)


def call(kernel, args, outs, flops, smem=0):
    return pl.pallas_call(
        kernel,
        out_shape=[jax.ShapeDtypeStruct(shape, dtype) for shape, dtype in outs],
        in_specs=[SMEM] * smem + [VMEM] * (len(args) - smem),
        out_specs=[VMEM] * len(outs),
        compiler_params=pltpu.CompilerParams(vmem_limit_bytes=24 * 1024 * 1024),
        cost_estimate=pl.CostEstimate(flops=flops, bytes_accessed=1000, transcendentals=0),
    )(*args)


def move(array, pairs):
    return lax.ppermute(array, "seq", pairs)


def plane(array, to):
    return move(array, [(index(z, x, c), index(to(z), x, c)) for z, x, c in CHIPS])


def along(array, shift):
    return move(array, [(index(z, x, c), index(z, x + shift, c)) for z, x, c in CHIPS])


def across(array, bit):
    return move(array, [(index(z, x, c), index(z, x ^ bit, c)) for z, x, c in CHIPS])


def swap(array):
    return move(array, [(index(z, x, c), index(z, x, 1 - c)) for z, x, c in CHIPS])


PAIR_NEXT = [(0, 1), (1, 0), (2, 3), (3, 2)]
PAIR_FAR = [(0, 3), (3, 0), (1, 2), (2, 1)]


def shards(tokens, wq, wk, wv, wo, gate):
    rows = lambda n: ((n, 2 * WIDTH), BF16)
    (mean,) = call(blocks_kernel, (tokens,), [((8, 1024), F32)], 2 * 10**8)
    mean_up = plane(mean, lambda z: 7 - z)
    kv, l1, s0, e1, z3, z4 = call(
        keys_kernel,
        (tokens, wk, wv),
        [rows(512), rows(128), rows(128), rows(96), rows(16), rows(16)],
        10**9,
    )
    wo_next = lax.ppermute(wo, "head", PAIR_NEXT)
    wo_far = lax.ppermute(wo, "head", PAIR_FAR)
    first = across(e1, 1)
    (pay,) = call(near_join_kernel, (e1, first), [rows(64)], 10**8)
    second = across(pay, 2)
    (pay,) = call(plane_join_kernel, (s0, first, second), [rows(256)], 10**8)
    other = swap(pay)
    qt, acc, ml = call(
        own_kernel,
        (gate, tokens, wq, kv, l1),
        [((WIDTH, 512), BF16), ((WIDTH, 512), F32), ((8, 512), F32)],
        3 * 10**9,
        smem=1,
    )
    (pay,) = call(far_rows_kernel, (mean_up, wk, wv, z4), [rows(16)], 2 * 10**8)
    got = plane(pay, lambda z: z ^ 2)
    (pay,) = call(joint_kernel, (z3, pay, got), [rows(32)], 10**8)
    got = plane(pay, lambda z: z ^ 1)
    (far,) = call(far_join_kernel, (pay, got), [rows(48)], 10**8)
    others = [along(far, shift) for shift in (1, -1, 2)]
    (far,) = call(row_join_kernel, (far, *others), [rows(192)], 10**8)
    far_other = swap(far)
    acc, ml = call(
        plane_kernel,
        (gate, qt, acc, ml, first, second, other),
        [((WIDTH, 512), F32), ((8, 512), F32)],
        3 * 10**9,
        smem=1,
    )
    halves = []
    for half in range(2):
        (att,) = call(
            functools.partial(far_kernel, half),
            (gate, qt, acc, ml, far, far_other),
            [((256, WIDTH), BF16)],
            2 * 10**9,
            smem=1,
        )
        halves.append(att)
    out = []
    pairs = (PAIR_NEXT, PAIR_FAR)
    for half in range(2):
        peer = lax.ppermute(halves[half], "head", pairs[half])
        keep, send = call(
            functools.partial(project_kernel, half),
            (halves[half], peer, wo, (wo_next, wo_far)[half]),
            [((256, WIDTH), F32), ((256, WIDTH), BF16)],
            10**8,
        )
        out.append(keep + lax.ppermute(send, "head", pairs[1 - half]).astype(F32))
    return jnp.concatenate(out, axis=0).astype(BF16)


def solution(mesh):
    placed = (
        P("seq", None),
        P(None, "head"),
        P(None, "head"),
        P(None, "head"),
        P("head", None),
        P("seq", None),
    )
    return jax.shard_map(
        shards, mesh=mesh, in_specs=placed, out_specs=P("seq", "head"), check_vma=False
    )
```

time: 205 us -> 56.5 us (0.28)
  waiting for transfers between devices: 122 us -> 15.1 us
  local copies, waits for them, and re-layouts: 40.7 us -> 3.89 us
  starting transfers between devices: 0.22 us -> 24.1 us
  matrix products: 19.2 us -> 0 us
  between operations: 13.9 us -> 0.18 us
  Pallas kernels: 0 us -> 11.6 us
  other arithmetic: 7.48 us -> 0.79 us
    all_gather x1 -> x0, waiting for transfers between devices: 90.7 us -> none  [shards(): gathered = lax.all_gather(stacked, 'seq', axis=1, tiled=True)]
    reduce_scatter x1 -> x0, waiting for transfers between devices: 31.3 us -> none  [shards(): lax.psum_scatter(partial_value, 'head', scatter_dimension=1, tiled=True)]
    slice x9 -> x0, local copies, waits for them, and re-layouts: 30.8 us -> none  [the longest x6 22.2 us: shards(): part_rows = whole[:, :, offset:offset + sizes[step]]]
    ppermute x0 -> x16, starting transfers between devices: none -> 24.1 us  [the longest x10 17 us: move(): return lax.ppermute(array, 'seq', pairs)]
    ppermute x0 -> x16, waiting for transfers between devices: none -> 15.1 us  [the longest x2 5.23 us: shards(): peer = lax.ppermute(halves[half], 'head', pairs[half])]
    dot_general x5 -> x0, matrix products: 13.8 us -> none  [the longest x1 7.51 us: attend(): jnp.einsum('ghqk,gkhd->gqhd', weights, value_rows, preferred_element_type...]
    pallas_call x0 -> x14, Pallas kernels: none -> 11.6 us  [call(): pl.pallas_call(kernel, out_shape=[jax.ShapeDtypeStruct(shape, dtype) for...]
    sub x1 -> x0, matrix products: 5.47 us -> none  [attend(): expo = jnp.exp(scores - top)]
  transfers between devices with their start and end apart: 2 -> 16, of which waited for: 2 -> 8; matrix products, arithmetic and copies ran while one was open for 4% -> 0% of each run, Pallas kernels for 0% -> 19%
where the time goes in v1:
time: 56.5 us; the launch traced here: 55.6 us
  starting transfers between devices  24.1 us (43%)
  waiting for transfers between devices  15.1 us (27%)
  Pallas kernels  11.6 us (21%)
  local copies, waits for them, and re-layouts  3.89 us (7%)
  other arithmetic  0.79 us (1%)
    ppermute x10, starting transfers between devices, move(): return lax.ppermute(array, 'seq', pairs)  17 us
    pallas_call x14, Pallas kernels, call(): pl.pallas_call(kernel, out_shape=[jax.ShapeDtypeStruct(shape, dtype) for...  11.6 us
    ppermute x2, waiting for transfers between devices, shards(): peer = lax.ppermute(halves[half], 'head', pairs[half])  5.23 us
    ppermute x10, waiting for transfers between devices, move(): return lax.ppermute(array, 'seq', pairs)  4.64 us
    ppermute x2, waiting for transfers between devices, shards(): out.append(keep + lax.ppermute(send, 'head', pairs[1 - half]).astype(F32))  4.57 us
    unnamed x18, local copies, waits for them, and re-layouts  3.89 us
    ppermute x1, starting transfers between devices, shards(): wo_far = lax.ppermute(wo, 'head', PAIR_FAR)  3.09 us
    ppermute x1, starting transfers between devices, shards(): wo_next = lax.ppermute(wo, 'head', PAIR_NEXT)  1.58 us
  transfers between devices with their start and end apart: 16, of which 8 were waited for; matrix products, arithmetic and copies ran while one was open for 0% of the time, Pallas kernels for 19%

profile of v1, /device:TPU:32, one launch (start us, length us, event | category | flops | bytes accessed | tf_op | source)
XLA Modules:
  0.0 55.6 jit_solution(8527199101742881865)
XLA Ops:
  0.0 1.2 %copy-done.1 = bf16[512,1024]{1,0:T(8,128)(2,1)S(1)} copy-done((bf16[512,1024]{1,0:T(8,128)(2,1)S(1)}, bf16[512,1024]{1,0:T(8,128)(2,1)}, u32[]{:S(2)}) %copy-start.1) | copy-done | bytes 1048600
  1.2 1.0 %copy-done.3 = bf16[1024,256]{1,0:T(8,128)(2,1)S(1)} copy-done((bf16[1024,256]{1,0:T(8,128)(2,1)S(1)}, bf16[1024,256]{1,0:T(8,128)(2,1)}, u32[]{:S(2)}) %copy-start.3) | copy-done | bytes 524312
  2.3 1.0 %copy-done.5 = bf16[1024,256]{1,0:T(8,128)(2,1)S(1)} copy-done((bf16[1024,256]{1,0:T(8,128)(2,1)S(1)}, bf16[1024,256]{1,0:T(8,128)(2,1)}, u32[]{:S(2)}) %copy-start.5) | copy-done | bytes 524312
  3.3 1.0 %shard_map.64 = (bf16[512,512]{1,0:T(8,128)(2,1)S(1)}, bf16[128,512]{1,0:T(8,128)(2,1)S(1)}, bf16[128,512]{1,0:T(8,128)(2,1)S(1)}, bf16[96,512]{1,0:T(8,128)(2,1...) custom-call(bf16[512,1024]{1,0:T(8,128)(2,1)S(1)} %copy-done.1, bf16[1024,256]{1,0:T(8,128)(2,1)S(1)} %copy-done.3, ...), custom_call_target="tpu_custom_call" | custom-call | flops 1000000000 | bytes 1000 | tf_op jit(solution)/shard_map/pallas_call | solution.py:238
  4.3 1.6 %collective-permute-start = (bf16[96,512]{1,0:T(8,128)(2,1)S(1)}, bf16[96,512]{1,0:T(8,128)(2,1)S(1)}, u32[]{:S(2)}, u32[]{:S(2)}) collective-permute-start(bf16[96,512]{1,0:T(8,128)(2,1)S(1)} %get-tuple-element.25.sent), channel_id=1, source_target_pairs={{0,8},{4,12},{8,0},{12,4},{16,24},{20,28},{24,16},{28,20},{32,40},... | collective-permute-start | bytes 294920 | tf_op jit(solution)/shard_map/ppermute | solution.py:249
  6.1 5.9 %collective-permute-start.3 = (f32[8,1024]{1,0:T(8,128)S(1)}, f32[8,1024]{1,0:T(8,128)S(1)}, u32[]{:S(2)}, u32[]{:S(2)}) collective-permute-start(f32[8,1024]{1,0:T(8,128)S(1)} %shard_map.69), channel_id=1, source_target_pairs={{0,224},{4,228},{8,232},{12,236},{16,240},{20,244},{24,248},{28,25... | collective-permute-start | bytes 98312 | tf_op jit(solution)/shard_map/ppermute | solution.py:249
  12.0 1.9 %collective-permute-done.3.mean = f32[8,1024]{1,0:T(8,128)S(1)} collective-permute-done((f32[8,1024]{1,0:T(8,128)S(1)}, f32[8,1024]{1,0:T(8,128)S(1)}, u32[]{:S(2)}, u32[]{:S(2)}) %collective-permute-start.3) | collective-permute-done | bytes 32800 | tf_op jit(solution)/shard_map/ppermute | solution.py:249
  14.9 2.8 %collective-permute-start.1 = (bf16[64,512]{1,0:T(8,128)(2,1)S(1)}, bf16[64,512]{1,0:T(8,128)(2,1)S(1)}, u32[]{:S(2)}, u32[]{:S(2)}) collective-permute-start(bf16[64,512]{1,0:T(8,128)(2,1)S(1)} %shard_map.66), channel_id=1, source_target_pairs={{0,16},{4,20},{8,24},{12,28},{16,0},{20,4},{24,8},{28,12},{32,48},... | collective-permute-start | bytes 196616 | tf_op jit(solution)/shard_map/ppermute | solution.py:249
  17.7 1.2 %collective-permute-done.4.got = bf16[16,512]{1,0:T(8,128)(2,1)S(1)} collective-permute-done((bf16[16,512]{1,0:T(8,128)(2,1)S(1)}, bf16[16,512]{1,0:T(8,128)(2,1)S(1)}, u32[]{:S(2)}, u32[]{:S(2)}) %collective-permute-start.4) | collective-permute-done | bytes 16416 | tf_op jit(solution)/shard_map/ppermute | solution.py:249
  18.9 0.8 %collective-permute-start.5 = (bf16[32,512]{1,0:T(8,128)(2,1)S(1)}, bf16[32,512]{1,0:T(8,128)(2,1)S(1)}, u32[]{:S(2)}, u32[]{:S(2)}) collective-permute-start(bf16[32,512]{1,0:T(8,128)(2,1)S(1)} %shard_map.71.sent), channel_id=1, source_target_pairs={{0,32},{4,36},{8,40},{12,44},{16,48},{20,52},{24,56},{28,60},{32,0... | collective-permute-start | bytes 98312 | tf_op jit(solution)/shard_map/ppermute | solution.py:249
  19.8 1.6 %collective-permute-start.11 = (bf16[256,1024]{1,0:T(8,128)(2,1)S(1)}, bf16[256,1024]{1,0:T(8,128)(2,1)S(1)}, u32[]{:S(2)}, u32[]{:S(2)}) collective-permute-start(bf16[256,1024]{1,0:T(8,128)(2,1)S(1)} %copy-done), channel_id=1, source_target_pairs={{0,1},{1,0},{2,3},{3,2},{4,5},{5,4},{6,7},{7,6},{8,9},{9,8},{10,11... | collective-permute-start | bytes 1572872 | tf_op jit(solution)/shard_map/ppermute | solution.py:282
  21.3 1.6 %collective-permute-done.5.got = bf16[32,512]{1,0:T(8,128)(2,1)S(1)} collective-permute-done((bf16[32,512]{1,0:T(8,128)(2,1)S(1)}, bf16[32,512]{1,0:T(8,128)(2,1)S(1)}, u32[]{:S(2)}, u32[]{:S(2)}) %collective-permute-start.5) | collective-permute-done | bytes 32800 | tf_op jit(solution)/shard_map/ppermute | solution.py:249
  23.5 2.7 %collective-permute-start.7 = (bf16[48,512]{1,0:T(8,128)(2,1)S(1)}, bf16[48,512]{1,0:T(8,128)(2,1)S(1)}, u32[]{:S(2)}, u32[]{:S(2)}) collective-permute-start(bf16[48,512]{1,0:T(8,128)(2,1)S(1)} %shard_map.72.a), channel_id=1, source_target_pairs={{0,24},{4,28},{8,0},{12,4},{16,8},{20,12},{24,16},{28,20},{32,56},... | collective-permute-start | bytes 147464 | tf_op jit(solution)/shard_map/ppermute | solution.py:249
  26.2 1.5 %collective-permute-start.8 = (bf16[48,512]{1,0:T(8,128)(2,1)S(1)}, bf16[48,512]{1,0:T(8,128)(2,1)S(1)}, u32[]{:S(2)}, u32[]{:S(2)}) collective-permute-start(bf16[48,512]{1,0:T(8,128)(2,1)S(1)} %shard_map.72.a), channel_id=1, source_target_pairs={{0,16},{4,20},{8,24},{12,28},{16,0},{20,4},{24,8},{28,12},{32,48},... | collective-permute-start | bytes 147464 | tf_op jit(solution)/shard_map/ppermute | solution.py:249
  28.4 2.8 %shard_map.65 = (bf16[256,512]{1,0:T(8,128)(2,1)S(1)}, f32[256,512]{1,0:T(8,128)S(1)}, f32[8,512]{1,0:T(8,128)S(1)}) custom-call(s32[4,16]{1,0:T(4,128)S(1)} %copy-done.8, bf16[512,1024]{1,0:T(8,128)(2,1)S(1)} %copy-done.2, bf16[1024,256]{1,0:T(8,128)(2,1)S(1)} %copy-done.7, bf16[512,512]{1,0:T(8,128)(2,1)S(1)} %get-tuple-element.20.kv, ...), custom_call_target="tpu_custom_call" | custom-call | flops 3000000000 | bytes 1000 | tf_op jit(solution)/shard_map/pallas_call | solution.py:238
  31.2 3.1 %collective-permute-start.14 = (bf16[256,1024]{1,0:T(8,128)(2,1)S(1)}, bf16[256,1024]{1,0:T(8,128)(2,1)S(1)}, u32[]{:S(2)}, u32[]{:S(2)}) collective-permute-start(bf16[256,1024]{1,0:T(8,128)(2,1)S(1)} %copy-done), channel_id=1, source_target_pairs={{0,3},{3,0},{1,2},{2,1},{4,7},{7,4},{5,6},{6,5},{8,11},{11,8},{9,1... | collective-permute-start | bytes 1572872 | tf_op jit(solution)/shard_map/ppermute | solution.py:283
  34.7 2.8 %shard_map.68 = (f32[256,512]{1,0:T(8,128)S(1)}, f32[8,512]{1,0:T(8,128)S(1)}) custom-call(s32[4,16]{1,0:T(4,128)S(1)} %copy-done.8, bf16[256,512]{1,0:T(8,128)(2,1)S(1)} %get-tuple-element.22.qt, f32[256,512]{1,0:T(8,128)S(1)} %get-tuple-element.23.acc, f32[8,512]{1,0:T(8,128)S(1)} %get-tuple-element.24.ml, ...), custom_call_target="tpu_custom_call" | custom-call | flops 3000000000 | bytes 1000 | tf_op jit(solution)/shard_map/pallas_call | solution.py:238
  37.5 1.9 %shard_map.74.mine_att = bf16[256,256]{1,0:T(8,128)(2,1)S(1)} custom-call(s32[4,16]{1,0:T(4,128)S(1)} %copy-done.8, bf16[256,512]{1,0:T(8,128)(2,1)S(1)} %get-tuple-element.22.qt, f32[256,512]{1,0:T(8,128)S(1)} %get-tuple-element.27.acc, f32[8,512]{1,0:T(8,128)S(1)} %get-tuple-element.28.ml, bf16[192,512]{1,0:T(8,128)(2,1)S(1)} %shard_map.73.mine, ...), custom_call_target="tpu_custom_call" | custom-call | flops 2000000000 | bytes 1000 | tf_op jit(solution)/shard_map/pallas_call | solution.py:238
  39.6 1.9 %shard_map.76.mine_att = bf16[256,256]{1,0:T(8,128)(2,1)S(1)} custom-call(s32[4,16]{1,0:T(4,128)S(1)} %copy-done.8, bf16[256,512]{1,0:T(8,128)(2,1)S(1)} %get-tuple-element.22.qt, f32[256,512]{1,0:T(8,128)S(1)} %get-tuple-element.27.acc, f32[8,512]{1,0:T(8,128)S(1)} %get-tuple-element.28.ml, bf16[192,512]{1,0:T(8,128)(2,1)S(1)} %shard_map.73.mine, ...), custom_call_target="tpu_custom_call" | custom-call | flops 2000000000 | bytes 1000 | tf_op jit(solution)/shard_map/pallas_call | solution.py:238
  41.5 1.1 %collective-permute-start.13 = (bf16[256,256]{1,0:T(8,128)(2,1)S(1)}, bf16[256,256]{1,0:T(8,128)(2,1)S(1)}, u32[]{:S(2)}, u32[]{:S(2)}) collective-permute-start(bf16[256,256]{1,0:T(8,128)(2,1)S(1)} %shard_map.76.mine_att), channel_id=1, source_target_pairs={{0,3},{3,0},{1,2},{2,1},{4,7},{7,4},{5,6},{6,5},{8,11},{11,8},{9,1... | collective-permute-start | bytes 393224 | tf_op jit(solution)/shard_map/ppermute | solution.py:324
  42.7 2.7 %collective-permute-done.10.peer_att = bf16[256,256]{1,0:T(8,128)(2,1)S(1)} collective-permute-done((bf16[256,256]{1,0:T(8,128)(2,1)S(1)}, bf16[256,256]{1,0:T(8,128)(2,1)S(1)}, u32[]{:S(2)}, u32[]{:S(2)}) %collective-permute-start.10) | collective-permute-done | bytes 131104 | tf_op jit(solution)/shard_map/ppermute | solution.py:324
  46.9 2.6 %collective-permute-done.13.peer_att = bf16[256,256]{1,0:T(8,128)(2,1)S(1)} collective-permute-done((bf16[256,256]{1,0:T(8,128)(2,1)S(1)}, bf16[256,256]{1,0:T(8,128)(2,1)S(1)}, u32[]{:S(2)}, u32[]{:S(2)}) %collective-permute-start.13) | collective-permute-done | bytes 131104 | tf_op jit(solution)/shard_map/ppermute | solution.py:324
  50.2 1.8 %collective-permute-done.12 = bf16[256,256]{1,0:T(8,128)(2,1)S(1)} collective-permute-done((bf16[256,256]{1,0:T(8,128)(2,1)S(1)}, bf16[256,256]{1,0:T(8,128)(2,1)S(1)}, u32[]{:S(2)}, u32[]{:S(2)}) %collective-permute-start.12) | collective-permute-done | bytes 131104 | tf_op jit(solution)/shard_map/ppermute | solution.py:331
  52.1 2.8 %collective-permute-done.15 = bf16[256,256]{1,0:T(8,128)(2,1)S(1)} collective-permute-done((bf16[256,256]{1,0:T(8,128)(2,1)S(1)}, bf16[256,256]{1,0:T(8,128)(2,1)S(1)}, u32[]{:S(2)}, u32[]{:S(2)}) %collective-permute-start.15) | collective-permute-done | bytes 131104 | tf_op jit(solution)/shard_map/ppermute | solution.py:331
  (43 shorter events, 6.1 us)
Async XLA Ops:
  0.0 1.2 %copy-start.1 = (bf16[512,1024]{1,0:T(8,128)(2,1)S(1)}, bf16[512,1024]{1,0:T(8,128)(2,1)}, u32[]{:S(2)}) copy-start(bf16[512,1024]{1,0:T(8,128)(2,1)} %tok.5) | copy-start | bytes 3145732
  1.2 1.0 %copy-start.3 = (bf16[1024,256]{1,0:T(8,128)(2,1)S(1)}, bf16[1024,256]{1,0:T(8,128)(2,1)}, u32[]{:S(2)}) copy-start(bf16[1024,256]{1,0:T(8,128)(2,1)} %wk.3) | copy-start | bytes 1572868
  2.3 1.0 %copy-start.5 = (bf16[1024,256]{1,0:T(8,128)(2,1)S(1)}, bf16[1024,256]{1,0:T(8,128)(2,1)}, u32[]{:S(2)}) copy-start(bf16[1024,256]{1,0:T(8,128)(2,1)} %wv.3) | copy-start | bytes 1572868
  4.3 9.6 %copy-start.4 = (bf16[1024,256]{1,0:T(8,128)(2,1)S(1)}, bf16[1024,256]{1,0:T(8,128)(2,1)}, u32[]{:S(2)}) copy-start(bf16[1024,256]{1,0:T(8,128)(2,1)} %wk.3) | copy-start | bytes 1572868
  4.3 9.6 %copy-start.6 = (bf16[1024,256]{1,0:T(8,128)(2,1)S(1)}, bf16[1024,256]{1,0:T(8,128)(2,1)}, u32[]{:S(2)}) copy-start(bf16[1024,256]{1,0:T(8,128)(2,1)} %wv.3) | copy-start | bytes 1572868
  4.3 10.6 %collective-permute-start = (bf16[96,512]{1,0:T(8,128)(2,1)S(1)}, bf16[96,512]{1,0:T(8,128)(2,1)S(1)}, u32[]{:S(2)}, u32[]{:S(2)}) collective-permute-start(bf16[96,512]{1,0:T(8,128)(2,1)S(1)} %get-tuple-element.25.sent), channel_id=1, source_target_pairs={{0,8},{4,12},{8,0},{12,4},{16,24},{20,28},{24,16},{28,20},{32,40},... | collective-permute-start | bytes 294920 | tf_op jit(solution)/shard_map/ppermute | solution.py:249
  6.1 7.8 %collective-permute-start.3 = (f32[8,1024]{1,0:T(8,128)S(1)}, f32[8,1024]{1,0:T(8,128)S(1)}, u32[]{:S(2)}, u32[]{:S(2)}) collective-permute-start(f32[8,1024]{1,0:T(8,128)S(1)} %shard_map.69), channel_id=1, source_target_pairs={{0,224},{4,228},{8,232},{12,236},{16,240},{20,244},{24,248},{28,25... | collective-permute-start | bytes 98312 | tf_op jit(solution)/shard_map/ppermute | solution.py:249
  13.9 13.9 %copy-start.7 = (bf16[1024,256]{1,0:T(8,128)(2,1)S(1)}, bf16[1024,256]{1,0:T(8,128)(2,1)}, u32[]{:S(2)}) copy-start(bf16[1024,256]{1,0:T(8,128)(2,1)} %wq.1) | copy-start | bytes 1572868
  14.2 5.6 %copy-start = (bf16[256,1024]{1,0:T(8,128)(2,1)S(1)}, bf16[256,1024]{1,0:T(8,128)(2,1)}, u32[]{:S(2)}) copy-start(bf16[256,1024]{1,0:T(8,128)(2,1)} %mine_w.3) | copy-start | bytes 1572868
  14.2 13.7 %copy-start.2 = (bf16[512,1024]{1,0:T(8,128)(2,1)S(1)}, bf16[512,1024]{1,0:T(8,128)(2,1)}, u32[]{:S(2)}) copy-start(bf16[512,1024]{1,0:T(8,128)(2,1)} %tok.5) | copy-start | bytes 3145732
  14.2 4.7 %collective-permute-start.4 = (bf16[16,512]{1,0:T(8,128)(2,1)S(1)}, bf16[16,512]{1,0:T(8,128)(2,1)S(1)}, u32[]{:S(2)}, u32[]{:S(2)}) collective-permute-start(bf16[16,512]{1,0:T(8,128)(2,1)S(1)} %shard_map.70.sent), channel_id=1, source_target_pairs={{0,64},{4,68},{8,72},{12,76},{16,80},{20,84},{24,88},{28,92},{32,9... | collective-permute-start | bytes 49160 | tf_op jit(solution)/shard_map/ppermute | solution.py:249
  14.9 12.8 %collective-permute-start.1 = (bf16[64,512]{1,0:T(8,128)(2,1)S(1)}, bf16[64,512]{1,0:T(8,128)(2,1)S(1)}, u32[]{:S(2)}, u32[]{:S(2)}) collective-permute-start(bf16[64,512]{1,0:T(8,128)(2,1)S(1)} %shard_map.66), channel_id=1, source_target_pairs={{0,16},{4,20},{8,24},{12,28},{16,0},{20,4},{24,8},{28,12},{32,48},... | collective-permute-start | bytes 196616 | tf_op jit(solution)/shard_map/ppermute | solution.py:249
  18.9 4.0 %collective-permute-start.5 = (bf16[32,512]{1,0:T(8,128)(2,1)S(1)}, bf16[32,512]{1,0:T(8,128)(2,1)S(1)}, u32[]{:S(2)}, u32[]{:S(2)}) collective-permute-start(bf16[32,512]{1,0:T(8,128)(2,1)S(1)} %shard_map.71.sent), channel_id=1, source_target_pairs={{0,32},{4,36},{8,40},{12,44},{16,48},{20,52},{24,56},{28,60},{32,0... | collective-permute-start | bytes 98312 | tf_op jit(solution)/shard_map/ppermute | solution.py:249
  19.8 22.9 %collective-permute-start.11 = (bf16[256,1024]{1,0:T(8,128)(2,1)S(1)}, bf16[256,1024]{1,0:T(8,128)(2,1)S(1)}, u32[]{:S(2)}, u32[]{:S(2)}) collective-permute-start(bf16[256,1024]{1,0:T(8,128)(2,1)S(1)} %copy-done), channel_id=1, source_target_pairs={{0,1},{1,0},{2,3},{3,2},{4,5},{5,4},{6,7},{7,6},{8,9},{9,8},{10,11... | collective-permute-start | bytes 1572872 | tf_op jit(solution)/shard_map/ppermute | solution.py:282
  22.9 8.3 %collective-permute-start.6 = (bf16[48,512]{1,0:T(8,128)(2,1)S(1)}, bf16[48,512]{1,0:T(8,128)(2,1)S(1)}, u32[]{:S(2)}, u32[]{:S(2)}) collective-permute-start(bf16[48,512]{1,0:T(8,128)(2,1)S(1)} %shard_map.72.a), channel_id=1, source_target_pairs={{0,8},{4,12},{8,16},{12,20},{16,24},{20,28},{24,0},{28,4},{32,40},... | collective-permute-start | bytes 147464 | tf_op jit(solution)/shard_map/ppermute | solution.py:249
  23.5 10.9 %collective-permute-start.7 = (bf16[48,512]{1,0:T(8,128)(2,1)S(1)}, bf16[48,512]{1,0:T(8,128)(2,1)S(1)}, u32[]{:S(2)}, u32[]{:S(2)}) collective-permute-start(bf16[48,512]{1,0:T(8,128)(2,1)S(1)} %shard_map.72.a), channel_id=1, source_target_pairs={{0,24},{4,28},{8,0},{12,4},{16,8},{20,12},{24,16},{28,20},{32,56},... | collective-permute-start | bytes 147464 | tf_op jit(solution)/shard_map/ppermute | solution.py:249
  26.2 8.2 %collective-permute-start.8 = (bf16[48,512]{1,0:T(8,128)(2,1)S(1)}, bf16[48,512]{1,0:T(8,128)(2,1)S(1)}, u32[]{:S(2)}, u32[]{:S(2)}) collective-permute-start(bf16[48,512]{1,0:T(8,128)(2,1)S(1)} %shard_map.72.a), channel_id=1, source_target_pairs={{0,16},{4,20},{8,24},{12,28},{16,0},{20,4},{24,8},{28,12},{32,48},... | collective-permute-start | bytes 147464 | tf_op jit(solution)/shard_map/ppermute | solution.py:249
  27.7 6.9 %collective-permute-start.2 = (bf16[256,512]{1,0:T(8,128)(2,1)S(1)}, bf16[256,512]{1,0:T(8,128)(2,1)S(1)}, u32[]{:S(2)}, u32[]{:S(2)}) collective-permute-start(bf16[256,512]{1,0:T(8,128)(2,1)S(1)} %shard_map.67), channel_id=1, source_target_pairs={{0,4},{4,0},{8,12},{12,8},{16,20},{20,16},{24,28},{28,24},{32,36},... | collective-permute-start | bytes 786440 | tf_op jit(solution)/shard_map/ppermute | solution.py:249
  31.2 15.7 %collective-permute-start.14 = (bf16[256,1024]{1,0:T(8,128)(2,1)S(1)}, bf16[256,1024]{1,0:T(8,128)(2,1)S(1)}, u32[]{:S(2)}, u32[]{:S(2)}) collective-permute-start(bf16[256,1024]{1,0:T(8,128)(2,1)S(1)} %copy-done), channel_id=1, source_target_pairs={{0,3},{3,0},{1,2},{2,1},{4,7},{7,4},{5,6},{6,5},{8,11},{11,8},{9,1... | collective-permute-start | bytes 1572872 | tf_op jit(solution)/shard_map/ppermute | solution.py:283
  34.4 3.1 %collective-permute-start.9 = (bf16[192,512]{1,0:T(8,128)(2,1)S(1)}, bf16[192,512]{1,0:T(8,128)(2,1)S(1)}, u32[]{:S(2)}, u32[]{:S(2)}) collective-permute-start(bf16[192,512]{1,0:T(8,128)(2,1)S(1)} %shard_map.73.mine), channel_id=1, source_target_pairs={{0,4},{4,0},{8,12},{12,8},{16,20},{20,16},{24,28},{28,24},{32,36},... | collective-permute-start | bytes 589832 | tf_op jit(solution)/shard_map/ppermute | solution.py:249
  39.4 5.9 %collective-permute-start.10 = (bf16[256,256]{1,0:T(8,128)(2,1)S(1)}, bf16[256,256]{1,0:T(8,128)(2,1)S(1)}, u32[]{:S(2)}, u32[]{:S(2)}) collective-permute-start(bf16[256,256]{1,0:T(8,128)(2,1)S(1)} %shard_map.74.mine_att), channel_id=1, source_target_pairs={{0,1},{1,0},{2,3},{3,2},{4,5},{5,4},{6,7},{7,6},{8,9},{9,8},{10,11... | collective-permute-start | bytes 393224 | tf_op jit(solution)/shard_map/ppermute | solution.py:324
  41.5 7.9 %collective-permute-start.13 = (bf16[256,256]{1,0:T(8,128)(2,1)S(1)}, bf16[256,256]{1,0:T(8,128)(2,1)S(1)}, u32[]{:S(2)}, u32[]{:S(2)}) collective-permute-start(bf16[256,256]{1,0:T(8,128)(2,1)S(1)} %shard_map.76.mine_att), channel_id=1, source_target_pairs={{0,3},{3,0},{1,2},{2,1},{4,7},{7,4},{5,6},{6,5},{8,11},{11,8},{9,1... | collective-permute-start | bytes 393224 | tf_op jit(solution)/shard_map/ppermute | solution.py:324
  45.7 6.4 %collective-permute-start.12 = (bf16[256,256]{1,0:T(8,128)(2,1)S(1)}, bf16[256,256]{1,0:T(8,128)(2,1)S(1)}, u32[]{:S(2)}, u32[]{:S(2)}) collective-permute-start(bf16[256,256]{1,0:T(8,128)(2,1)S(1)} %get-tuple-element.32), channel_id=1, source_target_pairs={{0,3},{3,0},{1,2},{2,1},{4,7},{7,4},{5,6},{6,5},{8,11},{11,8},{9,1... | collective-permute-start | bytes 393224 | tf_op jit(solution)/shard_map/ppermute | solution.py:331
  49.8 5.1 %collective-permute-start.15 = (bf16[256,256]{1,0:T(8,128)(2,1)S(1)}, bf16[256,256]{1,0:T(8,128)(2,1)S(1)}, u32[]{:S(2)}, u32[]{:S(2)}) collective-permute-start(bf16[256,256]{1,0:T(8,128)(2,1)S(1)} %get-tuple-element.34), channel_id=1, source_target_pairs={{0,1},{1,0},{2,3},{3,2},{4,5},{5,4},{6,7},{7,6},{8,9},{9,8},{10,11... | collective-permute-start | bytes 393224 | tf_op jit(solution)/shard_map/ppermute | solution.py:331
  (1 other events, 0.7 us)

commit v2 on v1

v2 whole, which is shorter than its diff:
```python
import functools
import math

import jax
import jax.numpy as jnp
from jax import lax
from jax.experimental import pallas as pl
from jax.experimental.pallas import tpu as pltpu
from jax.sharding import PartitionSpec as P

LOG_TWO = math.log(2.0)
NEG = -1e30
BLOCK = 128
WIDTH = 256
HEADS = 4
F32 = jnp.float32
BF16 = jnp.bfloat16

Z, X, C = 8, 4, 2


def index(z, x, c):
    return (z % Z) * 8 + (x % X) * 2 + c


CHIPS = [(z, x, c) for z in range(Z) for x in range(X) for c in range(C)]


def dot(a, b):
    return lax.dot_general(a, b, (((1,), (0,)), ((), ())), preferred_element_type=F32)


def pool_rows(rows, level):
    token = lax.broadcasted_iota(jnp.int32, (rows, 512), 1)
    row = lax.broadcasted_iota(jnp.int32, (rows, 512), 0)
    inverse = jnp.float32(0.0)
    for each in range(1, 8):
        inverse = jnp.where(level == each, jnp.float32(2.0**-each), inverse)
    hit = lax.shift_right_logical(token, jnp.full((rows, 512), level, jnp.int32)) == row
    return jnp.where(hit, inverse, 0.0).astype(BF16)


def my_core():
    return lax.axis_index("seq") % 2


def load_kernel(
    tok_hbm, wk_hbm, wv_hbm, wo_hbm,
    kv, l1, e1, share, to_next, to_far,
    tok, wk, wv, sems,
):
    head = lax.axis_index("head")
    near, far = next_head(head), 3 - head
    pairs = [(wk_hbm, wk)]
    pairs += [(tok_hbm.at[pl.ds(i * 256, 256)], tok.at[pl.ds(i * 256, 256)]) for i in range(2)]
    pairs.append((wv_hbm, wv))
    for out, first, second in ((to_next, near, 3 - near), (to_far, far, next_head(far))):
        pairs.append((wo_hbm.at[:, columns(first)], out.at[:, pl.ds(0, WIDTH)]))
        pairs.append((wo_hbm.at[:, columns(second)], out.at[:, pl.ds(WIDTH, WIDTH)]))
    copies = [pltpu.make_async_copy(*pair, sems.at[i]) for i, pair in enumerate(pairs)]
    for copy in copies:
        copy.start()
    parts = [
        pool_rows(n, level)
        for n, level in ((128, 1), (64, 3), (32, 4), (128, 2), (16, 5), (16, 6), (16, 7))
    ]
    for copy in copies[:3]:
        copy.wait()
    keys = dot(tok[...], wk[...]).astype(BF16)
    copies[3].wait()
    values = dot(tok[...], wv[...]).astype(BF16)
    both = jnp.concatenate([keys, values], axis=1)
    kv[...] = both
    pooled = dot(jnp.concatenate(parts, axis=0), both)
    l1[...] = pooled[0:128].astype(BF16)
    e1[...] = pooled[128:224].astype(BF16)
    share[...] = pooled[224:400].astype(BF16)
    for copy in copies[4:]:
        copy.wait()


def mirror_kernel(share, other, after, out):
    own, far = share[160:176, :].astype(F32)[:4], other[160:176, :].astype(F32)[:4]
    out[...] = jnp.concatenate([own, far, own, far], axis=0).astype(BF16)


def two_kernel(share, other, got, after0, after1, out):
    own, far = share[144:160, :].astype(F32)[:8], other[144:160, :].astype(F32)[:8]
    out[0:16, :] = jnp.concatenate([own, far], axis=0).astype(BF16)
    out[16:32, :] = got[...]


def joint_kernel(share, other, sent, got, after, out):
    out[0:16, :] = share[128:144, :]
    out[16:32, :] = other[128:144, :]
    out[32:48, :] = got[0:16, :]
    mine, peer = sent[16:32, :].astype(F32)[:8], got[16:32, :].astype(F32)[:8]
    out[48:64, :] = jnp.concatenate([mine, peer], axis=0).astype(BF16)


def far_join_kernel(sent, got, out):
    out[0:32, :] = got[0:32, :]
    for level in (1, 2):
        to, at = level * 32, 16 + level * 16
        out[to : to + 16, :] = sent[at : at + 16, :]
        out[to + 16 : to + 32, :] = got[at : at + 16, :]


def near_join_kernel(sent, got, out):
    out[0:32, :] = sent[64:96, :]
    out[32:64, :] = got[64:96, :]


def plane_join_kernel(first, second, out):
    out[0:64, :] = first[0:64, :]
    out[64:128, :] = second[...]


def row_join_kernel(a, b, c, d, *refs):
    out = refs[-1]
    for level in range(3):
        for step, piece in enumerate((a, b, c, d)):
            to = level * 128 + step * 32
            out[to : to + 32, :] = piece[level * 32 : (level + 1) * 32, :]


def columns(chunk):
    return pl.ds(pl.multiple_of(chunk * WIDTH, WIDTH), WIDTH)


def next_head(head):
    return head + 1 - 2 * (head % 2)


def stack_heads(query_t):
    head = lax.broadcasted_iota(jnp.int32, (WIDTH, BLOCK), 0) // 64
    zero = jnp.zeros_like(query_t)
    return jnp.concatenate([jnp.where(head == h, query_t, zero) for h in range(HEADS)], axis=1)


def turn(array):
    return array.astype(F32).T.astype(BF16)


def gate_bias(gate, block, level):
    return jnp.where(gate[block, level] == 1, jnp.float32(level * LOG_TWO), jnp.float32(NEG))


def attend(query_t, keys, values_t, biases, mask, old, old_top, old_total):
    scores = dot(keys, stack_heads(query_t))
    outs, tops, totals = [], [], []
    for h in range(HEADS):
        lanes = slice(h * BLOCK, (h + 1) * BLOCK)
        pieces = [scores[i * BLOCK : (i + 1) * BLOCK, lanes] for i in range(len(biases))]
        if mask is not None:
            pieces[0] = pieces[0] + mask
        top = None if old_top is None else old_top[:, lanes]
        for piece, bias in zip(pieces, biases):
            high = jnp.max(piece, axis=0, keepdims=True) + bias
            top = high if top is None else jnp.maximum(top, high)
        expo = [jnp.exp(piece - (top - bias)) for piece, bias in zip(pieces, biases)]
        total = sum(jnp.sum(piece, axis=0, keepdims=True) for piece in expo)
        weights = jnp.concatenate([piece.astype(BF16) for piece in expo], axis=0)
        rows = slice(h * 64, (h + 1) * 64)
        out = dot(values_t[rows, :], weights)
        if old is not None:
            scale = jnp.exp(old_top[:, lanes] - top)
            out = out + old[rows, :] * scale
            total = total + old_total[:, lanes] * scale
        outs.append(out)
        tops.append(top)
        totals.append(total)
    return outs, tops, totals


def own_half(half, gate, qt, kv, vt, l1, acc, ml):
    key = lax.broadcasted_iota(jnp.int32, (BLOCK, BLOCK), 0)
    row = lax.broadcasted_iota(jnp.int32, (BLOCK, BLOCK), 1)
    causal = jnp.where(key <= row, 0.0, NEG).astype(F32)
    if half:
        l1_t = turn(l1[:, WIDTH:])
    for step in range(2):
        b = half * 2 + step
        rows = slice(b * BLOCK, (b + 1) * BLOCK)
        keys = [kv[rows, :WIDTH]]
        values = [vt[:, rows]]
        biases = [jnp.float32(0.0)]
        if b & 1:
            before = slice((b - 1) * BLOCK, b * BLOCK)
            keys.append(kv[before, :WIDTH])
            values.append(vt[:, before])
            biases.append(gate_bias(gate, b, 0))
        if b & 2:
            keys.append(l1[:, :WIDTH])
            values.append(l1_t)
            biases.append(gate_bias(gate, b, 1))
        keys, values = jnp.concatenate(keys, axis=0), jnp.concatenate(values, axis=1)
        outs, tops, totals = attend(qt[:, rows], keys, values, biases, causal, None, None, None)
        acc[:, step * BLOCK : (step + 1) * BLOCK] = jnp.concatenate(outs, axis=0)
        ml[step : step + 1, :] = jnp.concatenate(tops, axis=1)
        ml[4 + step : 5 + step, :] = jnp.concatenate(totals, axis=1)


def own_blocks(gate, tok, wq, kv, l1, qt, acc0, ml0, acc1, ml1):
    query = dot(tok[...], wq[...]).astype(BF16).astype(F32) * 0.125
    query_t = query.T.astype(BF16)
    qt[...] = query_t
    values_t = turn(kv[:, WIDTH:])
    own_half(0, gate, query_t, kv, values_t, l1, acc0, ml0)
    own_half(1, gate, query_t, kv, values_t, l1, acc1, ml1)


def high_plane():
    return lax.axis_index("seq") >= 32


def early_kernel(gate, tok, wq, kv, l1, *outs):
    @pl.when(jnp.logical_not(high_plane()))
    def _():
        own_blocks(gate, tok, wq, kv, l1, *outs)


def late_kernel(gate, tok, wq, kv, l1, *refs):
    early, outs = refs[:5], refs[-5:]

    @pl.when(high_plane())
    def _():
        own_blocks(gate, tok, wq, kv, l1, *outs)

    @pl.when(jnp.logical_not(high_plane()))
    def _():
        for source, out in zip(early, outs):
            out[...] = source[...]


def level_biases(gate, block, first):
    seq = lax.axis_index("seq")
    out = []
    for level in range(first, first + 3):
        bit = lax.shift_right_logical(seq, level - 2) % 2
        out.append(jnp.where(bit == 1, gate_bias(gate, block, level), jnp.float32(NEG)))
    return out


def cross(b, first, gate, qt, acc, ml, keys, values_t):
    step = b % 2
    biases = level_biases(gate, b, first)
    old = (acc[:, step * BLOCK : (step + 1) * BLOCK], ml[step : step + 1, :], ml[4 + step : 5 + step, :])
    return attend(qt[:, b * BLOCK : (b + 1) * BLOCK], keys, values_t, biases, None, *old)


def plane_kernel(gate, qt, acc0, ml0, acc1, ml1, share, first, second, other, *refs):
    outs_refs = refs[-4:]
    pieces = [share[0:128, :], first[0:64, :], other[0:64, :], second[...], other[64:128, :]]
    keys = jnp.concatenate([piece[:, :WIDTH] for piece in pieces], axis=0)
    values_t = turn(jnp.concatenate([piece[:, WIDTH:] for piece in pieces], axis=0))
    for b in range(4):
        half, step = b // 2, b % 2
        acc, ml = ((acc0, ml0), (acc1, ml1))[half]
        acc_out, ml_out = outs_refs[2 * half : 2 * half + 2]
        outs, tops, totals = cross(b, 2, gate, qt, acc, ml, keys, values_t)
        acc_out[:, step * BLOCK : (step + 1) * BLOCK] = jnp.concatenate(outs, axis=0)
        ml_out[step : step + 1, :] = jnp.concatenate(tops, axis=1)
        ml_out[4 + step : 5 + step, :] = jnp.concatenate(totals, axis=1)


def far_kernel(half, gate, qt, acc, ml, mine, other, att):
    rows = jnp.where(my_core() == 1, mine[...], other[...])
    keys = rows[:, :WIDTH]
    values_t = turn(rows[:, WIDTH:])
    for step in range(2):
        outs, _, totals = cross(half * 2 + step, 5, gate, qt, acc, ml, keys, values_t)
        outs = [out / total for out, total in zip(outs, totals)]
        turned = jnp.concatenate(outs, axis=0).T.astype(BF16)
        att[step * BLOCK : (step + 1) * BLOCK, :] = turned


def project_kernel(half, mine_att, peer_att, mine_w, peer_w, keep, send):
    head = lax.axis_index("head")
    other = 3 - head if half == 0 else next_head(head)
    for chunk, part, ref in ((other, slice(WIDTH, 2 * WIDTH), send), (head, slice(0, WIDTH), keep)):
        total = dot(mine_att[...], mine_w[:, columns(chunk)]) + dot(peer_att[...], peer_w[:, part])
        ref[...] = total.astype(ref.dtype)


VMEM = pl.BlockSpec(memory_space=pltpu.VMEM)
SMEM = pl.BlockSpec(memory_space=pltpu.SMEM)
ANY = pl.BlockSpec(memory_space=pl.ANY)
HBM = pl.BlockSpec(memory_space=pltpu.HBM)


def call(kernel, args, outs, flops, smem=0, unread=0):
    return pl.pallas_call(
        kernel,
        name=getattr(kernel, "func", kernel).__name__,
        out_shape=[jax.ShapeDtypeStruct(shape, dtype) for shape, dtype in outs],
        in_specs=[SMEM] * smem + [VMEM] * (len(args) - smem - unread) + [ANY] * unread,
        out_specs=[VMEM] * len(outs),
        compiler_params=pltpu.CompilerParams(vmem_limit_bytes=24 * 1024 * 1024),
        cost_estimate=pl.CostEstimate(flops=flops, bytes_accessed=1000, transcendentals=0),
    )(*args)


def move(array, pairs, name):
    with jax.named_scope(name):
        return lax.ppermute(array, "seq", pairs)


def hub(array, to, idle, name):
    far = [(index(z, x, 1), index(*to(z, x), 1)) for z, x, c in CHIPS if c]
    near = [(index(z, x, 0), index(*idle(z, x), 0)) for z, x, c in CHIPS if not c]
    return move(array, far + near, name)


def idle_x(z, x):
    return z, x ^ 1


def idle_z(z, x):
    return z ^ 1, x


def across(array, bit, name):
    return move(array, [(index(z, x, c), index(z, x ^ bit, c)) for z, x, c in CHIPS], name)


def swap(array, name):
    return move(array, [(index(z, x, c), index(z, x, 1 - c)) for z, x, c in CHIPS], name)


PAIR_NEXT = [(0, 1), (1, 0), (2, 3), (3, 2)]
PAIR_FAR = [(0, 3), (3, 0), (1, 2), (2, 1)]


COST = 10**6


def shards(tokens, wq, wk, wv, wo, gate):
    rows = lambda n: ((n, 2 * WIDTH), BF16)
    kv, l1, e1, share, to_next, to_far = pl.pallas_call(
        load_kernel,
        name="load_kernel",
        out_shape=[
            jax.ShapeDtypeStruct(shape, BF16)
            for shape in ((512, 512), (128, 512), (96, 512), (176, 512))
            + ((WIDTH, 512),) * 2
        ],
        in_specs=[HBM] * 4,
        out_specs=[VMEM] * 6,
        scratch_shapes=[
            pltpu.VMEM((512, 1024), BF16),
            pltpu.VMEM((1024, WIDTH), BF16),
            pltpu.VMEM((1024, WIDTH), BF16),
            pltpu.SemaphoreType.DMA((8,)),
        ],
        compiler_params=pltpu.CompilerParams(vmem_limit_bytes=52 * 1024 * 1024),
        cost_estimate=pl.CostEstimate(flops=COST, bytes_accessed=1000, transcendentals=0),
    )(tokens, wk, wv, wo)
    share_other = swap(share, "swap_share")
    first = across(e1, 1, "across_one")
    state = [((WIDTH, 256), F32), ((8, 512), F32)]
    held = [((WIDTH, 512), BF16)] + state * 2
    early = call(early_kernel, (gate, tokens, wq, kv, l1), held, COST, smem=1)
    (pay,) = call(mirror_kernel, (share, share_other, early[2]), [rows(16)], COST, unread=1)
    far5 = hub(pay, lambda z, x: (7 - z, x), idle_x, "planes_mirror")
    qt, acc0, ml0, acc1, ml1 = call(
        late_kernel, (gate, tokens, wq, kv, l1, *early, pay), held, COST, smem=1, unread=1
    )
    own = [(acc0, ml0), (acc1, ml1)]
    first, ml = lax.optimization_barrier((first, own[1][1]))
    own[1] = (own[1][0], ml)
    (near,) = call(near_join_kernel, (e1, first), [rows(64)], COST)
    second = across(near, 2, "across_two")
    (pay,) = call(
        two_kernel, (share, share_other, far5, own[0][1], own[1][1]), [rows(32)], COST, unread=2
    )
    got = hub(pay, lambda z, x: (z ^ 2, x), idle_x, "planes_two")
    (pay,) = call(
        joint_kernel, (share, share_other, pay, got, own[0][1]), [rows(64)], COST, unread=1
    )
    got = hub(pay, lambda z, x: (z ^ 1, x), idle_x, "planes_one")
    (far,) = call(far_join_kernel, (pay, got), [rows(96)], COST)
    (near,) = call(plane_join_kernel, (first, second), [rows(128)], COST)
    other = swap(near, "swap_near")
    far, to_far, to_next = lax.optimization_barrier((far, to_far, to_next))
    w_next = lax.ppermute(to_next, "head", PAIR_NEXT)
    w_far = lax.ppermute(to_far, "head", PAIR_FAR)
    acc0, ml0, acc1, ml1 = call(
        plane_kernel,
        (gate, qt, *own[0], *own[1], share_other, first, second, other),
        state * 2,
        COST,
        smem=1,
    )
    others = [hub(far, lambda z, x, shift=shift: (z, x + shift), idle_z, "along") for shift in (1, -1, 2)]
    (far,) = call(row_join_kernel, (far, *others, ml0, w_next, w_far), [rows(384)], COST, unread=3)
    far_other = swap(far, "swap_far")
    held = ((acc0, ml0), (acc1, ml1))
    halves = []
    for half in range(2):
        (att,) = call(
            functools.partial(far_kernel, half),
            (gate, qt, *held[half], far, far_other),
            [((256, WIDTH), BF16)],
            COST,
            smem=1,
        )
        halves.append(att)
    out = []
    pairs = (PAIR_NEXT, PAIR_FAR)
    for half in range(2):
        peer = lax.ppermute(halves[half], "head", pairs[half])
        keep, send = call(
            functools.partial(project_kernel, half),
            (halves[half], peer, wo, (w_next, w_far)[half]),
            [((256, WIDTH), F32), ((256, WIDTH), BF16)],
            COST,
        )
        out.append(keep + lax.ppermute(send, "head", pairs[1 - half]).astype(F32))
    return jnp.concatenate(out, axis=0).astype(BF16)


def solution(mesh):
    placed = (
        P("seq", None),
        P(None, "head"),
        P(None, "head"),
        P(None, "head"),
        P("head", None),
        P("seq", None),
    )
    return jax.shard_map(
        shards, mesh=mesh, in_specs=placed, out_specs=P("seq", "head"), check_vma=False
    )
```

time: 56.5 us -> 51.3 us (0.908); the launches traced: 55.6 us -> 51.2 us
  starting transfers between devices: 24.1 us -> 18.9 us
  local copies, waits for them, and re-layouts: 3.89 us -> 1.15 us
  waiting for transfers between devices: 15.1 us -> 17.5 us
  Pallas kernels: 11.6 us -> 12.7 us
    ppermute x10 -> x11, starting transfers between devices: 17 us -> 10.5 us  [move(): return lax.ppermute(array, 'seq', pairs)]
    ppermute x10 -> x11, waiting for transfers between devices: 4.64 us -> 9.12 us  [move(): return lax.ppermute(array, 'seq', pairs)]
    unnamed x18 -> x10, local copies, waits for them, and re-layouts: 3.89 us -> 1.15 us
    ppermute x2, waiting for transfers between devices: 5.23 us -> 3.05 us  [shards(): peer = lax.ppermute(halves[half], 'head', pairs[half])]
    pallas_call x14 -> x15, Pallas kernels: 11.6 us -> 12.7 us  [the longest x14 9.71 us: call(): pl.pallas_call(kernel, name=getattr(kernel, 'func', kernel).__name__, out...]
    ppermute x2, starting transfers between devices: 1.35 us -> 2.51 us  [shards(): peer = lax.ppermute(halves[half], 'head', pairs[half])]
    ppermute x2, starting transfers between devices: 0.99 us -> 2.1 us  [shards(): out.append(keep + lax.ppermute(send, 'head', pairs[1 - half]).astype(F32))]
    ppermute x2, starting transfers between devices: 4.67 us -> 3.84 us  [the longest x1 2.18 us: shards(): w_far = lax.ppermute(to_far, 'head', PAIR_FAR)]
  transfers between devices with their start and end apart: 16 -> 17, of which waited for: 8 -> 11; matrix products, arithmetic and copies ran while one was open for 0% -> 0% of each run, Pallas kernels for 19% -> 16%
where the time goes in v2:
time: 51.3 us; the launch traced here: 51.2 us
  starting transfers between devices  18.9 us (37%)
  waiting for transfers between devices  17.5 us (34%)
  Pallas kernels  12.7 us (25%)
  local copies, waits for them, and re-layouts  1.15 us (2%)
  other arithmetic  0.79 us (2%)
    ppermute x11, starting transfers between devices, move(): return lax.ppermute(array, 'seq', pairs)  10.5 us
    pallas_call x14, Pallas kernels, call(): pl.pallas_call(kernel, name=getattr(kernel, 'func', kernel).__name__, out...  9.71 us
    ppermute x11, waiting for transfers between devices, move(): return lax.ppermute(array, 'seq', pairs)  9.12 us
    ppermute x2, waiting for transfers between devices, shards(): out.append(keep + lax.ppermute(send, 'head', pairs[1 - half]).astype(F32))  4.62 us
    ppermute x2, waiting for transfers between devices, shards(): peer = lax.ppermute(halves[half], 'head', pairs[half])  3.05 us
    pallas_call x1, Pallas kernels, shards(): pl.pallas_call(load_kernel, name='load_kernel', out_shape=[jax.ShapeDtype...  3.02 us
    ppermute x2, starting transfers between devices, shards(): peer = lax.ppermute(halves[half], 'head', pairs[half])  2.51 us
    ppermute x1, starting transfers between devices, shards(): w_far = lax.ppermute(to_far, 'head', PAIR_FAR)  2.18 us
  transfers between devices with their start and end apart: 17, of which 11 were waited for; matrix products, arithmetic and copies ran while one was open for 0% of the time, Pallas kernels for 16%

profile of v2, /device:TPU:32, one launch (start us, length us, event | category | flops | bytes accessed | tf_op | source)
XLA Modules:
  0.0 51.2 jit_solution(8826184535623078451)
XLA Ops:
  0.0 1.1 %copy-done.3 = bf16[1024,256]{1,0:T(8,128)(2,1)S(1)} copy-done((bf16[1024,256]{1,0:T(8,128)(2,1)S(1)}, bf16[1024,256]{1,0:T(8,128)(2,1)}, u32[]{:S(2)}) %copy-start.3) | copy-done | bytes 524312
  1.1 3.0 %load_kernel.1 = (bf16[512,512]{1,0:T(8,128)(2,1)S(1)}, bf16[128,512]{1,0:T(8,128)(2,1)S(1)}, bf16[96,512]{1,0:T(8,128)(2,1)S(1)}, bf16[176,512]{1,0:T(8,128)(2,...) custom-call(bf16[512,1024]{1,0:T(8,128)(2,1)} %tok.3, bf16[1024,256]{1,0:T(8,128)(2,1)S(1)} %copy-done.3, ...), custom_call_target="tpu_custom_call" | custom-call | flops 1000000 | bytes 1000 | tf_op jit(solution)/shard_map/load_kernel/pallas_call | solution.py:340
  4.3 1.6 %collective-permute-start.1 = (bf16[96,512]{1,0:T(8,128)(2,1)S(1)}, bf16[96,512]{1,0:T(8,128)(2,1)S(1)}, u32[]{:S(2)}, u32[]{:S(2)}) collective-permute-start(bf16[96,512]{1,0:T(8,128)(2,1)S(1)} %get-tuple-element.46.sent), channel_id=1, source_target_pairs={{0,8},{4,12},{8,0},{12,4},{16,24},{20,28},{24,16},{28,20},{32,40},... | collective-permute-start | bytes 294920 | tf_op jit(solution)/shard_map/across_one/ppermute | solution.py:306
  5.9 2.7 %early_kernel.1 = (bf16[256,512]{1,0:T(8,128)(2,1)S(1)}, f32[256,256]{1,0:T(8,128)S(1)}, f32[8,512]{1,0:T(8,128)S(1)}, f32[256,256]{1,0:T(8,128)S(1)}, f32[8,512]{1,0:T(8,128)S(1)}) custom-call(s32[4,16]{1,0:T(4,128)S(1)} %copy-done.4, bf16[512,1024]{1,0:T(8,128)(2,1)S(1)} %copy-done, bf16[1024,256]{1,0:T(8,128)(2,1)S(1)} %copy-done.2, ...), custom_call_target="tpu_custom_call" | custom-call | flops 1000000 | bytes 1000 | tf_op jit(solution)/shard_map/early_kernel/pallas_call | solution.py:293
  10.0 2.5 %collective-permute-done.4.got = bf16[16,512]{1,0:T(8,128)(2,1)S(1)} collective-permute-done((bf16[16,512]{1,0:T(8,128)(2,1)S(1)}, bf16[16,512]{1,0:T(8,128)(2,1)S(1)}, u32[]{:S(2)}, u32[]{:S(2)}) %collective-permute-start.4) | collective-permute-done | bytes 16416 | tf_op jit(solution)/shard_map/planes_mirror/ppermute | solution.py:306
  13.0 3.3 %collective-permute-done.5.got = bf16[32,512]{1,0:T(8,128)(2,1)S(1)} collective-permute-done((bf16[32,512]{1,0:T(8,128)(2,1)S(1)}, bf16[32,512]{1,0:T(8,128)(2,1)S(1)}, u32[]{:S(2)}, u32[]{:S(2)}) %collective-permute-start.5) | collective-permute-done | bytes 32800 | tf_op jit(solution)/shard_map/planes_two/ppermute | solution.py:306
  17.0 3.0 %collective-permute-start.2 = (bf16[64,512]{1,0:T(8,128)(2,1)S(1)}, bf16[64,512]{1,0:T(8,128)(2,1)S(1)}, u32[]{:S(2)}, u32[]{:S(2)}) collective-permute-start(bf16[64,512]{1,0:T(8,128)(2,1)S(1)} %near_join_kernel.1), channel_id=1, source_target_pairs={{0,16},{4,20},{8,24},{12,28},{16,0},{20,4},{24,8},{28,12},{32,48},... | collective-permute-start | bytes 196616 | tf_op jit(solution)/shard_map/across_two/ppermute | solution.py:306
  20.7 1.7 %collective-permute-start.10 = (bf16[256,512]{1,0:T(8,128)(2,1)S(1)}, bf16[256,512]{1,0:T(8,128)(2,1)S(1)}, u32[]{:S(2)}, u32[]{:S(2)}) collective-permute-start(bf16[256,512]{1,0:T(8,128)(2,1)S(1)} %get-tuple-element.55), channel_id=1, source_target_pairs={{0,1},{1,0},{2,3},{3,2},{4,5},{5,4},{6,7},{7,6},{8,9},{9,8},{10,11... | collective-permute-start | bytes 786440 | tf_op jit(solution)/shard_map/ppermute | solution.py:386
  22.3 2.2 %collective-permute-start.11 = (bf16[256,512]{1,0:T(8,128)(2,1)S(1)}, bf16[256,512]{1,0:T(8,128)(2,1)S(1)}, u32[]{:S(2)}, u32[]{:S(2)}) collective-permute-start(bf16[256,512]{1,0:T(8,128)(2,1)S(1)} %get-tuple-element.56), channel_id=1, source_target_pairs={{0,3},{3,0},{1,2},{2,1},{4,7},{7,4},{5,6},{6,5},{8,11},{11,8},{9,1... | collective-permute-start | bytes 786440 | tf_op jit(solution)/shard_map/ppermute | solution.py:387
  24.7 1.1 %collective-permute-start.7 = (bf16[96,512]{1,0:T(8,128)(2,1)S(1)}, bf16[96,512]{1,0:T(8,128)(2,1)S(1)}, u32[]{:S(2)}, u32[]{:S(2)}) collective-permute-start(bf16[96,512]{1,0:T(8,128)(2,1)S(1)} %far_join_kernel.1.a), channel_id=1, source_target_pairs={{4,12},{12,20},{20,28},{28,4},{36,44},{44,52},{52,60},{60,36},{68,... | collective-permute-start | bytes 294920 | tf_op jit(solution)/shard_map/along/ppermute | solution.py:306
  25.8 1.0 %collective-permute-start.8 = (bf16[96,512]{1,0:T(8,128)(2,1)S(1)}, bf16[96,512]{1,0:T(8,128)(2,1)S(1)}, u32[]{:S(2)}, u32[]{:S(2)}) collective-permute-start(bf16[96,512]{1,0:T(8,128)(2,1)S(1)} %far_join_kernel.1.a), channel_id=1, source_target_pairs={{4,28},{12,4},{20,12},{28,20},{36,60},{44,36},{52,44},{60,52},{68,... | collective-permute-start | bytes 294920 | tf_op jit(solution)/shard_map/along/ppermute | solution.py:306
  26.7 1.0 %collective-permute-start.9 = (bf16[96,512]{1,0:T(8,128)(2,1)S(1)}, bf16[96,512]{1,0:T(8,128)(2,1)S(1)}, u32[]{:S(2)}, u32[]{:S(2)}) collective-permute-start(bf16[96,512]{1,0:T(8,128)(2,1)S(1)} %far_join_kernel.1.a), channel_id=1, source_target_pairs={{4,20},{12,28},{20,4},{28,12},{36,52},{44,60},{52,36},{60,44},{68,... | collective-permute-start | bytes 294920 | tf_op jit(solution)/shard_map/along/ppermute | solution.py:306
  27.8 2.4 %plane_kernel.1 = (f32[256,256]{1,0:T(8,128)S(1)}, f32[8,512]{1,0:T(8,128)S(1)}, f32[256,256]{1,0:T(8,128)S(1)}, f32[8,512]{1,0:T(8,128)S(1)}) custom-call(s32[4,16]{1,0:T(4,128)S(1)} %copy-done.4, bf16[256,512]{1,0:T(8,128)(2,1)S(1)} %get-tuple-element.42.qt, f32[256,256]{1,0:T(8,128)S(1)} %get-tuple-element.43.acc0, ...), custom_call_target="tpu_custom_call" | custom-call | flops 1000000 | bytes 1000 | tf_op jit(solution)/shard_map/plane_kernel/pallas_call | solution.py:293
  30.4 1.1 %collective-permute-done.9.d = bf16[96,512]{1,0:T(8,128)(2,1)S(1)} collective-permute-done((bf16[96,512]{1,0:T(8,128)(2,1)S(1)}, bf16[96,512]{1,0:T(8,128)(2,1)S(1)}, u32[]{:S(2)}, u32[]{:S(2)}) %collective-permute-start.9) | collective-permute-done | bytes 98336 | tf_op jit(solution)/shard_map/along/ppermute | solution.py:306
  32.1 0.8 %collective-permute-start.12 = (bf16[384,512]{1,0:T(8,128)(2,1)S(1)}, bf16[384,512]{1,0:T(8,128)(2,1)S(1)}, u32[]{:S(2)}, u32[]{:S(2)}) collective-permute-start(bf16[384,512]{1,0:T(8,128)(2,1)S(1)} %row_join_kernel.1.mine), channel_id=1, source_target_pairs={{0,4},{4,0},{8,12},{12,8},{16,20},{20,16},{24,28},{28,24},{32,36},... | collective-permute-start | bytes 1179656 | tf_op jit(solution)/shard_map/swap_far/ppermute | solution.py:306
  32.9 1.3 %collective-permute-done.12.other = bf16[384,512]{1,0:T(8,128)(2,1)S(1)} collective-permute-done((bf16[384,512]{1,0:T(8,128)(2,1)S(1)}, bf16[384,512]{1,0:T(8,128)(2,1)S(1)}, u32[]{:S(2)}, u32[]{:S(2)}) %collective-permute-start.12) | collective-permute-done | bytes 393248 | tf_op jit(solution)/shard_map/swap_far/ppermute | solution.py:306
  34.3 1.6 %far_kernel.2.mine_att = bf16[256,256]{1,0:T(8,128)(2,1)S(1)} custom-call(s32[4,16]{1,0:T(4,128)S(1)} %copy-done.4, bf16[256,512]{1,0:T(8,128)(2,1)S(1)} %get-tuple-element.42.qt, f32[256,256]{1,0:T(8,128)S(1)} %get-tuple-element.50.acc, f32[8,512]{1,0:T(8,128)S(1)} %get-tuple-element.51.refs_0_.ml, bf16[384,512]{1,0:T(8,128)(2,1)S(1)} %row_join_kernel.1.mine, ...), custom_call_target="tpu_custom_call" | custom-call | flops 1000000 | bytes 1000 | tf_op jit(solution)/shard_map/far_kernel/pallas_call | solution.py:293
  36.7 1.6 %far_kernel.3.mine_att = bf16[256,256]{1,0:T(8,128)(2,1)S(1)} custom-call(s32[4,16]{1,0:T(4,128)S(1)} %copy-done.4, bf16[256,512]{1,0:T(8,128)(2,1)S(1)} %get-tuple-element.42.qt, f32[256,256]{1,0:T(8,128)S(1)} %get-tuple-element.59.acc, f32[8,512]{1,0:T(8,128)S(1)} %get-tuple-element.60.ml, bf16[384,512]{1,0:T(8,128)(2,1)S(1)} %row_join_kernel.1.mine, ...), custom_call_target="tpu_custom_call" | custom-call | flops 1000000 | bytes 1000 | tf_op jit(solution)/shard_map/far_kernel/pallas_call | solution.py:293
  38.3 1.7 %collective-permute-start.15 = (bf16[256,256]{1,0:T(8,128)(2,1)S(1)}, bf16[256,256]{1,0:T(8,128)(2,1)S(1)}, u32[]{:S(2)}, u32[]{:S(2)}) collective-permute-start(bf16[256,256]{1,0:T(8,128)(2,1)S(1)} %far_kernel.3.mine_att), channel_id=1, source_target_pairs={{0,3},{3,0},{1,2},{2,1},{4,7},{7,4},{5,6},{6,5},{8,11},{11,8},{9,1... | collective-permute-start | bytes 393224 | tf_op jit(solution)/shard_map/ppermute | solution.py:412
  40.0 1.7 %collective-permute-done.13.peer_att = bf16[256,256]{1,0:T(8,128)(2,1)S(1)} collective-permute-done((bf16[256,256]{1,0:T(8,128)(2,1)S(1)}, bf16[256,256]{1,0:T(8,128)(2,1)S(1)}, u32[]{:S(2)}, u32[]{:S(2)}) %collective-permute-start.13) | collective-permute-done | bytes 131104 | tf_op jit(solution)/shard_map/ppermute | solution.py:412
  42.1 1.7 %collective-permute-start.14 = (bf16[256,256]{1,0:T(8,128)(2,1)S(1)}, bf16[256,256]{1,0:T(8,128)(2,1)S(1)}, u32[]{:S(2)}, u32[]{:S(2)}) collective-permute-start(bf16[256,256]{1,0:T(8,128)(2,1)S(1)} %get-tuple-element.58), channel_id=1, source_target_pairs={{0,3},{3,0},{1,2},{2,1},{4,7},{7,4},{5,6},{6,5},{8,11},{11,8},{9,1... | collective-permute-start | bytes 393224 | tf_op jit(solution)/shard_map/ppermute | solution.py:419
  43.8 1.3 %collective-permute-done.15.peer_att = bf16[256,256]{1,0:T(8,128)(2,1)S(1)} collective-permute-done((bf16[256,256]{1,0:T(8,128)(2,1)S(1)}, bf16[256,256]{1,0:T(8,128)(2,1)S(1)}, u32[]{:S(2)}, u32[]{:S(2)}) %collective-permute-start.15) | collective-permute-done | bytes 131104 | tf_op jit(solution)/shard_map/ppermute | solution.py:412
  45.8 2.5 %collective-permute-done.14 = bf16[256,256]{1,0:T(8,128)(2,1)S(1)} collective-permute-done((bf16[256,256]{1,0:T(8,128)(2,1)S(1)}, bf16[256,256]{1,0:T(8,128)(2,1)S(1)}, u32[]{:S(2)}, u32[]{:S(2)}) %collective-permute-start.14) | collective-permute-done | bytes 131104 | tf_op jit(solution)/shard_map/ppermute | solution.py:419
  48.4 2.1 %collective-permute-done.16 = bf16[256,256]{1,0:T(8,128)(2,1)S(1)} collective-permute-done((bf16[256,256]{1,0:T(8,128)(2,1)S(1)}, bf16[256,256]{1,0:T(8,128)(2,1)S(1)}, u32[]{:S(2)}, u32[]{:S(2)}) %collective-permute-start.16) | collective-permute-done | bytes 131104 | tf_op jit(solution)/shard_map/ppermute | solution.py:419
  (38 shorter events, 6.8 us)
Async XLA Ops:
  0.0 5.9 %copy-start = (bf16[512,1024]{1,0:T(8,128)(2,1)S(1)}, bf16[512,1024]{1,0:T(8,128)(2,1)}, u32[]{:S(2)}) copy-start(bf16[512,1024]{1,0:T(8,128)(2,1)} %tok.3) | copy-start | bytes 3145732
  0.0 1.1 %copy-start.3 = (bf16[1024,256]{1,0:T(8,128)(2,1)S(1)}, bf16[1024,256]{1,0:T(8,128)(2,1)}, u32[]{:S(2)}) copy-start(bf16[1024,256]{1,0:T(8,128)(2,1)} %wk_hbm.1) | copy-start | bytes 1572868
  1.1 4.7 %copy-start.2 = (bf16[1024,256]{1,0:T(8,128)(2,1)S(1)}, bf16[1024,256]{1,0:T(8,128)(2,1)}, u32[]{:S(2)}) copy-start(bf16[1024,256]{1,0:T(8,128)(2,1)} %wq.3) | copy-start | bytes 1572868
  4.2 4.5 %collective-permute-start = (bf16[176,512]{1,0:T(8,128)(2,1)S(1)}, bf16[176,512]{1,0:T(8,128)(2,1)S(1)}, u32[]{:S(2)}, u32[]{:S(2)}) collective-permute-start(bf16[176,512]{1,0:T(8,128)(2,1)S(1)} %get-tuple-element.41.share), channel_id=1, source_target_pairs={{0,4},{4,0},{8,12},{12,8},{16,20},{20,16},{24,28},{28,24},{32,36},... | collective-permute-start | bytes 540680 | tf_op jit(solution)/shard_map/swap_share/ppermute | solution.py:306
  4.3 1.6 %copy-start.4 = (s32[4,16]{1,0:T(4,128)S(1)}, s32[4,16]{1,0:T(4,128)}, u32[]{:S(2)}) copy-start(s32[4,16]{1,0:T(4,128)} %gate.9) | copy-start | bytes 772
  4.3 5.7 %collective-permute-start.1 = (bf16[96,512]{1,0:T(8,128)(2,1)S(1)}, bf16[96,512]{1,0:T(8,128)(2,1)S(1)}, u32[]{:S(2)}, u32[]{:S(2)}) collective-permute-start(bf16[96,512]{1,0:T(8,128)(2,1)S(1)} %get-tuple-element.46.sent), channel_id=1, source_target_pairs={{0,8},{4,12},{8,0},{12,4},{16,24},{20,28},{24,16},{28,20},{32,40},... | collective-permute-start | bytes 294920 | tf_op jit(solution)/shard_map/across_one/ppermute | solution.py:306
  8.6 3.8 %collective-permute-start.4 = (bf16[16,512]{1,0:T(8,128)(2,1)S(1)}, bf16[16,512]{1,0:T(8,128)(2,1)S(1)}, u32[]{:S(2)}, u32[]{:S(2)}) collective-permute-start(bf16[16,512]{1,0:T(8,128)(2,1)S(1)} %mirror_kernel.1.refs_5_), channel_id=1, source_target_pairs={{4,228},{12,236},{20,244},{28,252},{36,196},{44,204},{52,212},{60,... | collective-permute-start | bytes 49160 | tf_op jit(solution)/shard_map/planes_mirror/ppermute | solution.py:306
  12.5 3.9 %collective-permute-start.5 = (bf16[32,512]{1,0:T(8,128)(2,1)S(1)}, bf16[32,512]{1,0:T(8,128)(2,1)S(1)}, u32[]{:S(2)}, u32[]{:S(2)}) collective-permute-start(bf16[32,512]{1,0:T(8,128)(2,1)S(1)} %two_kernel.1.sent), channel_id=1, source_target_pairs={{4,68},{12,76},{20,84},{28,92},{36,100},{44,108},{52,116},{60,124}... | collective-permute-start | bytes 98312 | tf_op jit(solution)/shard_map/planes_two/ppermute | solution.py:306
  16.4 4.3 %collective-permute-start.6 = (bf16[64,512]{1,0:T(8,128)(2,1)S(1)}, bf16[64,512]{1,0:T(8,128)(2,1)S(1)}, u32[]{:S(2)}, u32[]{:S(2)}) collective-permute-start(bf16[64,512]{1,0:T(8,128)(2,1)S(1)} %joint_kernel.1.sent), channel_id=1, source_target_pairs={{4,36},{12,44},{20,52},{28,60},{36,4},{44,12},{52,20},{60,28},{68,... | collective-permute-start | bytes 196616 | tf_op jit(solution)/shard_map/planes_one/ppermute | solution.py:306
  17.0 7.5 %collective-permute-start.2 = (bf16[64,512]{1,0:T(8,128)(2,1)S(1)}, bf16[64,512]{1,0:T(8,128)(2,1)S(1)}, u32[]{:S(2)}, u32[]{:S(2)}) collective-permute-start(bf16[64,512]{1,0:T(8,128)(2,1)S(1)} %near_join_kernel.1), channel_id=1, source_target_pairs={{0,16},{4,20},{8,24},{12,28},{16,0},{20,4},{24,8},{28,12},{32,48},... | collective-permute-start | bytes 196616 | tf_op jit(solution)/shard_map/across_two/ppermute | solution.py:306
  20.7 10.8 %collective-permute-start.10 = (bf16[256,512]{1,0:T(8,128)(2,1)S(1)}, bf16[256,512]{1,0:T(8,128)(2,1)S(1)}, u32[]{:S(2)}, u32[]{:S(2)}) collective-permute-start(bf16[256,512]{1,0:T(8,128)(2,1)S(1)} %get-tuple-element.55), channel_id=1, source_target_pairs={{0,1},{1,0},{2,3},{3,2},{4,5},{5,4},{6,7},{7,6},{8,9},{9,8},{10,11... | collective-permute-start | bytes 786440 | tf_op jit(solution)/shard_map/ppermute | solution.py:386
  22.3 9.8 %collective-permute-start.11 = (bf16[256,512]{1,0:T(8,128)(2,1)S(1)}, bf16[256,512]{1,0:T(8,128)(2,1)S(1)}, u32[]{:S(2)}, u32[]{:S(2)}) collective-permute-start(bf16[256,512]{1,0:T(8,128)(2,1)S(1)} %get-tuple-element.56), channel_id=1, source_target_pairs={{0,3},{3,0},{1,2},{2,1},{4,7},{7,4},{5,6},{6,5},{8,11},{11,8},{9,1... | collective-permute-start | bytes 786440 | tf_op jit(solution)/shard_map/ppermute | solution.py:387
  24.5 2.2 %collective-permute-start.3 = (bf16[128,512]{1,0:T(8,128)(2,1)S(1)}, bf16[128,512]{1,0:T(8,128)(2,1)S(1)}, u32[]{:S(2)}, u32[]{:S(2)}) collective-permute-start(bf16[128,512]{1,0:T(8,128)(2,1)S(1)} %plane_join_kernel.1), channel_id=1, source_target_pairs={{0,4},{4,0},{8,12},{12,8},{16,20},{20,16},{24,28},{28,24},{32,36},... | collective-permute-start | bytes 393224 | tf_op jit(solution)/shard_map/swap_near/ppermute | solution.py:306
  24.7 5.6 %collective-permute-start.7 = (bf16[96,512]{1,0:T(8,128)(2,1)S(1)}, bf16[96,512]{1,0:T(8,128)(2,1)S(1)}, u32[]{:S(2)}, u32[]{:S(2)}) collective-permute-start(bf16[96,512]{1,0:T(8,128)(2,1)S(1)} %far_join_kernel.1.a), channel_id=1, source_target_pairs={{4,12},{12,20},{20,28},{28,4},{36,44},{44,52},{52,60},{60,36},{68,... | collective-permute-start | bytes 294920 | tf_op jit(solution)/shard_map/along/ppermute | solution.py:306
  25.8 4.6 %collective-permute-start.8 = (bf16[96,512]{1,0:T(8,128)(2,1)S(1)}, bf16[96,512]{1,0:T(8,128)(2,1)S(1)}, u32[]{:S(2)}, u32[]{:S(2)}) collective-permute-start(bf16[96,512]{1,0:T(8,128)(2,1)S(1)} %far_join_kernel.1.a), channel_id=1, source_target_pairs={{4,28},{12,4},{20,12},{28,20},{36,60},{44,36},{52,44},{60,52},{68,... | collective-permute-start | bytes 294920 | tf_op jit(solution)/shard_map/along/ppermute | solution.py:306
  26.7 4.7 %collective-permute-start.9 = (bf16[96,512]{1,0:T(8,128)(2,1)S(1)}, bf16[96,512]{1,0:T(8,128)(2,1)S(1)}, u32[]{:S(2)}, u32[]{:S(2)}) collective-permute-start(bf16[96,512]{1,0:T(8,128)(2,1)S(1)} %far_join_kernel.1.a), channel_id=1, source_target_pairs={{4,20},{12,28},{20,4},{28,12},{36,52},{44,60},{52,36},{60,44},{68,... | collective-permute-start | bytes 294920 | tf_op jit(solution)/shard_map/along/ppermute | solution.py:306
  32.1 2.1 %collective-permute-start.12 = (bf16[384,512]{1,0:T(8,128)(2,1)S(1)}, bf16[384,512]{1,0:T(8,128)(2,1)S(1)}, u32[]{:S(2)}, u32[]{:S(2)}) collective-permute-start(bf16[384,512]{1,0:T(8,128)(2,1)S(1)} %row_join_kernel.1.mine), channel_id=1, source_target_pairs={{0,4},{4,0},{8,12},{12,8},{16,20},{20,16},{24,28},{28,24},{32,36},... | collective-permute-start | bytes 1179656 | tf_op jit(solution)/shard_map/swap_far/ppermute | solution.py:306
  35.9 5.9 %collective-permute-start.13 = (bf16[256,256]{1,0:T(8,128)(2,1)S(1)}, bf16[256,256]{1,0:T(8,128)(2,1)S(1)}, u32[]{:S(2)}, u32[]{:S(2)}) collective-permute-start(bf16[256,256]{1,0:T(8,128)(2,1)S(1)} %far_kernel.2.mine_att), channel_id=1, source_target_pairs={{0,1},{1,0},{2,3},{3,2},{4,5},{5,4},{6,7},{7,6},{8,9},{9,8},{10,11... | collective-permute-start | bytes 393224 | tf_op jit(solution)/shard_map/ppermute | solution.py:412
  36.7 5.1 %copy-start.1 = (bf16[256,1024]{1,0:T(8,128)(2,1)S(1)}, bf16[256,1024]{1,0:T(8,128)(2,1)}, u32[]{:S(2)}) copy-start(bf16[256,1024]{1,0:T(8,128)(2,1)} %mine_w.3) | copy-start | bytes 1572868
  38.3 6.8 %collective-permute-start.15 = (bf16[256,256]{1,0:T(8,128)(2,1)S(1)}, bf16[256,256]{1,0:T(8,128)(2,1)S(1)}, u32[]{:S(2)}, u32[]{:S(2)}) collective-permute-start(bf16[256,256]{1,0:T(8,128)(2,1)S(1)} %far_kernel.3.mine_att), channel_id=1, source_target_pairs={{0,3},{3,0},{1,2},{2,1},{4,7},{7,4},{5,6},{6,5},{8,11},{11,8},{9,1... | collective-permute-start | bytes 393224 | tf_op jit(solution)/shard_map/ppermute | solution.py:412
  42.1 6.3 %collective-permute-start.14 = (bf16[256,256]{1,0:T(8,128)(2,1)S(1)}, bf16[256,256]{1,0:T(8,128)(2,1)S(1)}, u32[]{:S(2)}, u32[]{:S(2)}) collective-permute-start(bf16[256,256]{1,0:T(8,128)(2,1)S(1)} %get-tuple-element.58), channel_id=1, source_target_pairs={{0,3},{3,0},{1,2},{2,1},{4,7},{7,4},{5,6},{6,5},{8,11},{11,8},{9,1... | collective-permute-start | bytes 393224 | tf_op jit(solution)/shard_map/ppermute | solution.py:419
  45.4 5.1 %collective-permute-start.16 = (bf16[256,256]{1,0:T(8,128)(2,1)S(1)}, bf16[256,256]{1,0:T(8,128)(2,1)S(1)}, u32[]{:S(2)}, u32[]{:S(2)}) collective-permute-start(bf16[256,256]{1,0:T(8,128)(2,1)S(1)} %get-tuple-element.62), channel_id=1, source_target_pairs={{0,1},{1,0},{2,3},{3,2},{4,5},{5,4},{6,7},{7,6},{8,9},{9,8},{10,11... | collective-permute-start | bytes 393224 | tf_op jit(solution)/shard_map/ppermute | solution.py:419

commit v3 on v2

--- a/solution.py
+++ b/solution.py
@@ -142,8 +142,20 @@
     return array.astype(F32).T.astype(BF16)
 
 
-def gate_bias(gate, block, level):
-    return jnp.where(gate[block, level] == 1, jnp.float32(level * LOG_TWO), jnp.float32(NEG))
+def bias_kernel(gate, out):
+    seq = lax.axis_index("seq")
+    for b in range(4):
+        for level in range(8):
+            used = gate[b : b + 1, level : level + 1] == 1
+            bias = jnp.where(used, jnp.float32(level * LOG_TWO), jnp.float32(NEG))
+            if level >= 2:
+                bit = lax.shift_right_logical(seq, level - 2) % 2
+                bias = jnp.where(bit == 1, bias, jnp.float32(NEG))
+            out[b * 8 + level : b * 8 + level + 1, :] = jnp.broadcast_to(bias, (1, BLOCK))
+
+
+def gate_bias(bias, block, level):
+    return bias[block * 8 + level : block * 8 + level + 1, :]
 
 
 def attend(query_t, keys, values_t, biases, mask, old, old_top, old_total):
@@ -233,13 +245,8 @@
             out[...] = source[...]
 
 
-def level_biases(gate, block, first):
-    seq = lax.axis_index("seq")
-    out = []
-    for level in range(first, first + 3):
-        bit = lax.shift_right_logical(seq, level - 2) % 2
-        out.append(jnp.where(bit == 1, gate_bias(gate, block, level), jnp.float32(NEG)))
-    return out
+def level_biases(bias, block, first):
+    return [gate_bias(bias, block, level) for level in range(first, first + 3)]
 
 
 def cross(b, first, gate, qt, acc, ml, keys, values_t):
@@ -264,7 +271,7 @@
         ml_out[4 + step : 5 + step, :] = jnp.concatenate(totals, axis=1)
 
 
-def far_kernel(half, gate, qt, acc, ml, mine, other, att):
+def far_kernel(half, gate, qt, acc, ml, mine, other, after, att):
     rows = jnp.where(my_core() == 1, mine[...], other[...])
     keys = rows[:, :WIDTH]
     values_t = turn(rows[:, WIDTH:])
@@ -284,17 +291,16 @@
 
 
 VMEM = pl.BlockSpec(memory_space=pltpu.VMEM)
-SMEM = pl.BlockSpec(memory_space=pltpu.SMEM)
 ANY = pl.BlockSpec(memory_space=pl.ANY)
 HBM = pl.BlockSpec(memory_space=pltpu.HBM)
 
 
-def call(kernel, args, outs, flops, smem=0, unread=0):
+def call(kernel, args, outs, flops, unread=0):
     return pl.pallas_call(
         kernel,
         name=getattr(kernel, "func", kernel).__name__,
         out_shape=[jax.ShapeDtypeStruct(shape, dtype) for shape, dtype in outs],
-        in_specs=[SMEM] * smem + [VMEM] * (len(args) - smem - unread) + [ANY] * unread,
+        in_specs=[VMEM] * (len(args) - unread) + [ANY] * unread,
         out_specs=[VMEM] * len(outs),
         compiler_params=pltpu.CompilerParams(vmem_limit_bytes=24 * 1024 * 1024),
         cost_estimate=pl.CostEstimate(flops=flops, bytes_accessed=1000, transcendentals=0),
@@ -360,11 +366,12 @@
     first = across(e1, 1, "across_one")
     state = [((WIDTH, 256), F32), ((8, 512), F32)]
     held = [((WIDTH, 512), BF16)] + state * 2
-    early = call(early_kernel, (gate, tokens, wq, kv, l1), held, COST, smem=1)
+    (gate,) = call(bias_kernel, (gate,), [((32, BLOCK), F32)], COST)
+    early = call(early_kernel, (gate, tokens, wq, kv, l1), held, COST)
     (pay,) = call(mirror_kernel, (share, share_other, early[2]), [rows(16)], COST, unread=1)
     far5 = hub(pay, lambda z, x: (7 - z, x), idle_x, "planes_mirror")
     qt, acc0, ml0, acc1, ml1 = call(
-        late_kernel, (gate, tokens, wq, kv, l1, *early, pay), held, COST, smem=1, unread=1
+        late_kernel, (gate, tokens, wq, kv, l1, *early, pay), held, COST, unread=1
     )
     own = [(acc0, ml0), (acc1, ml1)]
     first, ml = lax.optimization_barrier((first, own[1][1]))
@@ -390,7 +397,6 @@
         (gate, qt, *own[0], *own[1], share_other, first, second, other),
         state * 2,
         COST,
-        smem=1,
     )
     others = [hub(far, lambda z, x, shift=shift: (z, x + shift), idle_z, "along") for shift in (1, -1, 2)]
     (far,) = call(row_join_kernel, (far, *others, ml0, w_next, w_far), [rows(384)], COST, unread=3)
@@ -398,12 +404,13 @@
     held = ((acc0, ml0), (acc1, ml1))
     halves = []
     for half in range(2):
+        after = far_other if half == 0 else halves[0]
         (att,) = call(
             functools.partial(far_kernel, half),
-            (gate, qt, *held[half], far, far_other),
+            (gate, qt, *held[half], far, far_other, after),
             [((256, WIDTH), BF16)],
             COST,
-            smem=1,
+            unread=1,
         )
         halves.append(att)
     out = []

time: 51.3 us -> 49.8 us (0.971)
  Pallas kernels: 12.7 us -> 9.99 us
  waiting for transfers between devices: 17.5 us -> 18.7 us
    pallas_call x14 -> x15, Pallas kernels: 9.71 us -> 6.96 us  [call(): pl.pallas_call(kernel, name=getattr(kernel, 'func', kernel).__name__, out...]
    ppermute x11, waiting for transfers between devices: 9.12 us -> 10.4 us  [move(): return lax.ppermute(array, 'seq', pairs)]
  transfers between devices with their start and end apart: 17 -> 17, of which waited for: 11 -> 12; matrix products, arithmetic and copies ran while one was open for 0% -> 0% of each run, Pallas kernels for 16% -> 12%
where the time goes in v3:
time: 49.8 us; the launch traced here: 49.6 us
  starting transfers between devices  18.8 us (38%)
  waiting for transfers between devices  18.7 us (38%)
  Pallas kernels  9.99 us (20%)
  local copies, waits for them, and re-layouts  1.15 us (2%)
  other arithmetic  0.77 us (2%)
    ppermute x11, starting transfers between devices, move(): return lax.ppermute(array, 'seq', pairs)  10.4 us
    ppermute x11, waiting for transfers between devices, move(): return lax.ppermute(array, 'seq', pairs)  10.4 us
    pallas_call x15, Pallas kernels, call(): pl.pallas_call(kernel, name=getattr(kernel, 'func', kernel).__name__, out...  6.96 us
    ppermute x2, waiting for transfers between devices, shards(): out.append(keep + lax.ppermute(send, 'head', pairs[1 - half]).astype(F32))  4.8 us
    pallas_call x1, Pallas kernels, shards(): pl.pallas_call(load_kernel, name='load_kernel', out_shape=[jax.ShapeDtype...  3.02 us
    ppermute x2, waiting for transfers between devices, shards(): peer = lax.ppermute(halves[half], 'head', pairs[half])  2.9 us
    ppermute x2, starting transfers between devices, shards(): peer = lax.ppermute(halves[half], 'head', pairs[half])  2.59 us
    ppermute x1, starting transfers between devices, shards(): w_far = lax.ppermute(to_far, 'head', PAIR_FAR)  2.18 us
  transfers between devices with their start and end apart: 17, of which 12 were waited for; matrix products, arithmetic and copies ran while one was open for 0% of the time, Pallas kernels for 12%

profile of v3, /device:TPU:32, one launch (start us, length us, event | category | flops | bytes accessed | tf_op | source)
XLA Modules:
  0.0 49.6 jit_solution(9564938901717746235)
XLA Ops:
  0.0 1.1 %copy-done.3 = bf16[1024,256]{1,0:T(8,128)(2,1)S(1)} copy-done((bf16[1024,256]{1,0:T(8,128)(2,1)S(1)}, bf16[1024,256]{1,0:T(8,128)(2,1)}, u32[]{:S(2)}) %copy-start.3) | copy-done | bytes 524312
  1.1 3.0 %load_kernel.1 = (bf16[512,512]{1,0:T(8,128)(2,1)S(1)}, bf16[128,512]{1,0:T(8,128)(2,1)S(1)}, bf16[96,512]{1,0:T(8,128)(2,1)S(1)}, bf16[176,512]{1,0:T(8,128)(2,...) custom-call(bf16[512,1024]{1,0:T(8,128)(2,1)} %tok.3, bf16[1024,256]{1,0:T(8,128)(2,1)S(1)} %copy-done.3, ...), custom_call_target="tpu_custom_call" | custom-call | flops 1000000 | bytes 1000 | tf_op jit(solution)/shard_map/load_kernel/pallas_call | solution.py:346
  4.3 1.6 %collective-permute-start.1 = (bf16[96,512]{1,0:T(8,128)(2,1)S(1)}, bf16[96,512]{1,0:T(8,128)(2,1)S(1)}, u32[]{:S(2)}, u32[]{:S(2)}) collective-permute-start(bf16[96,512]{1,0:T(8,128)(2,1)S(1)} %get-tuple-element.46.sent), channel_id=1, source_target_pairs={{0,8},{4,12},{8,0},{12,4},{16,24},{20,28},{24,16},{28,20},{32,40},... | collective-permute-start | bytes 294920 | tf_op jit(solution)/shard_map/across_one/ppermute | solution.py:312
  6.0 2.2 %early_kernel.1 = (bf16[256,512]{1,0:T(8,128)(2,1)S(1)}, f32[256,256]{1,0:T(8,128)S(1)}, f32[8,512]{1,0:T(8,128)S(1)}, f32[256,256]{1,0:T(8,128)S(1)}, f32[8,512]{1,0:T(8,128)S(1)}) custom-call(f32[32,128]{1,0:T(8,128)S(1)} %bias_kernel.1.gate, bf16[512,1024]{1,0:T(8,128)(2,1)S(1)} %copy-done, bf16[1024,256]{1,0:T(8,128)(2,1)S(1)} %copy-done.2, ...), custom_call_target="tpu_custom_call" | custom-call | flops 1000000 | bytes 1000 | tf_op jit(solution)/shard_map/early_kernel/pallas_call | solution.py:299
  9.5 2.5 %collective-permute-done.4.got = bf16[16,512]{1,0:T(8,128)(2,1)S(1)} collective-permute-done((bf16[16,512]{1,0:T(8,128)(2,1)S(1)}, bf16[16,512]{1,0:T(8,128)(2,1)S(1)}, u32[]{:S(2)}, u32[]{:S(2)}) %collective-permute-start.4) | collective-permute-done | bytes 16416 | tf_op jit(solution)/shard_map/planes_mirror/ppermute | solution.py:312
  12.6 3.4 %collective-permute-done.5.got = bf16[32,512]{1,0:T(8,128)(2,1)S(1)} collective-permute-done((bf16[32,512]{1,0:T(8,128)(2,1)S(1)}, bf16[32,512]{1,0:T(8,128)(2,1)S(1)}, u32[]{:S(2)}, u32[]{:S(2)}) %collective-permute-start.5) | collective-permute-done | bytes 32800 | tf_op jit(solution)/shard_map/planes_two/ppermute | solution.py:312
  16.5 3.0 %collective-permute-start.2 = (bf16[64,512]{1,0:T(8,128)(2,1)S(1)}, bf16[64,512]{1,0:T(8,128)(2,1)S(1)}, u32[]{:S(2)}, u32[]{:S(2)}) collective-permute-start(bf16[64,512]{1,0:T(8,128)(2,1)S(1)} %near_join_kernel.1), channel_id=1, source_target_pairs={{0,16},{4,20},{8,24},{12,28},{16,0},{20,4},{24,8},{28,12},{32,48},... | collective-permute-start | bytes 196616 | tf_op jit(solution)/shard_map/across_two/ppermute | solution.py:312
  20.2 1.7 %collective-permute-start.10 = (bf16[256,512]{1,0:T(8,128)(2,1)S(1)}, bf16[256,512]{1,0:T(8,128)(2,1)S(1)}, u32[]{:S(2)}, u32[]{:S(2)}) collective-permute-start(bf16[256,512]{1,0:T(8,128)(2,1)S(1)} %get-tuple-element.55), channel_id=1, source_target_pairs={{0,1},{1,0},{2,3},{3,2},{4,5},{5,4},{6,7},{7,6},{8,9},{9,8},{10,11... | collective-permute-start | bytes 786440 | tf_op jit(solution)/shard_map/ppermute | solution.py:393
  21.9 2.2 %collective-permute-start.11 = (bf16[256,512]{1,0:T(8,128)(2,1)S(1)}, bf16[256,512]{1,0:T(8,128)(2,1)S(1)}, u32[]{:S(2)}, u32[]{:S(2)}) collective-permute-start(bf16[256,512]{1,0:T(8,128)(2,1)S(1)} %get-tuple-element.56), channel_id=1, source_target_pairs={{0,3},{3,0},{1,2},{2,1},{4,7},{7,4},{5,6},{6,5},{8,11},{11,8},{9,1... | collective-permute-start | bytes 786440 | tf_op jit(solution)/shard_map/ppermute | solution.py:394
  24.2 1.1 %collective-permute-start.7 = (bf16[96,512]{1,0:T(8,128)(2,1)S(1)}, bf16[96,512]{1,0:T(8,128)(2,1)S(1)}, u32[]{:S(2)}, u32[]{:S(2)}) collective-permute-start(bf16[96,512]{1,0:T(8,128)(2,1)S(1)} %far_join_kernel.1.a), channel_id=1, source_target_pairs={{4,12},{12,20},{20,28},{28,4},{36,44},{44,52},{52,60},{60,36},{68,... | collective-permute-start | bytes 294920 | tf_op jit(solution)/shard_map/along/ppermute | solution.py:312
  25.3 1.0 %collective-permute-start.8 = (bf16[96,512]{1,0:T(8,128)(2,1)S(1)}, bf16[96,512]{1,0:T(8,128)(2,1)S(1)}, u32[]{:S(2)}, u32[]{:S(2)}) collective-permute-start(bf16[96,512]{1,0:T(8,128)(2,1)S(1)} %far_join_kernel.1.a), channel_id=1, source_target_pairs={{4,28},{12,4},{20,12},{28,20},{36,60},{44,36},{52,44},{60,52},{68,... | collective-permute-start | bytes 294920 | tf_op jit(solution)/shard_map/along/ppermute | solution.py:312
  26.3 1.1 %collective-permute-start.9 = (bf16[96,512]{1,0:T(8,128)(2,1)S(1)}, bf16[96,512]{1,0:T(8,128)(2,1)S(1)}, u32[]{:S(2)}, u32[]{:S(2)}) collective-permute-start(bf16[96,512]{1,0:T(8,128)(2,1)S(1)} %far_join_kernel.1.a), channel_id=1, source_target_pairs={{4,20},{12,28},{20,4},{28,12},{36,52},{44,60},{52,36},{60,44},{68,... | collective-permute-start | bytes 294920 | tf_op jit(solution)/shard_map/along/ppermute | solution.py:312
  27.4 1.9 %plane_kernel.1 = (f32[256,256]{1,0:T(8,128)S(1)}, f32[8,512]{1,0:T(8,128)S(1)}, f32[256,256]{1,0:T(8,128)S(1)}, f32[8,512]{1,0:T(8,128)S(1)}) custom-call(f32[32,128]{1,0:T(8,128)S(1)} %bias_kernel.1.gate, bf16[256,512]{1,0:T(8,128)(2,1)S(1)} %get-tuple-element.42.qt, f32[256,256]{1,0:T(8,128)S(1)} %get-tuple-element.43.acc0, ...), custom_call_target="tpu_custom_call" | custom-call | flops 1000000 | bytes 1000 | tf_op jit(solution)/shard_map/plane_kernel/pallas_call | solution.py:299
  29.9 1.1 %collective-permute-done.9.d = bf16[96,512]{1,0:T(8,128)(2,1)S(1)} collective-permute-done((bf16[96,512]{1,0:T(8,128)(2,1)S(1)}, bf16[96,512]{1,0:T(8,128)(2,1)S(1)}, u32[]{:S(2)}, u32[]{:S(2)}) %collective-permute-start.9) | collective-permute-done | bytes 98336 | tf_op jit(solution)/shard_map/along/ppermute | solution.py:312
  31.7 0.8 %collective-permute-start.12 = (bf16[384,512]{1,0:T(8,128)(2,1)S(1)}, bf16[384,512]{1,0:T(8,128)(2,1)S(1)}, u32[]{:S(2)}, u32[]{:S(2)}) collective-permute-start(bf16[384,512]{1,0:T(8,128)(2,1)S(1)} %row_join_kernel.1.mine), channel_id=1, source_target_pairs={{0,4},{4,0},{8,12},{12,8},{16,20},{20,16},{24,28},{28,24},{32,36},... | collective-permute-start | bytes 1179656 | tf_op jit(solution)/shard_map/swap_far/ppermute | solution.py:312
  32.5 1.3 %collective-permute-done.12.other.after = bf16[384,512]{1,0:T(8,128)(2,1)S(1)} collective-permute-done((bf16[384,512]{1,0:T(8,128)(2,1)S(1)}, bf16[384,512]{1,0:T(8,128)(2,1)S(1)}, u32[]{:S(2)}, u32[]{:S(2)}) %collective-permute-start.12) | collective-permute-done | bytes 393248 | tf_op jit(solution)/shard_map/swap_far/ppermute | solution.py:312
  33.8 1.0 %far_kernel.2.mine_att.after = bf16[256,256]{1,0:T(8,128)(2,1)S(1)} custom-call(f32[32,128]{1,0:T(8,128)S(1)} %bias_kernel.1.gate, bf16[256,512]{1,0:T(8,128)(2,1)S(1)} %get-tuple-element.42.qt, f32[256,256]{1,0:T(8,128)S(1)} %get-tuple-element.50.acc, f32[8,512]{1,0:T(8,128)S(1)} %get-tuple-element.51.refs_0_.ml, bf16[384,512]{1,0:T(8,128)(2,1)S(1)} %row_join_kernel.1.mine, ...), custom_call_target="tpu_custom_call" | custom-call | flops 1000000 | bytes 1000 | tf_op jit(solution)/shard_map/far_kernel/pallas_call | solution.py:299
  34.9 0.8 %collective-permute-start.13 = (bf16[256,256]{1,0:T(8,128)(2,1)S(1)}, bf16[256,256]{1,0:T(8,128)(2,1)S(1)}, u32[]{:S(2)}, u32[]{:S(2)}) collective-permute-start(bf16[256,256]{1,0:T(8,128)(2,1)S(1)} %far_kernel.2.mine_att.after), channel_id=1, source_target_pairs={{0,1},{1,0},{2,3},{3,2},{4,5},{5,4},{6,7},{7,6},{8,9},{9,8},{10,11... | collective-permute-start | bytes 393224 | tf_op jit(solution)/shard_map/ppermute | solution.py:419
  35.7 1.1 %far_kernel.3.mine_att = bf16[256,256]{1,0:T(8,128)(2,1)S(1)} custom-call(f32[32,128]{1,0:T(8,128)S(1)} %bias_kernel.1.gate, bf16[256,512]{1,0:T(8,128)(2,1)S(1)} %get-tuple-element.42.qt, f32[256,256]{1,0:T(8,128)S(1)} %get-tuple-element.59.acc, f32[8,512]{1,0:T(8,128)S(1)} %get-tuple-element.60.ml, bf16[384,512]{1,0:T(8,128)(2,1)S(1)} %row_join_kernel.1.mine, ...), custom_call_target="tpu_custom_call" | custom-call | flops 1000000 | bytes 1000 | tf_op jit(solution)/shard_map/far_kernel/pallas_call | solution.py:299
  36.7 1.8 %collective-permute-start.15 = (bf16[256,256]{1,0:T(8,128)(2,1)S(1)}, bf16[256,256]{1,0:T(8,128)(2,1)S(1)}, u32[]{:S(2)}, u32[]{:S(2)}) collective-permute-start(bf16[256,256]{1,0:T(8,128)(2,1)S(1)} %far_kernel.3.mine_att), channel_id=1, source_target_pairs={{0,3},{3,0},{1,2},{2,1},{4,7},{7,4},{5,6},{6,5},{8,11},{11,8},{9,1... | collective-permute-start | bytes 393224 | tf_op jit(solution)/shard_map/ppermute | solution.py:419
  38.5 2.2 %collective-permute-done.13.peer_att = bf16[256,256]{1,0:T(8,128)(2,1)S(1)} collective-permute-done((bf16[256,256]{1,0:T(8,128)(2,1)S(1)}, bf16[256,256]{1,0:T(8,128)(2,1)S(1)}, u32[]{:S(2)}, u32[]{:S(2)}) %collective-permute-start.13) | collective-permute-done | bytes 131104 | tf_op jit(solution)/shard_map/ppermute | solution.py:419
  41.0 1.8 %collective-permute-start.14 = (bf16[256,256]{1,0:T(8,128)(2,1)S(1)}, bf16[256,256]{1,0:T(8,128)(2,1)S(1)}, u32[]{:S(2)}, u32[]{:S(2)}) collective-permute-start(bf16[256,256]{1,0:T(8,128)(2,1)S(1)} %get-tuple-element.58), channel_id=1, source_target_pairs={{0,3},{3,0},{1,2},{2,1},{4,7},{7,4},{5,6},{6,5},{8,11},{11,8},{9,1... | collective-permute-start | bytes 393224 | tf_op jit(solution)/shard_map/ppermute | solution.py:426
  44.0 3.3 %collective-permute-done.14 = bf16[256,256]{1,0:T(8,128)(2,1)S(1)} collective-permute-done((bf16[256,256]{1,0:T(8,128)(2,1)S(1)}, bf16[256,256]{1,0:T(8,128)(2,1)S(1)}, u32[]{:S(2)}, u32[]{:S(2)}) %collective-permute-start.14) | collective-permute-done | bytes 131104 | tf_op jit(solution)/shard_map/ppermute | solution.py:426
  47.3 1.5 %collective-permute-done.16 = bf16[256,256]{1,0:T(8,128)(2,1)S(1)} collective-permute-done((bf16[256,256]{1,0:T(8,128)(2,1)S(1)}, bf16[256,256]{1,0:T(8,128)(2,1)S(1)}, u32[]{:S(2)}, u32[]{:S(2)}) %collective-permute-start.16) | collective-permute-done | bytes 131104 | tf_op jit(solution)/shard_map/ppermute | solution.py:426
  (39 shorter events, 7.1 us)
Async XLA Ops:
  0.0 6.0 %copy-start = (bf16[512,1024]{1,0:T(8,128)(2,1)S(1)}, bf16[512,1024]{1,0:T(8,128)(2,1)}, u32[]{:S(2)}) copy-start(bf16[512,1024]{1,0:T(8,128)(2,1)} %tok.3) | copy-start | bytes 3145732
  0.0 1.1 %copy-start.3 = (bf16[1024,256]{1,0:T(8,128)(2,1)S(1)}, bf16[1024,256]{1,0:T(8,128)(2,1)}, u32[]{:S(2)}) copy-start(bf16[1024,256]{1,0:T(8,128)(2,1)} %wk_hbm.1) | copy-start | bytes 1572868
  1.1 4.9 %copy-start.2 = (bf16[1024,256]{1,0:T(8,128)(2,1)S(1)}, bf16[1024,256]{1,0:T(8,128)(2,1)}, u32[]{:S(2)}) copy-start(bf16[1024,256]{1,0:T(8,128)(2,1)} %wq.3) | copy-start | bytes 1572868
  4.2 1.7 %copy-start.4 = (s32[4,16]{1,0:T(4,128)S(1)}, s32[4,16]{1,0:T(4,128)}, u32[]{:S(2)}) copy-start(s32[4,16]{1,0:T(4,128)} %gate.1) | copy-start | bytes 772
  4.2 4.0 %collective-permute-start = (bf16[176,512]{1,0:T(8,128)(2,1)S(1)}, bf16[176,512]{1,0:T(8,128)(2,1)S(1)}, u32[]{:S(2)}, u32[]{:S(2)}) collective-permute-start(bf16[176,512]{1,0:T(8,128)(2,1)S(1)} %get-tuple-element.41.share), channel_id=1, source_target_pairs={{0,4},{4,0},{8,12},{12,8},{16,20},{20,16},{24,28},{28,24},{32,36},... | collective-permute-start | bytes 540680 | tf_op jit(solution)/shard_map/swap_share/ppermute | solution.py:312
  4.3 5.2 %collective-permute-start.1 = (bf16[96,512]{1,0:T(8,128)(2,1)S(1)}, bf16[96,512]{1,0:T(8,128)(2,1)S(1)}, u32[]{:S(2)}, u32[]{:S(2)}) collective-permute-start(bf16[96,512]{1,0:T(8,128)(2,1)S(1)} %get-tuple-element.46.sent), channel_id=1, source_target_pairs={{0,8},{4,12},{8,0},{12,4},{16,24},{20,28},{24,16},{28,20},{32,40},... | collective-permute-start | bytes 294920 | tf_op jit(solution)/shard_map/across_one/ppermute | solution.py:312
  8.2 3.8 %collective-permute-start.4 = (bf16[16,512]{1,0:T(8,128)(2,1)S(1)}, bf16[16,512]{1,0:T(8,128)(2,1)S(1)}, u32[]{:S(2)}, u32[]{:S(2)}) collective-permute-start(bf16[16,512]{1,0:T(8,128)(2,1)S(1)} %mirror_kernel.1.refs_5_), channel_id=1, source_target_pairs={{4,228},{12,236},{20,244},{28,252},{36,196},{44,204},{52,212},{60,... | collective-permute-start | bytes 49160 | tf_op jit(solution)/shard_map/planes_mirror/ppermute | solution.py:312
  12.0 3.9 %collective-permute-start.5 = (bf16[32,512]{1,0:T(8,128)(2,1)S(1)}, bf16[32,512]{1,0:T(8,128)(2,1)S(1)}, u32[]{:S(2)}, u32[]{:S(2)}) collective-permute-start(bf16[32,512]{1,0:T(8,128)(2,1)S(1)} %two_kernel.1.sent), channel_id=1, source_target_pairs={{4,68},{12,76},{20,84},{28,92},{36,100},{44,108},{52,116},{60,124}... | collective-permute-start | bytes 98312 | tf_op jit(solution)/shard_map/planes_two/ppermute | solution.py:312
  16.0 4.3 %collective-permute-start.6 = (bf16[64,512]{1,0:T(8,128)(2,1)S(1)}, bf16[64,512]{1,0:T(8,128)(2,1)S(1)}, u32[]{:S(2)}, u32[]{:S(2)}) collective-permute-start(bf16[64,512]{1,0:T(8,128)(2,1)S(1)} %joint_kernel.1.sent), channel_id=1, source_target_pairs={{4,36},{12,44},{20,52},{28,60},{36,4},{44,12},{52,20},{60,28},{68,... | collective-permute-start | bytes 196616 | tf_op jit(solution)/shard_map/planes_one/ppermute | solution.py:312
  16.5 7.6 %collective-permute-start.2 = (bf16[64,512]{1,0:T(8,128)(2,1)S(1)}, bf16[64,512]{1,0:T(8,128)(2,1)S(1)}, u32[]{:S(2)}, u32[]{:S(2)}) collective-permute-start(bf16[64,512]{1,0:T(8,128)(2,1)S(1)} %near_join_kernel.1), channel_id=1, source_target_pairs={{0,16},{4,20},{8,24},{12,28},{16,0},{20,4},{24,8},{28,12},{32,48},... | collective-permute-start | bytes 196616 | tf_op jit(solution)/shard_map/across_two/ppermute | solution.py:312
  20.2 10.8 %collective-permute-start.10 = (bf16[256,512]{1,0:T(8,128)(2,1)S(1)}, bf16[256,512]{1,0:T(8,128)(2,1)S(1)}, u32[]{:S(2)}, u32[]{:S(2)}) collective-permute-start(bf16[256,512]{1,0:T(8,128)(2,1)S(1)} %get-tuple-element.55), channel_id=1, source_target_pairs={{0,1},{1,0},{2,3},{3,2},{4,5},{5,4},{6,7},{7,6},{8,9},{9,8},{10,11... | collective-permute-start | bytes 786440 | tf_op jit(solution)/shard_map/ppermute | solution.py:393
  21.9 9.7 %collective-permute-start.11 = (bf16[256,512]{1,0:T(8,128)(2,1)S(1)}, bf16[256,512]{1,0:T(8,128)(2,1)S(1)}, u32[]{:S(2)}, u32[]{:S(2)}) collective-permute-start(bf16[256,512]{1,0:T(8,128)(2,1)S(1)} %get-tuple-element.56), channel_id=1, source_target_pairs={{0,3},{3,0},{1,2},{2,1},{4,7},{7,4},{5,6},{6,5},{8,11},{11,8},{9,1... | collective-permute-start | bytes 786440 | tf_op jit(solution)/shard_map/ppermute | solution.py:394
  24.1 2.2 %collective-permute-start.3 = (bf16[128,512]{1,0:T(8,128)(2,1)S(1)}, bf16[128,512]{1,0:T(8,128)(2,1)S(1)}, u32[]{:S(2)}, u32[]{:S(2)}) collective-permute-start(bf16[128,512]{1,0:T(8,128)(2,1)S(1)} %plane_join_kernel.1), channel_id=1, source_target_pairs={{0,4},{4,0},{8,12},{12,8},{16,20},{20,16},{24,28},{28,24},{32,36},... | collective-permute-start | bytes 393224 | tf_op jit(solution)/shard_map/swap_near/ppermute | solution.py:312
  24.2 5.0 %collective-permute-start.7 = (bf16[96,512]{1,0:T(8,128)(2,1)S(1)}, bf16[96,512]{1,0:T(8,128)(2,1)S(1)}, u32[]{:S(2)}, u32[]{:S(2)}) collective-permute-start(bf16[96,512]{1,0:T(8,128)(2,1)S(1)} %far_join_kernel.1.a), channel_id=1, source_target_pairs={{4,12},{12,20},{20,28},{28,4},{36,44},{44,52},{52,60},{60,36},{68,... | collective-permute-start | bytes 294920 | tf_op jit(solution)/shard_map/along/ppermute | solution.py:312
  25.3 4.6 %collective-permute-start.8 = (bf16[96,512]{1,0:T(8,128)(2,1)S(1)}, bf16[96,512]{1,0:T(8,128)(2,1)S(1)}, u32[]{:S(2)}, u32[]{:S(2)}) collective-permute-start(bf16[96,512]{1,0:T(8,128)(2,1)S(1)} %far_join_kernel.1.a), channel_id=1, source_target_pairs={{4,28},{12,4},{20,12},{28,20},{36,60},{44,36},{52,44},{60,52},{68,... | collective-permute-start | bytes 294920 | tf_op jit(solution)/shard_map/along/ppermute | solution.py:312
  26.3 4.7 %collective-permute-start.9 = (bf16[96,512]{1,0:T(8,128)(2,1)S(1)}, bf16[96,512]{1,0:T(8,128)(2,1)S(1)}, u32[]{:S(2)}, u32[]{:S(2)}) collective-permute-start(bf16[96,512]{1,0:T(8,128)(2,1)S(1)} %far_join_kernel.1.a), channel_id=1, source_target_pairs={{4,20},{12,28},{20,4},{28,12},{36,52},{44,60},{52,36},{60,44},{68,... | collective-permute-start | bytes 294920 | tf_op jit(solution)/shard_map/along/ppermute | solution.py:312
  31.7 2.1 %collective-permute-start.12 = (bf16[384,512]{1,0:T(8,128)(2,1)S(1)}, bf16[384,512]{1,0:T(8,128)(2,1)S(1)}, u32[]{:S(2)}, u32[]{:S(2)}) collective-permute-start(bf16[384,512]{1,0:T(8,128)(2,1)S(1)} %row_join_kernel.1.mine), channel_id=1, source_target_pairs={{0,4},{4,0},{8,12},{12,8},{16,20},{20,16},{24,28},{28,24},{32,36},... | collective-permute-start | bytes 1179656 | tf_op jit(solution)/shard_map/swap_far/ppermute | solution.py:312
  34.9 5.9 %collective-permute-start.13 = (bf16[256,256]{1,0:T(8,128)(2,1)S(1)}, bf16[256,256]{1,0:T(8,128)(2,1)S(1)}, u32[]{:S(2)}, u32[]{:S(2)}) collective-permute-start(bf16[256,256]{1,0:T(8,128)(2,1)S(1)} %far_kernel.2.mine_att.after), channel_id=1, source_target_pairs={{0,1},{1,0},{2,3},{3,2},{4,5},{5,4},{6,7},{7,6},{8,9},{9,8},{10,11... | collective-permute-start | bytes 393224 | tf_op jit(solution)/shard_map/ppermute | solution.py:419
  35.7 5.1 %copy-start.1 = (bf16[256,1024]{1,0:T(8,128)(2,1)S(1)}, bf16[256,1024]{1,0:T(8,128)(2,1)}, u32[]{:S(2)}) copy-start(bf16[256,1024]{1,0:T(8,128)(2,1)} %mine_w.3) | copy-start | bytes 1572868
  36.7 6.8 %collective-permute-start.15 = (bf16[256,256]{1,0:T(8,128)(2,1)S(1)}, bf16[256,256]{1,0:T(8,128)(2,1)S(1)}, u32[]{:S(2)}, u32[]{:S(2)}) collective-permute-start(bf16[256,256]{1,0:T(8,128)(2,1)S(1)} %far_kernel.3.mine_att), channel_id=1, source_target_pairs={{0,3},{3,0},{1,2},{2,1},{4,7},{7,4},{5,6},{6,5},{8,11},{11,8},{9,1... | collective-permute-start | bytes 393224 | tf_op jit(solution)/shard_map/ppermute | solution.py:419
  41.0 6.3 %collective-permute-start.14 = (bf16[256,256]{1,0:T(8,128)(2,1)S(1)}, bf16[256,256]{1,0:T(8,128)(2,1)S(1)}, u32[]{:S(2)}, u32[]{:S(2)}) collective-permute-start(bf16[256,256]{1,0:T(8,128)(2,1)S(1)} %get-tuple-element.58), channel_id=1, source_target_pairs={{0,3},{3,0},{1,2},{2,1},{4,7},{7,4},{5,6},{6,5},{8,11},{11,8},{9,1... | collective-permute-start | bytes 393224 | tf_op jit(solution)/shard_map/ppermute | solution.py:426
  43.8 5.1 %collective-permute-start.16 = (bf16[256,256]{1,0:T(8,128)(2,1)S(1)}, bf16[256,256]{1,0:T(8,128)(2,1)S(1)}, u32[]{:S(2)}, u32[]{:S(2)}) collective-permute-start(bf16[256,256]{1,0:T(8,128)(2,1)S(1)} %get-tuple-element.62), channel_id=1, source_target_pairs={{0,1},{1,0},{2,3},{3,2},{4,5},{5,4},{6,7},{7,6},{8,9},{9,8},{10,11... | collective-permute-start | bytes 393224 | tf_op jit(solution)/shard_map/ppermute | solution.py:426

commit v4 on v3

--- a/solution.py
+++ b/solution.py
@@ -98,7 +98,7 @@
     out[48:64, :] = jnp.concatenate([mine, peer], axis=0).astype(BF16)
 
 
-def far_join_kernel(sent, got, out):
+def far_join_kernel(sent, got, w_next, w_far, out):
     out[0:32, :] = got[0:32, :]
     for level in (1, 2):
         to, at = level * 32, 16 + level * 16
@@ -116,8 +116,7 @@
     out[64:128, :] = second[...]
 
 
-def row_join_kernel(a, b, c, d, *refs):
-    out = refs[-1]
+def row_join_kernel(a, b, c, d, after, out):
     for level in range(3):
         for step, piece in enumerate((a, b, c, d)):
             to = level * 128 + step * 32
@@ -359,9 +358,11 @@
             pltpu.VMEM((1024, WIDTH), BF16),
             pltpu.SemaphoreType.DMA((8,)),
         ],
-        compiler_params=pltpu.CompilerParams(vmem_limit_bytes=52 * 1024 * 1024),
+        compiler_params=pltpu.CompilerParams(vmem_limit_bytes=105 * 512 * 1024),
         cost_estimate=pl.CostEstimate(flops=COST, bytes_accessed=1000, transcendentals=0),
     )(tokens, wk, wv, wo)
+    w_next = lax.ppermute(to_next, "head", PAIR_NEXT)
+    w_far = lax.ppermute(to_far, "head", PAIR_FAR)
     share_other = swap(share, "swap_share")
     first = across(e1, 1, "across_one")
     state = [((WIDTH, 256), F32), ((8, 512), F32)]
@@ -386,12 +387,9 @@
         joint_kernel, (share, share_other, pay, got, own[0][1]), [rows(64)], COST, unread=1
     )
     got = hub(pay, lambda z, x: (z ^ 1, x), idle_x, "planes_one")
-    (far,) = call(far_join_kernel, (pay, got), [rows(96)], COST)
+    (far,) = call(far_join_kernel, (pay, got, w_next, w_far), [rows(96)], COST, unread=2)
     (near,) = call(plane_join_kernel, (first, second), [rows(128)], COST)
     other = swap(near, "swap_near")
-    far, to_far, to_next = lax.optimization_barrier((far, to_far, to_next))
-    w_next = lax.ppermute(to_next, "head", PAIR_NEXT)
-    w_far = lax.ppermute(to_far, "head", PAIR_FAR)
     acc0, ml0, acc1, ml1 = call(
         plane_kernel,
         (gate, qt, *own[0], *own[1], share_other, first, second, other),
@@ -399,7 +397,7 @@
         COST,
     )
     others = [hub(far, lambda z, x, shift=shift: (z, x + shift), idle_z, "along") for shift in (1, -1, 2)]
-    (far,) = call(row_join_kernel, (far, *others, ml0, w_next, w_far), [rows(384)], COST, unread=3)
+    (far,) = call(row_join_kernel, (far, *others, ml0), [rows(384)], COST, unread=1)
     far_other = swap(far, "swap_far")
     held = ((acc0, ml0), (acc1, ml1))
     halves = []

time: 49.8 us -> 48.4 us (0.972)
  local copies, waits for them, and re-layouts: 1.15 us -> 0.02 us
  starting transfers between devices: 18.8 us -> 17.9 us
  waiting for transfers between devices: 18.7 us -> 19.4 us
    ppermute x2, waiting for transfers between devices: 2.9 us -> 4.42 us  [shards(): peer = lax.ppermute(halves[half], 'head', pairs[half])]
    unnamed x10 -> x8, local copies, waits for them, and re-layouts: 1.15 us -> 0.02 us
    ppermute x2, starting transfers between devices: 2.59 us -> 1.69 us  [shards(): peer = lax.ppermute(halves[half], 'head', pairs[half])]
    ppermute x1, waiting for transfers between devices: 0.65 us -> 0.01 us  [shards(): w_far = lax.ppermute(to_far, 'head', PAIR_FAR)]
    ppermute x2, starting transfers between devices: 1.98 us -> 1.36 us  [shards(): out.append(keep + lax.ppermute(send, 'head', pairs[1 - half]).astype(F32))]
    ppermute x11, starting transfers between devices: 10.4 us -> 11 us  [move(): return lax.ppermute(array, 'seq', pairs)]
  transfers between devices with their start and end apart: 17 -> 17, of which waited for: 12 -> 11; matrix products, arithmetic and copies ran while one was open for 0% -> 0% of each run, Pallas kernels for 12% -> 12%
where the time goes in v4:
time: 48.4 us; the launch traced here: 48.3 us
  waiting for transfers between devices  19.4 us (40%)
  starting transfers between devices  17.9 us (37%)
  Pallas kernels  10.2 us (21%)
  other arithmetic  0.77 us (2%)
    ppermute x11, starting transfers between devices, move(): return lax.ppermute(array, 'seq', pairs)  11 us
    ppermute x11, waiting for transfers between devices, move(): return lax.ppermute(array, 'seq', pairs)  10.1 us
    pallas_call x15, Pallas kernels, call(): pl.pallas_call(kernel, name=getattr(kernel, 'func', kernel).__name__, out...  6.97 us
    ppermute x2, waiting for transfers between devices, shards(): out.append(keep + lax.ppermute(send, 'head', pairs[1 - half]).astype(F32))  4.8 us
    ppermute x2, waiting for transfers between devices, shards(): peer = lax.ppermute(halves[half], 'head', pairs[half])  4.42 us
    pallas_call x1, Pallas kernels, shards(): pl.pallas_call(load_kernel, name='load_kernel', out_shape=[jax.ShapeDtype...  3.21 us
    ppermute x1, starting transfers between devices, shards(): w_far = lax.ppermute(to_far, 'head', PAIR_FAR)  2.18 us
    ppermute x2, starting transfers between devices, shards(): peer = lax.ppermute(halves[half], 'head', pairs[half])  1.69 us
  transfers between devices with their start and end apart: 17, of which 11 were waited for; matrix products, arithmetic and copies ran while one was open for 0% of the time, Pallas kernels for 12%

profile of v4, /device:TPU:32, one launch (start us, length us, event | category | flops | bytes accessed | tf_op | source)
XLA Modules:
  0.0 48.3 jit_solution(191832113892750810)
XLA Ops:
  0.0 3.2 %load_kernel.1 = (bf16[512,512]{1,0:T(8,128)(2,1)S(1)}, bf16[128,512]{1,0:T(8,128)(2,1)S(1)}, bf16[96,512]{1,0:T(8,128)(2,1)S(1)}, bf16[176,512]{1,0:T(8,128)(2,...) custom-call(bf16[512,1024]{1,0:T(8,128)(2,1)} %tok.3, bf16[1024,256]{1,0:T(8,128)(2,1)} %wk_hbm.1, ...), custom_call_target="tpu_custom_call" | custom-call | flops 1000000 | bytes 1000 | tf_op jit(solution)/shard_map/load_kernel/pallas_call | solution.py:345
  3.3 1.7 %collective-permute-start.7 = (bf16[256,512]{1,0:T(8,128)(2,1)S(1)}, bf16[256,512]{1,0:T(8,128)(2,1)S(1)}, u32[]{:S(2)}, u32[]{:S(2)}) collective-permute-start(bf16[256,512]{1,0:T(8,128)(2,1)S(1)} %get-tuple-element.49), channel_id=1, source_target_pairs={{0,1},{1,0},{2,3},{3,2},{4,5},{5,4},{6,7},{7,6},{8,9},{9,8},{10,11... | collective-permute-start | bytes 786440 | tf_op jit(solution)/shard_map/ppermute | solution.py:364
  5.0 2.2 %collective-permute-start.8 = (bf16[256,512]{1,0:T(8,128)(2,1)S(1)}, bf16[256,512]{1,0:T(8,128)(2,1)S(1)}, u32[]{:S(2)}, u32[]{:S(2)}) collective-permute-start(bf16[256,512]{1,0:T(8,128)(2,1)S(1)} %get-tuple-element.50), channel_id=1, source_target_pairs={{0,3},{3,0},{1,2},{2,1},{4,7},{7,4},{5,6},{6,5},{8,11},{11,8},{9,1... | collective-permute-start | bytes 786440 | tf_op jit(solution)/shard_map/ppermute | solution.py:365
  7.2 1.5 %collective-permute-start.1 = (bf16[96,512]{1,0:T(8,128)(2,1)S(1)}, bf16[96,512]{1,0:T(8,128)(2,1)S(1)}, u32[]{:S(2)}, u32[]{:S(2)}) collective-permute-start(bf16[96,512]{1,0:T(8,128)(2,1)S(1)} %get-tuple-element.43.sent), channel_id=1, source_target_pairs={{0,8},{4,12},{8,0},{12,4},{16,24},{20,28},{24,16},{28,20},{32,40},... | collective-permute-start | bytes 294920 | tf_op jit(solution)/shard_map/across_one/ppermute | solution.py:311
  8.8 2.2 %early_kernel.1 = (bf16[256,512]{1,0:T(8,128)(2,1)S(1)}, f32[256,256]{1,0:T(8,128)S(1)}, f32[8,512]{1,0:T(8,128)S(1)}, f32[256,256]{1,0:T(8,128)S(1)}, f32[8,512]{1,0:T(8,128)S(1)}) custom-call(f32[32,128]{1,0:T(8,128)S(1)} %bias_kernel.1.gate, bf16[512,1024]{1,0:T(8,128)(2,1)S(1)} %copy-done, bf16[1024,256]{1,0:T(8,128)(2,1)S(1)} %copy-done.2, ...), custom_call_target="tpu_custom_call" | custom-call | flops 1000000 | bytes 1000 | tf_op jit(solution)/shard_map/early_kernel/pallas_call | solution.py:298
  11.8 3.1 %collective-permute-start.2 = (bf16[64,512]{1,0:T(8,128)(2,1)S(1)}, bf16[64,512]{1,0:T(8,128)(2,1)S(1)}, u32[]{:S(2)}, u32[]{:S(2)}) collective-permute-start(bf16[64,512]{1,0:T(8,128)(2,1)S(1)} %near_join_kernel.1), channel_id=1, source_target_pairs={{0,16},{4,20},{8,24},{12,28},{16,0},{20,4},{24,8},{28,12},{32,48},... | collective-permute-start | bytes 196616 | tf_op jit(solution)/shard_map/across_two/ppermute | solution.py:311
  15.5 3.4 %collective-permute-done.5.got = bf16[32,512]{1,0:T(8,128)(2,1)S(1)} collective-permute-done((bf16[32,512]{1,0:T(8,128)(2,1)S(1)}, bf16[32,512]{1,0:T(8,128)(2,1)S(1)}, u32[]{:S(2)}, u32[]{:S(2)}) %collective-permute-start.5) | collective-permute-done | bytes 32800 | tf_op jit(solution)/shard_map/planes_two/ppermute | solution.py:311
  19.5 1.0 %collective-permute-start.3 = (bf16[128,512]{1,0:T(8,128)(2,1)S(1)}, bf16[128,512]{1,0:T(8,128)(2,1)S(1)}, u32[]{:S(2)}, u32[]{:S(2)}) collective-permute-start(bf16[128,512]{1,0:T(8,128)(2,1)S(1)} %plane_join_kernel.1), channel_id=1, source_target_pairs={{0,4},{4,0},{8,12},{12,8},{16,20},{20,16},{24,28},{28,24},{32,36},... | collective-permute-start | bytes 393224 | tf_op jit(solution)/shard_map/swap_near/ppermute | solution.py:311
  20.5 2.6 %collective-permute-done.6.got = bf16[64,512]{1,0:T(8,128)(2,1)S(1)} collective-permute-done((bf16[64,512]{1,0:T(8,128)(2,1)S(1)}, bf16[64,512]{1,0:T(8,128)(2,1)S(1)}, u32[]{:S(2)}, u32[]{:S(2)}) %collective-permute-start.6) | collective-permute-done | bytes 65568 | tf_op jit(solution)/shard_map/planes_one/ppermute | solution.py:311
  23.3 1.9 %collective-permute-start.11 = (bf16[96,512]{1,0:T(8,128)(2,1)S(1)}, bf16[96,512]{1,0:T(8,128)(2,1)S(1)}, u32[]{:S(2)}, u32[]{:S(2)}) collective-permute-start(bf16[96,512]{1,0:T(8,128)(2,1)S(1)} %far_join_kernel.1.a), channel_id=1, source_target_pairs={{4,20},{12,28},{20,4},{28,12},{36,52},{44,60},{52,36},{60,44},{68,... | collective-permute-start | bytes 294920 | tf_op jit(solution)/shard_map/along/ppermute | solution.py:311
  25.4 1.9 %plane_kernel.1 = (f32[256,256]{1,0:T(8,128)S(1)}, f32[8,512]{1,0:T(8,128)S(1)}, f32[256,256]{1,0:T(8,128)S(1)}, f32[8,512]{1,0:T(8,128)S(1)}) custom-call(f32[32,128]{1,0:T(8,128)S(1)} %bias_kernel.1.gate, bf16[256,512]{1,0:T(8,128)(2,1)S(1)} %get-tuple-element.39.qt, f32[256,256]{1,0:T(8,128)S(1)} %get-tuple-element.40.acc0, ...), custom_call_target="tpu_custom_call" | custom-call | flops 1000000 | bytes 1000 | tf_op jit(solution)/shard_map/plane_kernel/pallas_call | solution.py:298
  27.8 1.1 %collective-permute-done.11.d = bf16[96,512]{1,0:T(8,128)(2,1)S(1)} collective-permute-done((bf16[96,512]{1,0:T(8,128)(2,1)S(1)}, bf16[96,512]{1,0:T(8,128)(2,1)S(1)}, u32[]{:S(2)}, u32[]{:S(2)}) %collective-permute-start.11) | collective-permute-done | bytes 98336 | tf_op jit(solution)/shard_map/along/ppermute | solution.py:311
  28.9 1.1 %collective-permute-done.9.b = bf16[96,512]{1,0:T(8,128)(2,1)S(1)} collective-permute-done((bf16[96,512]{1,0:T(8,128)(2,1)S(1)}, bf16[96,512]{1,0:T(8,128)(2,1)S(1)}, u32[]{:S(2)}, u32[]{:S(2)}) %collective-permute-start.9) | collective-permute-done | bytes 98336 | tf_op jit(solution)/shard_map/along/ppermute | solution.py:311
  30.0 1.2 %collective-permute-start.12 = (bf16[384,512]{1,0:T(8,128)(2,1)S(1)}, bf16[384,512]{1,0:T(8,128)(2,1)S(1)}, u32[]{:S(2)}, u32[]{:S(2)}) collective-permute-start(bf16[384,512]{1,0:T(8,128)(2,1)S(1)} %row_join_kernel.1.mine), channel_id=1, source_target_pairs={{0,4},{4,0},{8,12},{12,8},{16,20},{20,16},{24,28},{28,24},{32,36},... | collective-permute-start | bytes 1179656 | tf_op jit(solution)/shard_map/swap_far/ppermute | solution.py:311
  31.2 1.3 %collective-permute-done.12.other.after = bf16[384,512]{1,0:T(8,128)(2,1)S(1)} collective-permute-done((bf16[384,512]{1,0:T(8,128)(2,1)S(1)}, bf16[384,512]{1,0:T(8,128)(2,1)S(1)}, u32[]{:S(2)}, u32[]{:S(2)}) %collective-permute-start.12) | collective-permute-done | bytes 393248 | tf_op jit(solution)/shard_map/swap_far/ppermute | solution.py:311
  32.6 1.0 %far_kernel.2.mine_att.after = bf16[256,256]{1,0:T(8,128)(2,1)S(1)} custom-call(f32[32,128]{1,0:T(8,128)S(1)} %bias_kernel.1.gate, bf16[256,512]{1,0:T(8,128)(2,1)S(1)} %get-tuple-element.39.qt, f32[256,256]{1,0:T(8,128)S(1)} %get-tuple-element.47.acc, f32[8,512]{1,0:T(8,128)S(1)} %get-tuple-element.48.after.ml, bf16[384,512]{1,0:T(8,128)(2,1)S(1)} %row_join_kernel.1.mine, ...), custom_call_target="tpu_custom_call" | custom-call | flops 1000000 | bytes 1000 | tf_op jit(solution)/shard_map/far_kernel/pallas_call | solution.py:298
  33.6 0.8 %collective-permute-start.13 = (bf16[256,256]{1,0:T(8,128)(2,1)S(1)}, bf16[256,256]{1,0:T(8,128)(2,1)S(1)}, u32[]{:S(2)}, u32[]{:S(2)}) collective-permute-start(bf16[256,256]{1,0:T(8,128)(2,1)S(1)} %far_kernel.2.mine_att.after), channel_id=1, source_target_pairs={{0,1},{1,0},{2,3},{3,2},{4,5},{5,4},{6,7},{7,6},{8,9},{9,8},{10,11... | collective-permute-start | bytes 393224 | tf_op jit(solution)/shard_map/ppermute | solution.py:417
  34.4 1.1 %far_kernel.3.mine_att = bf16[256,256]{1,0:T(8,128)(2,1)S(1)} custom-call(f32[32,128]{1,0:T(8,128)S(1)} %bias_kernel.1.gate, bf16[256,512]{1,0:T(8,128)(2,1)S(1)} %get-tuple-element.39.qt, f32[256,256]{1,0:T(8,128)S(1)} %get-tuple-element.53.acc, f32[8,512]{1,0:T(8,128)S(1)} %get-tuple-element.54.ml, bf16[384,512]{1,0:T(8,128)(2,1)S(1)} %row_join_kernel.1.mine, ...), custom_call_target="tpu_custom_call" | custom-call | flops 1000000 | bytes 1000 | tf_op jit(solution)/shard_map/far_kernel/pallas_call | solution.py:298
  35.5 0.9 %collective-permute-start.15 = (bf16[256,256]{1,0:T(8,128)(2,1)S(1)}, bf16[256,256]{1,0:T(8,128)(2,1)S(1)}, u32[]{:S(2)}, u32[]{:S(2)}) collective-permute-start(bf16[256,256]{1,0:T(8,128)(2,1)S(1)} %far_kernel.3.mine_att), channel_id=1, source_target_pairs={{0,3},{3,0},{1,2},{2,1},{4,7},{7,4},{5,6},{6,5},{8,11},{11,8},{9,1... | collective-permute-start | bytes 393224 | tf_op jit(solution)/shard_map/ppermute | solution.py:417
  36.4 3.1 %collective-permute-done.13.peer_att = bf16[256,256]{1,0:T(8,128)(2,1)S(1)} collective-permute-done((bf16[256,256]{1,0:T(8,128)(2,1)S(1)}, bf16[256,256]{1,0:T(8,128)(2,1)S(1)}, u32[]{:S(2)}, u32[]{:S(2)}) %collective-permute-start.13) | collective-permute-done | bytes 131104 | tf_op jit(solution)/shard_map/ppermute | solution.py:417
  39.8 1.1 %collective-permute-start.14 = (bf16[256,256]{1,0:T(8,128)(2,1)S(1)}, bf16[256,256]{1,0:T(8,128)(2,1)S(1)}, u32[]{:S(2)}, u32[]{:S(2)}) collective-permute-start(bf16[256,256]{1,0:T(8,128)(2,1)S(1)} %get-tuple-element.52), channel_id=1, source_target_pairs={{0,3},{3,0},{1,2},{2,1},{4,7},{7,4},{5,6},{6,5},{8,11},{11,8},{9,1... | collective-permute-start | bytes 393224 | tf_op jit(solution)/shard_map/ppermute | solution.py:424
  40.9 1.3 %collective-permute-done.15.peer_att = bf16[256,256]{1,0:T(8,128)(2,1)S(1)} collective-permute-done((bf16[256,256]{1,0:T(8,128)(2,1)S(1)}, bf16[256,256]{1,0:T(8,128)(2,1)S(1)}, u32[]{:S(2)}, u32[]{:S(2)}) %collective-permute-start.15) | collective-permute-done | bytes 131104 | tf_op jit(solution)/shard_map/ppermute | solution.py:417
  42.8 3.3 %collective-permute-done.14 = bf16[256,256]{1,0:T(8,128)(2,1)S(1)} collective-permute-done((bf16[256,256]{1,0:T(8,128)(2,1)S(1)}, bf16[256,256]{1,0:T(8,128)(2,1)S(1)}, u32[]{:S(2)}, u32[]{:S(2)}) %collective-permute-start.14) | collective-permute-done | bytes 131104 | tf_op jit(solution)/shard_map/ppermute | solution.py:424
  46.1 1.5 %collective-permute-done.16 = bf16[256,256]{1,0:T(8,128)(2,1)S(1)} collective-permute-done((bf16[256,256]{1,0:T(8,128)(2,1)S(1)}, bf16[256,256]{1,0:T(8,128)(2,1)S(1)}, u32[]{:S(2)}, u32[]{:S(2)}) %collective-permute-start.16) | collective-permute-done | bytes 131104 | tf_op jit(solution)/shard_map/ppermute | solution.py:424
  (37 shorter events, 4.8 us)
Async XLA Ops:
  0.0 8.8 %copy-start = (bf16[512,1024]{1,0:T(8,128)(2,1)S(1)}, bf16[512,1024]{1,0:T(8,128)(2,1)}, u32[]{:S(2)}) copy-start(bf16[512,1024]{1,0:T(8,128)(2,1)} %tok.3) | copy-start | bytes 3145732
  0.0 8.8 %copy-start.2 = (bf16[1024,256]{1,0:T(8,128)(2,1)S(1)}, bf16[1024,256]{1,0:T(8,128)(2,1)}, u32[]{:S(2)}) copy-start(bf16[1024,256]{1,0:T(8,128)(2,1)} %wq.3) | copy-start | bytes 1572868
  3.2 7.8 %collective-permute-start = (bf16[176,512]{1,0:T(8,128)(2,1)S(1)}, bf16[176,512]{1,0:T(8,128)(2,1)S(1)}, u32[]{:S(2)}, u32[]{:S(2)}) collective-permute-start(bf16[176,512]{1,0:T(8,128)(2,1)S(1)} %get-tuple-element.38.share), channel_id=1, source_target_pairs={{0,4},{4,0},{8,12},{12,8},{16,20},{20,16},{24,28},{28,24},{32,36},... | collective-permute-start | bytes 540680 | tf_op jit(solution)/shard_map/swap_share/ppermute | solution.py:311
  3.3 5.4 %copy-start.3 = (s32[4,16]{1,0:T(4,128)S(1)}, s32[4,16]{1,0:T(4,128)}, u32[]{:S(2)}) copy-start(s32[4,16]{1,0:T(4,128)} %gate.1) | copy-start | bytes 772
  3.3 17.2 %collective-permute-start.7 = (bf16[256,512]{1,0:T(8,128)(2,1)S(1)}, bf16[256,512]{1,0:T(8,128)(2,1)S(1)}, u32[]{:S(2)}, u32[]{:S(2)}) collective-permute-start(bf16[256,512]{1,0:T(8,128)(2,1)S(1)} %get-tuple-element.49), channel_id=1, source_target_pairs={{0,1},{1,0},{2,3},{3,2},{4,5},{5,4},{6,7},{7,6},{8,9},{9,8},{10,11... | collective-permute-start | bytes 786440 | tf_op jit(solution)/shard_map/ppermute | solution.py:364
  5.0 15.5 %collective-permute-start.8 = (bf16[256,512]{1,0:T(8,128)(2,1)S(1)}, bf16[256,512]{1,0:T(8,128)(2,1)S(1)}, u32[]{:S(2)}, u32[]{:S(2)}) collective-permute-start(bf16[256,512]{1,0:T(8,128)(2,1)S(1)} %get-tuple-element.50), channel_id=1, source_target_pairs={{0,3},{3,0},{1,2},{2,1},{4,7},{7,4},{5,6},{6,5},{8,11},{11,8},{9,1... | collective-permute-start | bytes 786440 | tf_op jit(solution)/shard_map/ppermute | solution.py:365
  7.2 4.6 %collective-permute-start.1 = (bf16[96,512]{1,0:T(8,128)(2,1)S(1)}, bf16[96,512]{1,0:T(8,128)(2,1)S(1)}, u32[]{:S(2)}, u32[]{:S(2)}) collective-permute-start(bf16[96,512]{1,0:T(8,128)(2,1)S(1)} %get-tuple-element.43.sent), channel_id=1, source_target_pairs={{0,8},{4,12},{8,0},{12,4},{16,24},{20,28},{24,16},{28,20},{32,40},... | collective-permute-start | bytes 294920 | tf_op jit(solution)/shard_map/across_one/ppermute | solution.py:311
  11.0 3.8 %collective-permute-start.4 = (bf16[16,512]{1,0:T(8,128)(2,1)S(1)}, bf16[16,512]{1,0:T(8,128)(2,1)S(1)}, u32[]{:S(2)}, u32[]{:S(2)}) collective-permute-start(bf16[16,512]{1,0:T(8,128)(2,1)S(1)} %mirror_kernel.1.refs_5_), channel_id=1, source_target_pairs={{4,228},{12,236},{20,244},{28,252},{36,196},{44,204},{52,212},{60,... | collective-permute-start | bytes 49160 | tf_op jit(solution)/shard_map/planes_mirror/ppermute | solution.py:311
  11.8 7.7 %collective-permute-start.2 = (bf16[64,512]{1,0:T(8,128)(2,1)S(1)}, bf16[64,512]{1,0:T(8,128)(2,1)S(1)}, u32[]{:S(2)}, u32[]{:S(2)}) collective-permute-start(bf16[64,512]{1,0:T(8,128)(2,1)S(1)} %near_join_kernel.1), channel_id=1, source_target_pairs={{0,16},{4,20},{8,24},{12,28},{16,0},{20,4},{24,8},{28,12},{32,48},... | collective-permute-start | bytes 196616 | tf_op jit(solution)/shard_map/across_two/ppermute | solution.py:311
  14.9 4.0 %collective-permute-start.5 = (bf16[32,512]{1,0:T(8,128)(2,1)S(1)}, bf16[32,512]{1,0:T(8,128)(2,1)S(1)}, u32[]{:S(2)}, u32[]{:S(2)}) collective-permute-start(bf16[32,512]{1,0:T(8,128)(2,1)S(1)} %two_kernel.1.sent), channel_id=1, source_target_pairs={{4,68},{12,76},{20,84},{28,92},{36,100},{44,108},{52,116},{60,124}... | collective-permute-start | bytes 98312 | tf_op jit(solution)/shard_map/planes_two/ppermute | solution.py:311
  18.9 4.3 %collective-permute-start.6 = (bf16[64,512]{1,0:T(8,128)(2,1)S(1)}, bf16[64,512]{1,0:T(8,128)(2,1)S(1)}, u32[]{:S(2)}, u32[]{:S(2)}) collective-permute-start(bf16[64,512]{1,0:T(8,128)(2,1)S(1)} %joint_kernel.1.sent), channel_id=1, source_target_pairs={{4,36},{12,44},{20,52},{28,60},{36,4},{44,12},{52,20},{60,28},{68,... | collective-permute-start | bytes 196616 | tf_op jit(solution)/shard_map/planes_one/ppermute | solution.py:311
  19.5 5.9 %collective-permute-start.3 = (bf16[128,512]{1,0:T(8,128)(2,1)S(1)}, bf16[128,512]{1,0:T(8,128)(2,1)S(1)}, u32[]{:S(2)}, u32[]{:S(2)}) collective-permute-start(bf16[128,512]{1,0:T(8,128)(2,1)S(1)} %plane_join_kernel.1), channel_id=1, source_target_pairs={{0,4},{4,0},{8,12},{12,8},{16,20},{20,16},{24,28},{28,24},{32,36},... | collective-permute-start | bytes 393224 | tf_op jit(solution)/shard_map/swap_near/ppermute | solution.py:311
  23.1 4.7 %collective-permute-start.10 = (bf16[96,512]{1,0:T(8,128)(2,1)S(1)}, bf16[96,512]{1,0:T(8,128)(2,1)S(1)}, u32[]{:S(2)}, u32[]{:S(2)}) collective-permute-start(bf16[96,512]{1,0:T(8,128)(2,1)S(1)} %far_join_kernel.1.a), channel_id=1, source_target_pairs={{4,28},{12,4},{20,12},{28,20},{36,60},{44,36},{52,44},{60,52},{68,... | collective-permute-start | bytes 294920 | tf_op jit(solution)/shard_map/along/ppermute | solution.py:311
  23.3 5.5 %collective-permute-start.11 = (bf16[96,512]{1,0:T(8,128)(2,1)S(1)}, bf16[96,512]{1,0:T(8,128)(2,1)S(1)}, u32[]{:S(2)}, u32[]{:S(2)}) collective-permute-start(bf16[96,512]{1,0:T(8,128)(2,1)S(1)} %far_join_kernel.1.a), channel_id=1, source_target_pairs={{4,20},{12,28},{20,4},{28,12},{36,52},{44,60},{52,36},{60,44},{68,... | collective-permute-start | bytes 294920 | tf_op jit(solution)/shard_map/along/ppermute | solution.py:311
  25.2 4.7 %collective-permute-start.9 = (bf16[96,512]{1,0:T(8,128)(2,1)S(1)}, bf16[96,512]{1,0:T(8,128)(2,1)S(1)}, u32[]{:S(2)}, u32[]{:S(2)}) collective-permute-start(bf16[96,512]{1,0:T(8,128)(2,1)S(1)} %far_join_kernel.1.a), channel_id=1, source_target_pairs={{4,12},{12,20},{20,28},{28,4},{36,44},{44,52},{52,60},{60,36},{68,... | collective-permute-start | bytes 294920 | tf_op jit(solution)/shard_map/along/ppermute | solution.py:311
  30.0 2.6 %collective-permute-start.12 = (bf16[384,512]{1,0:T(8,128)(2,1)S(1)}, bf16[384,512]{1,0:T(8,128)(2,1)S(1)}, u32[]{:S(2)}, u32[]{:S(2)}) collective-permute-start(bf16[384,512]{1,0:T(8,128)(2,1)S(1)} %row_join_kernel.1.mine), channel_id=1, source_target_pairs={{0,4},{4,0},{8,12},{12,8},{16,20},{20,16},{24,28},{28,24},{32,36},... | collective-permute-start | bytes 1179656 | tf_op jit(solution)/shard_map/swap_far/ppermute | solution.py:311
  33.6 5.9 %collective-permute-start.13 = (bf16[256,256]{1,0:T(8,128)(2,1)S(1)}, bf16[256,256]{1,0:T(8,128)(2,1)S(1)}, u32[]{:S(2)}, u32[]{:S(2)}) collective-permute-start(bf16[256,256]{1,0:T(8,128)(2,1)S(1)} %far_kernel.2.mine_att.after), channel_id=1, source_target_pairs={{0,1},{1,0},{2,3},{3,2},{4,5},{5,4},{6,7},{7,6},{8,9},{9,8},{10,11... | collective-permute-start | bytes 393224 | tf_op jit(solution)/shard_map/ppermute | solution.py:417
  34.4 5.1 %copy-start.1 = (bf16[256,1024]{1,0:T(8,128)(2,1)S(1)}, bf16[256,1024]{1,0:T(8,128)(2,1)}, u32[]{:S(2)}) copy-start(bf16[256,1024]{1,0:T(8,128)(2,1)} %mine_w.3) | copy-start | bytes 1572868
  35.5 6.8 %collective-permute-start.15 = (bf16[256,256]{1,0:T(8,128)(2,1)S(1)}, bf16[256,256]{1,0:T(8,128)(2,1)S(1)}, u32[]{:S(2)}, u32[]{:S(2)}) collective-permute-start(bf16[256,256]{1,0:T(8,128)(2,1)S(1)} %far_kernel.3.mine_att), channel_id=1, source_target_pairs={{0,3},{3,0},{1,2},{2,1},{4,7},{7,4},{5,6},{6,5},{8,11},{11,8},{9,1... | collective-permute-start | bytes 393224 | tf_op jit(solution)/shard_map/ppermute | solution.py:417
  39.8 6.3 %collective-permute-start.14 = (bf16[256,256]{1,0:T(8,128)(2,1)S(1)}, bf16[256,256]{1,0:T(8,128)(2,1)S(1)}, u32[]{:S(2)}, u32[]{:S(2)}) collective-permute-start(bf16[256,256]{1,0:T(8,128)(2,1)S(1)} %get-tuple-element.52), channel_id=1, source_target_pairs={{0,3},{3,0},{1,2},{2,1},{4,7},{7,4},{5,6},{6,5},{8,11},{11,8},{9,1... | collective-permute-start | bytes 393224 | tf_op jit(solution)/shard_map/ppermute | solution.py:424
  42.5 5.1 %collective-permute-start.16 = (bf16[256,256]{1,0:T(8,128)(2,1)S(1)}, bf16[256,256]{1,0:T(8,128)(2,1)S(1)}, u32[]{:S(2)}, u32[]{:S(2)}) collective-permute-start(bf16[256,256]{1,0:T(8,128)(2,1)S(1)} %get-tuple-element.56), channel_id=1, source_target_pairs={{0,1},{1,0},{2,3},{3,2},{4,5},{5,4},{6,7},{7,6},{8,9},{9,8},{10,11... | collective-permute-start | bytes 393224 | tf_op jit(solution)/shard_map/ppermute | solution.py:424

commit v5 on v4

--- a/solution.py
+++ b/solution.py
@@ -325,6 +325,10 @@
     return z ^ 1, x
 
 
+def idle_z_odd(z, x):
+    return (z + 1 if z % 2 else z - 1) % Z, x
+
+
 def across(array, bit, name):
     return move(array, [(index(z, x, c), index(z, x ^ bit, c)) for z, x, c in CHIPS], name)
 
@@ -370,7 +374,7 @@
     (gate,) = call(bias_kernel, (gate,), [((32, BLOCK), F32)], COST)
     early = call(early_kernel, (gate, tokens, wq, kv, l1), held, COST)
     (pay,) = call(mirror_kernel, (share, share_other, early[2]), [rows(16)], COST, unread=1)
-    far5 = hub(pay, lambda z, x: (7 - z, x), idle_x, "planes_mirror")
+    far5 = hub(pay, lambda z, x: (z ^ 6, x), idle_x, "planes_mirror")
     qt, acc0, ml0, acc1, ml1 = call(
         late_kernel, (gate, tokens, wq, kv, l1, *early, pay), held, COST, unread=1
     )
@@ -396,7 +400,10 @@
         state * 2,
         COST,
     )
-    others = [hub(far, lambda z, x, shift=shift: (z, x + shift), idle_z, "along") for shift in (1, -1, 2)]
+    others = [
+        hub(far, lambda z, x, shift=shift: (z, x + shift), idle, "along")
+        for shift, idle in ((1, idle_z), (-1, idle_z_odd), (2, idle_z))
+    ]
     (far,) = call(row_join_kernel, (far, *others, ml0), [rows(384)], COST, unread=1)
     far_other = swap(far, "swap_far")
     held = ((acc0, ml0), (acc1, ml1))

time: 48.4 us -> 51.3 us (1.060)
  starting transfers between devices: 17.9 us -> 20.9 us
    ppermute x11, starting transfers between devices: 11 us -> 14 us  [move(): return lax.ppermute(array, 'seq', pairs)]
  transfers between devices with their start and end apart: 17 -> 17, of which waited for: 11 -> 10; matrix products, arithmetic and copies ran while one was open for 0% -> 0% of each run, Pallas kernels for 12% -> 12%
where the time goes in v5:
time: 51.3 us; the launch traced here: 51.1 us
  starting transfers between devices  20.9 us (41%)
  waiting for transfers between devices  19.1 us (37%)
  Pallas kernels  10.2 us (20%)
  other arithmetic  0.77 us (2%)
    ppermute x11, starting transfers between devices, move(): return lax.ppermute(array, 'seq', pairs)  14 us
    ppermute x11, waiting for transfers between devices, move(): return lax.ppermute(array, 'seq', pairs)  10.1 us
    pallas_call x15, Pallas kernels, call(): pl.pallas_call(kernel, name=getattr(kernel, 'func', kernel).__name__, out...  6.97 us
    ppermute x2, waiting for transfers between devices, shards(): out.append(keep + lax.ppermute(send, 'head', pairs[1 - half]).astype(F32))  4.81 us
    ppermute x2, waiting for transfers between devices, shards(): peer = lax.ppermute(halves[half], 'head', pairs[half])  4.18 us
    pallas_call x1, Pallas kernels, shards(): pl.pallas_call(load_kernel, name='load_kernel', out_shape=[jax.ShapeDtype...  3.21 us
    ppermute x1, starting transfers between devices, shards(): w_far = lax.ppermute(to_far, 'head', PAIR_FAR)  2.18 us
    ppermute x2, starting transfers between devices, shards(): peer = lax.ppermute(halves[half], 'head', pairs[half])  1.69 us
  transfers between devices with their start and end apart: 17, of which 10 were waited for; matrix products, arithmetic and copies ran while one was open for 0% of the time, Pallas kernels for 12%

profile of v5, /device:TPU:32, one launch (start us, length us, event | category | flops | bytes accessed | tf_op | source)
XLA Modules:
  0.0 51.1 jit_solution(9246633082291820586)
XLA Ops:
  0.0 3.2 %load_kernel.1 = (bf16[512,512]{1,0:T(8,128)(2,1)S(1)}, bf16[128,512]{1,0:T(8,128)(2,1)S(1)}, bf16[96,512]{1,0:T(8,128)(2,1)S(1)}, bf16[176,512]{1,0:T(8,128)(2,...) custom-call(bf16[512,1024]{1,0:T(8,128)(2,1)} %tok.3, bf16[1024,256]{1,0:T(8,128)(2,1)} %wk_hbm.1, ...), custom_call_target="tpu_custom_call" | custom-call | flops 1000000 | bytes 1000 | tf_op jit(solution)/shard_map/load_kernel/pallas_call | solution.py:349
  3.3 1.7 %collective-permute-start.7 = (bf16[256,512]{1,0:T(8,128)(2,1)S(1)}, bf16[256,512]{1,0:T(8,128)(2,1)S(1)}, u32[]{:S(2)}, u32[]{:S(2)}) collective-permute-start(bf16[256,512]{1,0:T(8,128)(2,1)S(1)} %get-tuple-element.49), channel_id=1, source_target_pairs={{0,1},{1,0},{2,3},{3,2},{4,5},{5,4},{6,7},{7,6},{8,9},{9,8},{10,11... | collective-permute-start | bytes 786440 | tf_op jit(solution)/shard_map/ppermute | solution.py:368
  5.0 2.2 %collective-permute-start.8 = (bf16[256,512]{1,0:T(8,128)(2,1)S(1)}, bf16[256,512]{1,0:T(8,128)(2,1)S(1)}, u32[]{:S(2)}, u32[]{:S(2)}) collective-permute-start(bf16[256,512]{1,0:T(8,128)(2,1)S(1)} %get-tuple-element.50), channel_id=1, source_target_pairs={{0,3},{3,0},{1,2},{2,1},{4,7},{7,4},{5,6},{6,5},{8,11},{11,8},{9,1... | collective-permute-start | bytes 786440 | tf_op jit(solution)/shard_map/ppermute | solution.py:369
  7.2 1.5 %collective-permute-start.1 = (bf16[96,512]{1,0:T(8,128)(2,1)S(1)}, bf16[96,512]{1,0:T(8,128)(2,1)S(1)}, u32[]{:S(2)}, u32[]{:S(2)}) collective-permute-start(bf16[96,512]{1,0:T(8,128)(2,1)S(1)} %get-tuple-element.43.sent), channel_id=1, source_target_pairs={{0,8},{4,12},{8,0},{12,4},{16,24},{20,28},{24,16},{28,20},{32,40},... | collective-permute-start | bytes 294920 | tf_op jit(solution)/shard_map/across_one/ppermute | solution.py:311
  8.8 2.2 %early_kernel.1 = (bf16[256,512]{1,0:T(8,128)(2,1)S(1)}, f32[256,256]{1,0:T(8,128)S(1)}, f32[8,512]{1,0:T(8,128)S(1)}, f32[256,256]{1,0:T(8,128)S(1)}, f32[8,512]{1,0:T(8,128)S(1)}) custom-call(f32[32,128]{1,0:T(8,128)S(1)} %bias_kernel.1.gate, bf16[512,1024]{1,0:T(8,128)(2,1)S(1)} %copy-done, bf16[1024,256]{1,0:T(8,128)(2,1)S(1)} %copy-done.2, ...), custom_call_target="tpu_custom_call" | custom-call | flops 1000000 | bytes 1000 | tf_op jit(solution)/shard_map/early_kernel/pallas_call | solution.py:298
  11.8 3.1 %collective-permute-start.2 = (bf16[64,512]{1,0:T(8,128)(2,1)S(1)}, bf16[64,512]{1,0:T(8,128)(2,1)S(1)}, u32[]{:S(2)}, u32[]{:S(2)}) collective-permute-start(bf16[64,512]{1,0:T(8,128)(2,1)S(1)} %near_join_kernel.1), channel_id=1, source_target_pairs={{0,16},{4,20},{8,24},{12,28},{16,0},{20,4},{24,8},{28,12},{32,48},... | collective-permute-start | bytes 196616 | tf_op jit(solution)/shard_map/across_two/ppermute | solution.py:311
  15.5 3.3 %collective-permute-done.5.got = bf16[32,512]{1,0:T(8,128)(2,1)S(1)} collective-permute-done((bf16[32,512]{1,0:T(8,128)(2,1)S(1)}, bf16[32,512]{1,0:T(8,128)(2,1)S(1)}, u32[]{:S(2)}, u32[]{:S(2)}) %collective-permute-start.5) | collective-permute-done | bytes 32800 | tf_op jit(solution)/shard_map/planes_two/ppermute | solution.py:311
  18.8 1.1 %collective-permute-start.6 = (bf16[64,512]{1,0:T(8,128)(2,1)S(1)}, bf16[64,512]{1,0:T(8,128)(2,1)S(1)}, u32[]{:S(2)}, u32[]{:S(2)}) collective-permute-start(bf16[64,512]{1,0:T(8,128)(2,1)S(1)} %joint_kernel.1.sent), channel_id=1, source_target_pairs={{4,36},{12,44},{20,52},{28,60},{36,4},{44,12},{52,20},{60,28},{68,... | collective-permute-start | bytes 196616 | tf_op jit(solution)/shard_map/planes_one/ppermute | solution.py:311
  19.9 0.9 %collective-permute-start.3 = (bf16[128,512]{1,0:T(8,128)(2,1)S(1)}, bf16[128,512]{1,0:T(8,128)(2,1)S(1)}, u32[]{:S(2)}, u32[]{:S(2)}) collective-permute-start(bf16[128,512]{1,0:T(8,128)(2,1)S(1)} %plane_join_kernel.1), channel_id=1, source_target_pairs={{0,4},{4,0},{8,12},{12,8},{16,20},{20,16},{24,28},{28,24},{32,36},... | collective-permute-start | bytes 393224 | tf_op jit(solution)/shard_map/swap_near/ppermute | solution.py:311
  20.8 2.3 %collective-permute-done.6.got = bf16[64,512]{1,0:T(8,128)(2,1)S(1)} collective-permute-done((bf16[64,512]{1,0:T(8,128)(2,1)S(1)}, bf16[64,512]{1,0:T(8,128)(2,1)S(1)}, u32[]{:S(2)}, u32[]{:S(2)}) %collective-permute-start.6) | collective-permute-done | bytes 65568 | tf_op jit(solution)/shard_map/planes_one/ppermute | solution.py:311
  23.1 2.0 %collective-permute-start.10 = (bf16[96,512]{1,0:T(8,128)(2,1)S(1)}, bf16[96,512]{1,0:T(8,128)(2,1)S(1)}, u32[]{:S(2)}, u32[]{:S(2)}) collective-permute-start(bf16[96,512]{1,0:T(8,128)(2,1)S(1)} %far_join_kernel.1.a), channel_id=1, source_target_pairs={{4,28},{12,4},{20,12},{28,20},{36,60},{44,36},{52,44},{60,52},{68,... | collective-permute-start | bytes 294920 | tf_op jit(solution)/shard_map/along/ppermute | solution.py:311
  25.1 4.0 %collective-permute-start.11 = (bf16[96,512]{1,0:T(8,128)(2,1)S(1)}, bf16[96,512]{1,0:T(8,128)(2,1)S(1)}, u32[]{:S(2)}, u32[]{:S(2)}) collective-permute-start(bf16[96,512]{1,0:T(8,128)(2,1)S(1)} %far_join_kernel.1.a), channel_id=1, source_target_pairs={{4,20},{12,28},{20,4},{28,12},{36,52},{44,60},{52,36},{60,44},{68,... | collective-permute-start | bytes 294920 | tf_op jit(solution)/shard_map/along/ppermute | solution.py:311
  29.1 1.8 %plane_kernel.1 = (f32[256,256]{1,0:T(8,128)S(1)}, f32[8,512]{1,0:T(8,128)S(1)}, f32[256,256]{1,0:T(8,128)S(1)}, f32[8,512]{1,0:T(8,128)S(1)}) custom-call(f32[32,128]{1,0:T(8,128)S(1)} %bias_kernel.1.gate, bf16[256,512]{1,0:T(8,128)(2,1)S(1)} %get-tuple-element.39.qt, f32[256,256]{1,0:T(8,128)S(1)} %get-tuple-element.40.acc0, ...), custom_call_target="tpu_custom_call" | custom-call | flops 1000000 | bytes 1000 | tf_op jit(solution)/shard_map/plane_kernel/pallas_call | solution.py:298
  31.7 2.0 %collective-permute-done.9.b = bf16[96,512]{1,0:T(8,128)(2,1)S(1)} collective-permute-done((bf16[96,512]{1,0:T(8,128)(2,1)S(1)}, bf16[96,512]{1,0:T(8,128)(2,1)S(1)}, u32[]{:S(2)}, u32[]{:S(2)}) %collective-permute-start.9) | collective-permute-done | bytes 98336 | tf_op jit(solution)/shard_map/along/ppermute | solution.py:311
  33.8 1.7 %collective-permute-done.12.other.after = bf16[384,512]{1,0:T(8,128)(2,1)S(1)} collective-permute-done((bf16[384,512]{1,0:T(8,128)(2,1)S(1)}, bf16[384,512]{1,0:T(8,128)(2,1)S(1)}, u32[]{:S(2)}, u32[]{:S(2)}) %collective-permute-start.12) | collective-permute-done | bytes 393248 | tf_op jit(solution)/shard_map/swap_far/ppermute | solution.py:311
  35.5 1.1 %far_kernel.2.mine_att.after = bf16[256,256]{1,0:T(8,128)(2,1)S(1)} custom-call(f32[32,128]{1,0:T(8,128)S(1)} %bias_kernel.1.gate, bf16[256,512]{1,0:T(8,128)(2,1)S(1)} %get-tuple-element.39.qt, f32[256,256]{1,0:T(8,128)S(1)} %get-tuple-element.47.acc, f32[8,512]{1,0:T(8,128)S(1)} %get-tuple-element.48.after.ml, bf16[384,512]{1,0:T(8,128)(2,1)S(1)} %row_join_kernel.1.mine, ...), custom_call_target="tpu_custom_call" | custom-call | flops 1000000 | bytes 1000 | tf_op jit(solution)/shard_map/far_kernel/pallas_call | solution.py:298
  36.6 0.8 %collective-permute-start.13 = (bf16[256,256]{1,0:T(8,128)(2,1)S(1)}, bf16[256,256]{1,0:T(8,128)(2,1)S(1)}, u32[]{:S(2)}, u32[]{:S(2)}) collective-permute-start(bf16[256,256]{1,0:T(8,128)(2,1)S(1)} %far_kernel.2.mine_att.after), channel_id=1, source_target_pairs={{0,1},{1,0},{2,3},{3,2},{4,5},{5,4},{6,7},{7,6},{8,9},{9,8},{10,11... | collective-permute-start | bytes 393224 | tf_op jit(solution)/shard_map/ppermute | solution.py:424
  37.4 1.1 %far_kernel.3.mine_att = bf16[256,256]{1,0:T(8,128)(2,1)S(1)} custom-call(f32[32,128]{1,0:T(8,128)S(1)} %bias_kernel.1.gate, bf16[256,512]{1,0:T(8,128)(2,1)S(1)} %get-tuple-element.39.qt, f32[256,256]{1,0:T(8,128)S(1)} %get-tuple-element.53.acc, f32[8,512]{1,0:T(8,128)S(1)} %get-tuple-element.54.ml, bf16[384,512]{1,0:T(8,128)(2,1)S(1)} %row_join_kernel.1.mine, ...), custom_call_target="tpu_custom_call" | custom-call | flops 1000000 | bytes 1000 | tf_op jit(solution)/shard_map/far_kernel/pallas_call | solution.py:298
  38.4 0.9 %collective-permute-start.15 = (bf16[256,256]{1,0:T(8,128)(2,1)S(1)}, bf16[256,256]{1,0:T(8,128)(2,1)S(1)}, u32[]{:S(2)}, u32[]{:S(2)}) collective-permute-start(bf16[256,256]{1,0:T(8,128)(2,1)S(1)} %far_kernel.3.mine_att), channel_id=1, source_target_pairs={{0,3},{3,0},{1,2},{2,1},{4,7},{7,4},{5,6},{6,5},{8,11},{11,8},{9,1... | collective-permute-start | bytes 393224 | tf_op jit(solution)/shard_map/ppermute | solution.py:424
  39.3 2.9 %collective-permute-done.13.peer_att = bf16[256,256]{1,0:T(8,128)(2,1)S(1)} collective-permute-done((bf16[256,256]{1,0:T(8,128)(2,1)S(1)}, bf16[256,256]{1,0:T(8,128)(2,1)S(1)}, u32[]{:S(2)}, u32[]{:S(2)}) %collective-permute-start.13) | collective-permute-done | bytes 131104 | tf_op jit(solution)/shard_map/ppermute | solution.py:424
  42.5 1.1 %collective-permute-start.14 = (bf16[256,256]{1,0:T(8,128)(2,1)S(1)}, bf16[256,256]{1,0:T(8,128)(2,1)S(1)}, u32[]{:S(2)}, u32[]{:S(2)}) collective-permute-start(bf16[256,256]{1,0:T(8,128)(2,1)S(1)} %get-tuple-element.52), channel_id=1, source_target_pairs={{0,3},{3,0},{1,2},{2,1},{4,7},{7,4},{5,6},{6,5},{8,11},{11,8},{9,1... | collective-permute-start | bytes 393224 | tf_op jit(solution)/shard_map/ppermute | solution.py:431
  43.7 1.3 %collective-permute-done.15.peer_att = bf16[256,256]{1,0:T(8,128)(2,1)S(1)} collective-permute-done((bf16[256,256]{1,0:T(8,128)(2,1)S(1)}, bf16[256,256]{1,0:T(8,128)(2,1)S(1)}, u32[]{:S(2)}, u32[]{:S(2)}) %collective-permute-start.15) | collective-permute-done | bytes 131104 | tf_op jit(solution)/shard_map/ppermute | solution.py:424
  45.5 3.3 %collective-permute-done.14 = bf16[256,256]{1,0:T(8,128)(2,1)S(1)} collective-permute-done((bf16[256,256]{1,0:T(8,128)(2,1)S(1)}, bf16[256,256]{1,0:T(8,128)(2,1)S(1)}, u32[]{:S(2)}, u32[]{:S(2)}) %collective-permute-start.14) | collective-permute-done | bytes 131104 | tf_op jit(solution)/shard_map/ppermute | solution.py:431
  48.8 1.5 %collective-permute-done.16 = bf16[256,256]{1,0:T(8,128)(2,1)S(1)} collective-permute-done((bf16[256,256]{1,0:T(8,128)(2,1)S(1)}, bf16[256,256]{1,0:T(8,128)(2,1)S(1)}, u32[]{:S(2)}, u32[]{:S(2)}) %collective-permute-start.16) | collective-permute-done | bytes 131104 | tf_op jit(solution)/shard_map/ppermute | solution.py:431
  (37 shorter events, 4.1 us)
Async XLA Ops:
  0.0 8.8 %copy-start = (bf16[512,1024]{1,0:T(8,128)(2,1)S(1)}, bf16[512,1024]{1,0:T(8,128)(2,1)}, u32[]{:S(2)}) copy-start(bf16[512,1024]{1,0:T(8,128)(2,1)} %tok.3) | copy-start | bytes 3145732
  0.0 8.8 %copy-start.2 = (bf16[1024,256]{1,0:T(8,128)(2,1)S(1)}, bf16[1024,256]{1,0:T(8,128)(2,1)}, u32[]{:S(2)}) copy-start(bf16[1024,256]{1,0:T(8,128)(2,1)} %wq.3) | copy-start | bytes 1572868
  3.2 7.8 %collective-permute-start = (bf16[176,512]{1,0:T(8,128)(2,1)S(1)}, bf16[176,512]{1,0:T(8,128)(2,1)S(1)}, u32[]{:S(2)}, u32[]{:S(2)}) collective-permute-start(bf16[176,512]{1,0:T(8,128)(2,1)S(1)} %get-tuple-element.38.share), channel_id=1, source_target_pairs={{0,4},{4,0},{8,12},{12,8},{16,20},{20,16},{24,28},{28,24},{32,36},... | collective-permute-start | bytes 540680 | tf_op jit(solution)/shard_map/swap_share/ppermute | solution.py:311
  3.3 5.4 %copy-start.3 = (s32[4,16]{1,0:T(4,128)S(1)}, s32[4,16]{1,0:T(4,128)}, u32[]{:S(2)}) copy-start(s32[4,16]{1,0:T(4,128)} %gate.1) | copy-start | bytes 772
  3.3 17.5 %collective-permute-start.7 = (bf16[256,512]{1,0:T(8,128)(2,1)S(1)}, bf16[256,512]{1,0:T(8,128)(2,1)S(1)}, u32[]{:S(2)}, u32[]{:S(2)}) collective-permute-start(bf16[256,512]{1,0:T(8,128)(2,1)S(1)} %get-tuple-element.49), channel_id=1, source_target_pairs={{0,1},{1,0},{2,3},{3,2},{4,5},{5,4},{6,7},{7,6},{8,9},{9,8},{10,11... | collective-permute-start | bytes 786440 | tf_op jit(solution)/shard_map/ppermute | solution.py:368
  5.0 15.8 %collective-permute-start.8 = (bf16[256,512]{1,0:T(8,128)(2,1)S(1)}, bf16[256,512]{1,0:T(8,128)(2,1)S(1)}, u32[]{:S(2)}, u32[]{:S(2)}) collective-permute-start(bf16[256,512]{1,0:T(8,128)(2,1)S(1)} %get-tuple-element.50), channel_id=1, source_target_pairs={{0,3},{3,0},{1,2},{2,1},{4,7},{7,4},{5,6},{6,5},{8,11},{11,8},{9,1... | collective-permute-start | bytes 786440 | tf_op jit(solution)/shard_map/ppermute | solution.py:369
  7.2 4.6 %collective-permute-start.1 = (bf16[96,512]{1,0:T(8,128)(2,1)S(1)}, bf16[96,512]{1,0:T(8,128)(2,1)S(1)}, u32[]{:S(2)}, u32[]{:S(2)}) collective-permute-start(bf16[96,512]{1,0:T(8,128)(2,1)S(1)} %get-tuple-element.43.sent), channel_id=1, source_target_pairs={{0,8},{4,12},{8,0},{12,4},{16,24},{20,28},{24,16},{28,20},{32,40},... | collective-permute-start | bytes 294920 | tf_op jit(solution)/shard_map/across_one/ppermute | solution.py:311
  11.0 3.8 %collective-permute-start.4 = (bf16[16,512]{1,0:T(8,128)(2,1)S(1)}, bf16[16,512]{1,0:T(8,128)(2,1)S(1)}, u32[]{:S(2)}, u32[]{:S(2)}) collective-permute-start(bf16[16,512]{1,0:T(8,128)(2,1)S(1)} %mirror_kernel.1.refs_5_), channel_id=1, source_target_pairs={{4,196},{12,204},{20,212},{28,220},{36,228},{44,236},{52,244},{60,... | collective-permute-start | bytes 49160 | tf_op jit(solution)/shard_map/planes_mirror/ppermute | solution.py:311
  11.8 8.0 %collective-permute-start.2 = (bf16[64,512]{1,0:T(8,128)(2,1)S(1)}, bf16[64,512]{1,0:T(8,128)(2,1)S(1)}, u32[]{:S(2)}, u32[]{:S(2)}) collective-permute-start(bf16[64,512]{1,0:T(8,128)(2,1)S(1)} %near_join_kernel.1), channel_id=1, source_target_pairs={{0,16},{4,20},{8,24},{12,28},{16,0},{20,4},{24,8},{28,12},{32,48},... | collective-permute-start | bytes 196616 | tf_op jit(solution)/shard_map/across_two/ppermute | solution.py:311
  14.9 3.9 %collective-permute-start.5 = (bf16[32,512]{1,0:T(8,128)(2,1)S(1)}, bf16[32,512]{1,0:T(8,128)(2,1)S(1)}, u32[]{:S(2)}, u32[]{:S(2)}) collective-permute-start(bf16[32,512]{1,0:T(8,128)(2,1)S(1)} %two_kernel.1.sent), channel_id=1, source_target_pairs={{4,68},{12,76},{20,84},{28,92},{36,100},{44,108},{52,116},{60,124}... | collective-permute-start | bytes 98312 | tf_op jit(solution)/shard_map/planes_two/ppermute | solution.py:311
  18.8 4.3 %collective-permute-start.6 = (bf16[64,512]{1,0:T(8,128)(2,1)S(1)}, bf16[64,512]{1,0:T(8,128)(2,1)S(1)}, u32[]{:S(2)}, u32[]{:S(2)}) collective-permute-start(bf16[64,512]{1,0:T(8,128)(2,1)S(1)} %joint_kernel.1.sent), channel_id=1, source_target_pairs={{4,36},{12,44},{20,52},{28,60},{36,4},{44,12},{52,20},{60,28},{68,... | collective-permute-start | bytes 196616 | tf_op jit(solution)/shard_map/planes_one/ppermute | solution.py:311
  19.9 9.3 %collective-permute-start.3 = (bf16[128,512]{1,0:T(8,128)(2,1)S(1)}, bf16[128,512]{1,0:T(8,128)(2,1)S(1)}, u32[]{:S(2)}, u32[]{:S(2)}) collective-permute-start(bf16[128,512]{1,0:T(8,128)(2,1)S(1)} %plane_join_kernel.1), channel_id=1, source_target_pairs={{0,4},{4,0},{8,12},{12,8},{16,20},{20,16},{24,28},{28,24},{32,36},... | collective-permute-start | bytes 393224 | tf_op jit(solution)/shard_map/swap_near/ppermute | solution.py:311
  23.1 7.9 %collective-permute-start.10 = (bf16[96,512]{1,0:T(8,128)(2,1)S(1)}, bf16[96,512]{1,0:T(8,128)(2,1)S(1)}, u32[]{:S(2)}, u32[]{:S(2)}) collective-permute-start(bf16[96,512]{1,0:T(8,128)(2,1)S(1)} %far_join_kernel.1.a), channel_id=1, source_target_pairs={{4,28},{12,4},{20,12},{28,20},{36,60},{44,36},{52,44},{60,52},{68,... | collective-permute-start | bytes 294920 | tf_op jit(solution)/shard_map/along/ppermute | solution.py:311
  25.1 6.6 %collective-permute-start.11 = (bf16[96,512]{1,0:T(8,128)(2,1)S(1)}, bf16[96,512]{1,0:T(8,128)(2,1)S(1)}, u32[]{:S(2)}, u32[]{:S(2)}) collective-permute-start(bf16[96,512]{1,0:T(8,128)(2,1)S(1)} %far_join_kernel.1.a), channel_id=1, source_target_pairs={{4,20},{12,28},{20,4},{28,12},{36,52},{44,60},{52,36},{60,44},{68,... | collective-permute-start | bytes 294920 | tf_op jit(solution)/shard_map/along/ppermute | solution.py:311
  29.1 4.6 %collective-permute-start.9 = (bf16[96,512]{1,0:T(8,128)(2,1)S(1)}, bf16[96,512]{1,0:T(8,128)(2,1)S(1)}, u32[]{:S(2)}, u32[]{:S(2)}) collective-permute-start(bf16[96,512]{1,0:T(8,128)(2,1)S(1)} %far_join_kernel.1.a), channel_id=1, source_target_pairs={{4,12},{12,20},{20,28},{28,4},{36,44},{44,52},{52,60},{60,36},{68,... | collective-permute-start | bytes 294920 | tf_op jit(solution)/shard_map/along/ppermute | solution.py:311
  33.7 1.8 %collective-permute-start.12 = (bf16[384,512]{1,0:T(8,128)(2,1)S(1)}, bf16[384,512]{1,0:T(8,128)(2,1)S(1)}, u32[]{:S(2)}, u32[]{:S(2)}) collective-permute-start(bf16[384,512]{1,0:T(8,128)(2,1)S(1)} %row_join_kernel.1.mine), channel_id=1, source_target_pairs={{0,4},{4,0},{8,12},{12,8},{16,20},{20,16},{24,28},{28,24},{32,36},... | collective-permute-start | bytes 1179656 | tf_op jit(solution)/shard_map/swap_far/ppermute | solution.py:311
  36.6 5.6 %collective-permute-start.13 = (bf16[256,256]{1,0:T(8,128)(2,1)S(1)}, bf16[256,256]{1,0:T(8,128)(2,1)S(1)}, u32[]{:S(2)}, u32[]{:S(2)}) collective-permute-start(bf16[256,256]{1,0:T(8,128)(2,1)S(1)} %far_kernel.2.mine_att.after), channel_id=1, source_target_pairs={{0,1},{1,0},{2,3},{3,2},{4,5},{5,4},{6,7},{7,6},{8,9},{9,8},{10,11... | collective-permute-start | bytes 393224 | tf_op jit(solution)/shard_map/ppermute | solution.py:424
  37.4 4.9 %copy-start.1 = (bf16[256,1024]{1,0:T(8,128)(2,1)S(1)}, bf16[256,1024]{1,0:T(8,128)(2,1)}, u32[]{:S(2)}) copy-start(bf16[256,1024]{1,0:T(8,128)(2,1)} %mine_w.3) | copy-start | bytes 1572868
  38.4 6.6 %collective-permute-start.15 = (bf16[256,256]{1,0:T(8,128)(2,1)S(1)}, bf16[256,256]{1,0:T(8,128)(2,1)S(1)}, u32[]{:S(2)}, u32[]{:S(2)}) collective-permute-start(bf16[256,256]{1,0:T(8,128)(2,1)S(1)} %far_kernel.3.mine_att), channel_id=1, source_target_pairs={{0,3},{3,0},{1,2},{2,1},{4,7},{7,4},{5,6},{6,5},{8,11},{11,8},{9,1... | collective-permute-start | bytes 393224 | tf_op jit(solution)/shard_map/ppermute | solution.py:424
  42.5 6.3 %collective-permute-start.14 = (bf16[256,256]{1,0:T(8,128)(2,1)S(1)}, bf16[256,256]{1,0:T(8,128)(2,1)S(1)}, u32[]{:S(2)}, u32[]{:S(2)}) collective-permute-start(bf16[256,256]{1,0:T(8,128)(2,1)S(1)} %get-tuple-element.52), channel_id=1, source_target_pairs={{0,3},{3,0},{1,2},{2,1},{4,7},{7,4},{5,6},{6,5},{8,11},{11,8},{9,1... | collective-permute-start | bytes 393224 | tf_op jit(solution)/shard_map/ppermute | solution.py:431
  45.3 5.1 %collective-permute-start.16 = (bf16[256,256]{1,0:T(8,128)(2,1)S(1)}, bf16[256,256]{1,0:T(8,128)(2,1)S(1)}, u32[]{:S(2)}, u32[]{:S(2)}) collective-permute-start(bf16[256,256]{1,0:T(8,128)(2,1)S(1)} %get-tuple-element.56), channel_id=1, source_target_pairs={{0,1},{1,0},{2,3},{3,2},{4,5},{5,4},{6,7},{7,6},{8,9},{9,8},{10,11... | collective-permute-start | bytes 393224 | tf_op jit(solution)/shard_map/ppermute | solution.py:431

commit v6 on v4

--- a/solution.py
+++ b/solution.py
@@ -370,7 +370,7 @@
     (gate,) = call(bias_kernel, (gate,), [((32, BLOCK), F32)], COST)
     early = call(early_kernel, (gate, tokens, wq, kv, l1), held, COST)
     (pay,) = call(mirror_kernel, (share, share_other, early[2]), [rows(16)], COST, unread=1)
-    far5 = hub(pay, lambda z, x: (7 - z, x), idle_x, "planes_mirror")
+    far5 = hub(pay, lambda z, x: (z ^ 6, x), idle_x, "planes_mirror")
     qt, acc0, ml0, acc1, ml1 = call(
         late_kernel, (gate, tokens, wq, kv, l1, *early, pay), held, COST, unread=1
     )

time: 48.4 us -> 48.4 us (level)
  waiting for transfers between devices: 19.4 us -> 18.8 us
  starting transfers between devices: 17.9 us -> 18.4 us
    ppermute x11, waiting for transfers between devices: 10.1 us -> 9.4 us  [move(): return lax.ppermute(array, 'seq', pairs)]
    ppermute x11, starting transfers between devices: 11 us -> 11.7 us  [move(): return lax.ppermute(array, 'seq', pairs)]
where the time goes in v6:
time: 48.4 us; the launch traced here: 48.3 us
  waiting for transfers between devices  18.8 us (39%)
  starting transfers between devices  18.4 us (38%)
  Pallas kernels  10.2 us (21%)
  other arithmetic  0.77 us (2%)
    ppermute x11, starting transfers between devices, move(): return lax.ppermute(array, 'seq', pairs)  11.7 us
    ppermute x11, waiting for transfers between devices, move(): return lax.ppermute(array, 'seq', pairs)  9.4 us
    pallas_call x15, Pallas kernels, call(): pl.pallas_call(kernel, name=getattr(kernel, 'func', kernel).__name__, out...  6.97 us
    ppermute x2, waiting for transfers between devices, shards(): out.append(keep + lax.ppermute(send, 'head', pairs[1 - half]).astype(F32))  4.81 us
    ppermute x2, waiting for transfers between devices, shards(): peer = lax.ppermute(halves[half], 'head', pairs[half])  4.59 us
    pallas_call x1, Pallas kernels, shards(): pl.pallas_call(load_kernel, name='load_kernel', out_shape=[jax.ShapeDtype...  3.21 us
    ppermute x1, starting transfers between devices, shards(): w_far = lax.ppermute(to_far, 'head', PAIR_FAR)  2.18 us
    ppermute x1, starting transfers between devices, shards(): w_next = lax.ppermute(to_next, 'head', PAIR_NEXT)  1.66 us
  transfers between devices with their start and end apart: 17, of which 11 were waited for; matrix products, arithmetic and copies ran while one was open for 0% of the time, Pallas kernels for 12%

profile of v6, /device:TPU:32, one launch (start us, length us, event | category | flops | bytes accessed | tf_op | source)
XLA Modules:
  0.0 48.3 jit_solution(1438700263504489284)
XLA Ops:
  0.0 3.2 %load_kernel.1 = (bf16[512,512]{1,0:T(8,128)(2,1)S(1)}, bf16[128,512]{1,0:T(8,128)(2,1)S(1)}, bf16[96,512]{1,0:T(8,128)(2,1)S(1)}, bf16[176,512]{1,0:T(8,128)(2,...) custom-call(bf16[512,1024]{1,0:T(8,128)(2,1)} %tok.3, bf16[1024,256]{1,0:T(8,128)(2,1)} %wk_hbm.1, ...), custom_call_target="tpu_custom_call" | custom-call | flops 1000000 | bytes 1000 | tf_op jit(solution)/shard_map/load_kernel/pallas_call | solution.py:345
  3.3 1.7 %collective-permute-start.7 = (bf16[256,512]{1,0:T(8,128)(2,1)S(1)}, bf16[256,512]{1,0:T(8,128)(2,1)S(1)}, u32[]{:S(2)}, u32[]{:S(2)}) collective-permute-start(bf16[256,512]{1,0:T(8,128)(2,1)S(1)} %get-tuple-element.49), channel_id=1, source_target_pairs={{0,1},{1,0},{2,3},{3,2},{4,5},{5,4},{6,7},{7,6},{8,9},{9,8},{10,11... | collective-permute-start | bytes 786440 | tf_op jit(solution)/shard_map/ppermute | solution.py:364
  5.0 2.2 %collective-permute-start.8 = (bf16[256,512]{1,0:T(8,128)(2,1)S(1)}, bf16[256,512]{1,0:T(8,128)(2,1)S(1)}, u32[]{:S(2)}, u32[]{:S(2)}) collective-permute-start(bf16[256,512]{1,0:T(8,128)(2,1)S(1)} %get-tuple-element.50), channel_id=1, source_target_pairs={{0,3},{3,0},{1,2},{2,1},{4,7},{7,4},{5,6},{6,5},{8,11},{11,8},{9,1... | collective-permute-start | bytes 786440 | tf_op jit(solution)/shard_map/ppermute | solution.py:365
  7.2 1.5 %collective-permute-start.1 = (bf16[96,512]{1,0:T(8,128)(2,1)S(1)}, bf16[96,512]{1,0:T(8,128)(2,1)S(1)}, u32[]{:S(2)}, u32[]{:S(2)}) collective-permute-start(bf16[96,512]{1,0:T(8,128)(2,1)S(1)} %get-tuple-element.43.sent), channel_id=1, source_target_pairs={{0,8},{4,12},{8,0},{12,4},{16,24},{20,28},{24,16},{28,20},{32,40},... | collective-permute-start | bytes 294920 | tf_op jit(solution)/shard_map/across_one/ppermute | solution.py:311
  8.8 2.2 %early_kernel.1 = (bf16[256,512]{1,0:T(8,128)(2,1)S(1)}, f32[256,256]{1,0:T(8,128)S(1)}, f32[8,512]{1,0:T(8,128)S(1)}, f32[256,256]{1,0:T(8,128)S(1)}, f32[8,512]{1,0:T(8,128)S(1)}) custom-call(f32[32,128]{1,0:T(8,128)S(1)} %bias_kernel.1.gate, bf16[512,1024]{1,0:T(8,128)(2,1)S(1)} %copy-done, bf16[1024,256]{1,0:T(8,128)(2,1)S(1)} %copy-done.2, ...), custom_call_target="tpu_custom_call" | custom-call | flops 1000000 | bytes 1000 | tf_op jit(solution)/shard_map/early_kernel/pallas_call | solution.py:298
  11.8 3.1 %collective-permute-start.2 = (bf16[64,512]{1,0:T(8,128)(2,1)S(1)}, bf16[64,512]{1,0:T(8,128)(2,1)S(1)}, u32[]{:S(2)}, u32[]{:S(2)}) collective-permute-start(bf16[64,512]{1,0:T(8,128)(2,1)S(1)} %near_join_kernel.1), channel_id=1, source_target_pairs={{0,16},{4,20},{8,24},{12,28},{16,0},{20,4},{24,8},{28,12},{32,48},... | collective-permute-start | bytes 196616 | tf_op jit(solution)/shard_map/across_two/ppermute | solution.py:311
  15.5 3.3 %collective-permute-done.5.got = bf16[32,512]{1,0:T(8,128)(2,1)S(1)} collective-permute-done((bf16[32,512]{1,0:T(8,128)(2,1)S(1)}, bf16[32,512]{1,0:T(8,128)(2,1)S(1)}, u32[]{:S(2)}, u32[]{:S(2)}) %collective-permute-start.5) | collective-permute-done | bytes 32800 | tf_op jit(solution)/shard_map/planes_two/ppermute | solution.py:311
  18.8 1.1 %collective-permute-start.6 = (bf16[64,512]{1,0:T(8,128)(2,1)S(1)}, bf16[64,512]{1,0:T(8,128)(2,1)S(1)}, u32[]{:S(2)}, u32[]{:S(2)}) collective-permute-start(bf16[64,512]{1,0:T(8,128)(2,1)S(1)} %joint_kernel.1.sent), channel_id=1, source_target_pairs={{4,36},{12,44},{20,52},{28,60},{36,4},{44,12},{52,20},{60,28},{68,... | collective-permute-start | bytes 196616 | tf_op jit(solution)/shard_map/planes_one/ppermute | solution.py:311
  19.9 0.9 %collective-permute-start.3 = (bf16[128,512]{1,0:T(8,128)(2,1)S(1)}, bf16[128,512]{1,0:T(8,128)(2,1)S(1)}, u32[]{:S(2)}, u32[]{:S(2)}) collective-permute-start(bf16[128,512]{1,0:T(8,128)(2,1)S(1)} %plane_join_kernel.1), channel_id=1, source_target_pairs={{0,4},{4,0},{8,12},{12,8},{16,20},{20,16},{24,28},{28,24},{32,36},... | collective-permute-start | bytes 393224 | tf_op jit(solution)/shard_map/swap_near/ppermute | solution.py:311
  20.8 2.3 %collective-permute-done.6.got = bf16[64,512]{1,0:T(8,128)(2,1)S(1)} collective-permute-done((bf16[64,512]{1,0:T(8,128)(2,1)S(1)}, bf16[64,512]{1,0:T(8,128)(2,1)S(1)}, u32[]{:S(2)}, u32[]{:S(2)}) %collective-permute-start.6) | collective-permute-done | bytes 65568 | tf_op jit(solution)/shard_map/planes_one/ppermute | solution.py:311
  23.6 1.6 %collective-permute-start.11 = (bf16[96,512]{1,0:T(8,128)(2,1)S(1)}, bf16[96,512]{1,0:T(8,128)(2,1)S(1)}, u32[]{:S(2)}, u32[]{:S(2)}) collective-permute-start(bf16[96,512]{1,0:T(8,128)(2,1)S(1)} %far_join_kernel.1.a), channel_id=1, source_target_pairs={{4,20},{12,28},{20,4},{28,12},{36,52},{44,60},{52,36},{60,44},{68,... | collective-permute-start | bytes 294920 | tf_op jit(solution)/shard_map/along/ppermute | solution.py:311
  25.6 1.9 %plane_kernel.1 = (f32[256,256]{1,0:T(8,128)S(1)}, f32[8,512]{1,0:T(8,128)S(1)}, f32[256,256]{1,0:T(8,128)S(1)}, f32[8,512]{1,0:T(8,128)S(1)}) custom-call(f32[32,128]{1,0:T(8,128)S(1)} %bias_kernel.1.gate, bf16[256,512]{1,0:T(8,128)(2,1)S(1)} %get-tuple-element.39.qt, f32[256,256]{1,0:T(8,128)S(1)} %get-tuple-element.40.acc0, ...), custom_call_target="tpu_custom_call" | custom-call | flops 1000000 | bytes 1000 | tf_op jit(solution)/shard_map/plane_kernel/pallas_call | solution.py:298
  27.8 1.1 %collective-permute-done.11.d = bf16[96,512]{1,0:T(8,128)(2,1)S(1)} collective-permute-done((bf16[96,512]{1,0:T(8,128)(2,1)S(1)}, bf16[96,512]{1,0:T(8,128)(2,1)S(1)}, u32[]{:S(2)}, u32[]{:S(2)}) %collective-permute-start.11) | collective-permute-done | bytes 98336 | tf_op jit(solution)/shard_map/along/ppermute | solution.py:311
  28.8 1.1 %collective-permute-done.9.b = bf16[96,512]{1,0:T(8,128)(2,1)S(1)} collective-permute-done((bf16[96,512]{1,0:T(8,128)(2,1)S(1)}, bf16[96,512]{1,0:T(8,128)(2,1)S(1)}, u32[]{:S(2)}, u32[]{:S(2)}) %collective-permute-start.9) | collective-permute-done | bytes 98336 | tf_op jit(solution)/shard_map/along/ppermute | solution.py:311
  29.9 1.3 %collective-permute-start.12 = (bf16[384,512]{1,0:T(8,128)(2,1)S(1)}, bf16[384,512]{1,0:T(8,128)(2,1)S(1)}, u32[]{:S(2)}, u32[]{:S(2)}) collective-permute-start(bf16[384,512]{1,0:T(8,128)(2,1)S(1)} %row_join_kernel.1.mine), channel_id=1, source_target_pairs={{0,4},{4,0},{8,12},{12,8},{16,20},{20,16},{24,28},{28,24},{32,36},... | collective-permute-start | bytes 1179656 | tf_op jit(solution)/shard_map/swap_far/ppermute | solution.py:311
  31.2 1.3 %collective-permute-done.12.other.after = bf16[384,512]{1,0:T(8,128)(2,1)S(1)} collective-permute-done((bf16[384,512]{1,0:T(8,128)(2,1)S(1)}, bf16[384,512]{1,0:T(8,128)(2,1)S(1)}, u32[]{:S(2)}, u32[]{:S(2)}) %collective-permute-start.12) | collective-permute-done | bytes 393248 | tf_op jit(solution)/shard_map/swap_far/ppermute | solution.py:311
  32.5 1.0 %far_kernel.2.mine_att.after = bf16[256,256]{1,0:T(8,128)(2,1)S(1)} custom-call(f32[32,128]{1,0:T(8,128)S(1)} %bias_kernel.1.gate, bf16[256,512]{1,0:T(8,128)(2,1)S(1)} %get-tuple-element.39.qt, f32[256,256]{1,0:T(8,128)S(1)} %get-tuple-element.47.acc, f32[8,512]{1,0:T(8,128)S(1)} %get-tuple-element.48.after.ml, bf16[384,512]{1,0:T(8,128)(2,1)S(1)} %row_join_kernel.1.mine, ...), custom_call_target="tpu_custom_call" | custom-call | flops 1000000 | bytes 1000 | tf_op jit(solution)/shard_map/far_kernel/pallas_call | solution.py:298
  33.6 0.8 %collective-permute-start.13 = (bf16[256,256]{1,0:T(8,128)(2,1)S(1)}, bf16[256,256]{1,0:T(8,128)(2,1)S(1)}, u32[]{:S(2)}, u32[]{:S(2)}) collective-permute-start(bf16[256,256]{1,0:T(8,128)(2,1)S(1)} %far_kernel.2.mine_att.after), channel_id=1, source_target_pairs={{0,1},{1,0},{2,3},{3,2},{4,5},{5,4},{6,7},{7,6},{8,9},{9,8},{10,11... | collective-permute-start | bytes 393224 | tf_op jit(solution)/shard_map/ppermute | solution.py:417
  34.4 1.0 %far_kernel.3.mine_att = bf16[256,256]{1,0:T(8,128)(2,1)S(1)} custom-call(f32[32,128]{1,0:T(8,128)S(1)} %bias_kernel.1.gate, bf16[256,512]{1,0:T(8,128)(2,1)S(1)} %get-tuple-element.39.qt, f32[256,256]{1,0:T(8,128)S(1)} %get-tuple-element.53.acc, f32[8,512]{1,0:T(8,128)S(1)} %get-tuple-element.54.ml, bf16[384,512]{1,0:T(8,128)(2,1)S(1)} %row_join_kernel.1.mine, ...), custom_call_target="tpu_custom_call" | custom-call | flops 1000000 | bytes 1000 | tf_op jit(solution)/shard_map/far_kernel/pallas_call | solution.py:298
  36.1 3.3 %collective-permute-done.13.peer_att = bf16[256,256]{1,0:T(8,128)(2,1)S(1)} collective-permute-done((bf16[256,256]{1,0:T(8,128)(2,1)S(1)}, bf16[256,256]{1,0:T(8,128)(2,1)S(1)}, u32[]{:S(2)}, u32[]{:S(2)}) %collective-permute-start.13) | collective-permute-done | bytes 131104 | tf_op jit(solution)/shard_map/ppermute | solution.py:417
  39.7 1.1 %collective-permute-start.14 = (bf16[256,256]{1,0:T(8,128)(2,1)S(1)}, bf16[256,256]{1,0:T(8,128)(2,1)S(1)}, u32[]{:S(2)}, u32[]{:S(2)}) collective-permute-start(bf16[256,256]{1,0:T(8,128)(2,1)S(1)} %get-tuple-element.52), channel_id=1, source_target_pairs={{0,3},{3,0},{1,2},{2,1},{4,7},{7,4},{5,6},{6,5},{8,11},{11,8},{9,1... | collective-permute-start | bytes 393224 | tf_op jit(solution)/shard_map/ppermute | solution.py:424
  40.9 1.3 %collective-permute-done.15.peer_att = bf16[256,256]{1,0:T(8,128)(2,1)S(1)} collective-permute-done((bf16[256,256]{1,0:T(8,128)(2,1)S(1)}, bf16[256,256]{1,0:T(8,128)(2,1)S(1)}, u32[]{:S(2)}, u32[]{:S(2)}) %collective-permute-start.15) | collective-permute-done | bytes 131104 | tf_op jit(solution)/shard_map/ppermute | solution.py:417
  42.7 3.3 %collective-permute-done.14 = bf16[256,256]{1,0:T(8,128)(2,1)S(1)} collective-permute-done((bf16[256,256]{1,0:T(8,128)(2,1)S(1)}, bf16[256,256]{1,0:T(8,128)(2,1)S(1)}, u32[]{:S(2)}, u32[]{:S(2)}) %collective-permute-start.14) | collective-permute-done | bytes 131104 | tf_op jit(solution)/shard_map/ppermute | solution.py:424
  46.0 1.5 %collective-permute-done.16 = bf16[256,256]{1,0:T(8,128)(2,1)S(1)} collective-permute-done((bf16[256,256]{1,0:T(8,128)(2,1)S(1)}, bf16[256,256]{1,0:T(8,128)(2,1)S(1)}, u32[]{:S(2)}, u32[]{:S(2)}) %collective-permute-start.16) | collective-permute-done | bytes 131104 | tf_op jit(solution)/shard_map/ppermute | solution.py:424
  (37 shorter events, 5.2 us)
Async XLA Ops:
  0.0 8.8 %copy-start = (bf16[512,1024]{1,0:T(8,128)(2,1)S(1)}, bf16[512,1024]{1,0:T(8,128)(2,1)}, u32[]{:S(2)}) copy-start(bf16[512,1024]{1,0:T(8,128)(2,1)} %tok.3) | copy-start | bytes 3145732
  0.0 8.8 %copy-start.2 = (bf16[1024,256]{1,0:T(8,128)(2,1)S(1)}, bf16[1024,256]{1,0:T(8,128)(2,1)}, u32[]{:S(2)}) copy-start(bf16[1024,256]{1,0:T(8,128)(2,1)} %wq.3) | copy-start | bytes 1572868
  3.2 7.8 %collective-permute-start = (bf16[176,512]{1,0:T(8,128)(2,1)S(1)}, bf16[176,512]{1,0:T(8,128)(2,1)S(1)}, u32[]{:S(2)}, u32[]{:S(2)}) collective-permute-start(bf16[176,512]{1,0:T(8,128)(2,1)S(1)} %get-tuple-element.38.share), channel_id=1, source_target_pairs={{0,4},{4,0},{8,12},{12,8},{16,20},{20,16},{24,28},{28,24},{32,36},... | collective-permute-start | bytes 540680 | tf_op jit(solution)/shard_map/swap_share/ppermute | solution.py:311
  3.3 5.4 %copy-start.3 = (s32[4,16]{1,0:T(4,128)S(1)}, s32[4,16]{1,0:T(4,128)}, u32[]{:S(2)}) copy-start(s32[4,16]{1,0:T(4,128)} %gate.1) | copy-start | bytes 772
  3.3 17.5 %collective-permute-start.7 = (bf16[256,512]{1,0:T(8,128)(2,1)S(1)}, bf16[256,512]{1,0:T(8,128)(2,1)S(1)}, u32[]{:S(2)}, u32[]{:S(2)}) collective-permute-start(bf16[256,512]{1,0:T(8,128)(2,1)S(1)} %get-tuple-element.49), channel_id=1, source_target_pairs={{0,1},{1,0},{2,3},{3,2},{4,5},{5,4},{6,7},{7,6},{8,9},{9,8},{10,11... | collective-permute-start | bytes 786440 | tf_op jit(solution)/shard_map/ppermute | solution.py:364
  5.0 15.8 %collective-permute-start.8 = (bf16[256,512]{1,0:T(8,128)(2,1)S(1)}, bf16[256,512]{1,0:T(8,128)(2,1)S(1)}, u32[]{:S(2)}, u32[]{:S(2)}) collective-permute-start(bf16[256,512]{1,0:T(8,128)(2,1)S(1)} %get-tuple-element.50), channel_id=1, source_target_pairs={{0,3},{3,0},{1,2},{2,1},{4,7},{7,4},{5,6},{6,5},{8,11},{11,8},{9,1... | collective-permute-start | bytes 786440 | tf_op jit(solution)/shard_map/ppermute | solution.py:365
  7.2 4.6 %collective-permute-start.1 = (bf16[96,512]{1,0:T(8,128)(2,1)S(1)}, bf16[96,512]{1,0:T(8,128)(2,1)S(1)}, u32[]{:S(2)}, u32[]{:S(2)}) collective-permute-start(bf16[96,512]{1,0:T(8,128)(2,1)S(1)} %get-tuple-element.43.sent), channel_id=1, source_target_pairs={{0,8},{4,12},{8,0},{12,4},{16,24},{20,28},{24,16},{28,20},{32,40},... | collective-permute-start | bytes 294920 | tf_op jit(solution)/shard_map/across_one/ppermute | solution.py:311
  11.0 3.8 %collective-permute-start.4 = (bf16[16,512]{1,0:T(8,128)(2,1)S(1)}, bf16[16,512]{1,0:T(8,128)(2,1)S(1)}, u32[]{:S(2)}, u32[]{:S(2)}) collective-permute-start(bf16[16,512]{1,0:T(8,128)(2,1)S(1)} %mirror_kernel.1.refs_5_), channel_id=1, source_target_pairs={{4,196},{12,204},{20,212},{28,220},{36,228},{44,236},{52,244},{60,... | collective-permute-start | bytes 49160 | tf_op jit(solution)/shard_map/planes_mirror/ppermute | solution.py:311
  11.8 8.0 %collective-permute-start.2 = (bf16[64,512]{1,0:T(8,128)(2,1)S(1)}, bf16[64,512]{1,0:T(8,128)(2,1)S(1)}, u32[]{:S(2)}, u32[]{:S(2)}) collective-permute-start(bf16[64,512]{1,0:T(8,128)(2,1)S(1)} %near_join_kernel.1), channel_id=1, source_target_pairs={{0,16},{4,20},{8,24},{12,28},{16,0},{20,4},{24,8},{28,12},{32,48},... | collective-permute-start | bytes 196616 | tf_op jit(solution)/shard_map/across_two/ppermute | solution.py:311
  14.9 3.9 %collective-permute-start.5 = (bf16[32,512]{1,0:T(8,128)(2,1)S(1)}, bf16[32,512]{1,0:T(8,128)(2,1)S(1)}, u32[]{:S(2)}, u32[]{:S(2)}) collective-permute-start(bf16[32,512]{1,0:T(8,128)(2,1)S(1)} %two_kernel.1.sent), channel_id=1, source_target_pairs={{4,68},{12,76},{20,84},{28,92},{36,100},{44,108},{52,116},{60,124}... | collective-permute-start | bytes 98312 | tf_op jit(solution)/shard_map/planes_two/ppermute | solution.py:311
  18.8 4.3 %collective-permute-start.6 = (bf16[64,512]{1,0:T(8,128)(2,1)S(1)}, bf16[64,512]{1,0:T(8,128)(2,1)S(1)}, u32[]{:S(2)}, u32[]{:S(2)}) collective-permute-start(bf16[64,512]{1,0:T(8,128)(2,1)S(1)} %joint_kernel.1.sent), channel_id=1, source_target_pairs={{4,36},{12,44},{20,52},{28,60},{36,4},{44,12},{52,20},{60,28},{68,... | collective-permute-start | bytes 196616 | tf_op jit(solution)/shard_map/planes_one/ppermute | solution.py:311
  19.9 5.8 %collective-permute-start.3 = (bf16[128,512]{1,0:T(8,128)(2,1)S(1)}, bf16[128,512]{1,0:T(8,128)(2,1)S(1)}, u32[]{:S(2)}, u32[]{:S(2)}) collective-permute-start(bf16[128,512]{1,0:T(8,128)(2,1)S(1)} %plane_join_kernel.1), channel_id=1, source_target_pairs={{0,4},{4,0},{8,12},{12,8},{16,20},{20,16},{24,28},{28,24},{32,36},... | collective-permute-start | bytes 393224 | tf_op jit(solution)/shard_map/swap_near/ppermute | solution.py:311
  23.1 4.7 %collective-permute-start.10 = (bf16[96,512]{1,0:T(8,128)(2,1)S(1)}, bf16[96,512]{1,0:T(8,128)(2,1)S(1)}, u32[]{:S(2)}, u32[]{:S(2)}) collective-permute-start(bf16[96,512]{1,0:T(8,128)(2,1)S(1)} %far_join_kernel.1.a), channel_id=1, source_target_pairs={{4,28},{12,4},{20,12},{28,20},{36,60},{44,36},{52,44},{60,52},{68,... | collective-permute-start | bytes 294920 | tf_op jit(solution)/shard_map/along/ppermute | solution.py:311
  23.6 5.2 %collective-permute-start.11 = (bf16[96,512]{1,0:T(8,128)(2,1)S(1)}, bf16[96,512]{1,0:T(8,128)(2,1)S(1)}, u32[]{:S(2)}, u32[]{:S(2)}) collective-permute-start(bf16[96,512]{1,0:T(8,128)(2,1)S(1)} %far_join_kernel.1.a), channel_id=1, source_target_pairs={{4,20},{12,28},{20,4},{28,12},{36,52},{44,60},{52,36},{60,44},{68,... | collective-permute-start | bytes 294920 | tf_op jit(solution)/shard_map/along/ppermute | solution.py:311
  25.2 4.7 %collective-permute-start.9 = (bf16[96,512]{1,0:T(8,128)(2,1)S(1)}, bf16[96,512]{1,0:T(8,128)(2,1)S(1)}, u32[]{:S(2)}, u32[]{:S(2)}) collective-permute-start(bf16[96,512]{1,0:T(8,128)(2,1)S(1)} %far_join_kernel.1.a), channel_id=1, source_target_pairs={{4,12},{12,20},{20,28},{28,4},{36,44},{44,52},{52,60},{60,36},{68,... | collective-permute-start | bytes 294920 | tf_op jit(solution)/shard_map/along/ppermute | solution.py:311
  29.9 2.6 %collective-permute-start.12 = (bf16[384,512]{1,0:T(8,128)(2,1)S(1)}, bf16[384,512]{1,0:T(8,128)(2,1)S(1)}, u32[]{:S(2)}, u32[]{:S(2)}) collective-permute-start(bf16[384,512]{1,0:T(8,128)(2,1)S(1)} %row_join_kernel.1.mine), channel_id=1, source_target_pairs={{0,4},{4,0},{8,12},{12,8},{16,20},{20,16},{24,28},{28,24},{32,36},... | collective-permute-start | bytes 1179656 | tf_op jit(solution)/shard_map/swap_far/ppermute | solution.py:311
  33.6 5.9 %collective-permute-start.13 = (bf16[256,256]{1,0:T(8,128)(2,1)S(1)}, bf16[256,256]{1,0:T(8,128)(2,1)S(1)}, u32[]{:S(2)}, u32[]{:S(2)}) collective-permute-start(bf16[256,256]{1,0:T(8,128)(2,1)S(1)} %far_kernel.2.mine_att.after), channel_id=1, source_target_pairs={{0,1},{1,0},{2,3},{3,2},{4,5},{5,4},{6,7},{7,6},{8,9},{9,8},{10,11... | collective-permute-start | bytes 393224 | tf_op jit(solution)/shard_map/ppermute | solution.py:417
  34.4 5.1 %copy-start.1 = (bf16[256,1024]{1,0:T(8,128)(2,1)S(1)}, bf16[256,1024]{1,0:T(8,128)(2,1)}, u32[]{:S(2)}) copy-start(bf16[256,1024]{1,0:T(8,128)(2,1)} %mine_w.3) | copy-start | bytes 1572868
  35.4 6.8 %collective-permute-start.15 = (bf16[256,256]{1,0:T(8,128)(2,1)S(1)}, bf16[256,256]{1,0:T(8,128)(2,1)S(1)}, u32[]{:S(2)}, u32[]{:S(2)}) collective-permute-start(bf16[256,256]{1,0:T(8,128)(2,1)S(1)} %far_kernel.3.mine_att), channel_id=1, source_target_pairs={{0,3},{3,0},{1,2},{2,1},{4,7},{7,4},{5,6},{6,5},{8,11},{11,8},{9,1... | collective-permute-start | bytes 393224 | tf_op jit(solution)/shard_map/ppermute | solution.py:417
  39.7 6.3 %collective-permute-start.14 = (bf16[256,256]{1,0:T(8,128)(2,1)S(1)}, bf16[256,256]{1,0:T(8,128)(2,1)S(1)}, u32[]{:S(2)}, u32[]{:S(2)}) collective-permute-start(bf16[256,256]{1,0:T(8,128)(2,1)S(1)} %get-tuple-element.52), channel_id=1, source_target_pairs={{0,3},{3,0},{1,2},{2,1},{4,7},{7,4},{5,6},{6,5},{8,11},{11,8},{9,1... | collective-permute-start | bytes 393224 | tf_op jit(solution)/shard_map/ppermute | solution.py:424
  42.5 5.1 %collective-permute-start.16 = (bf16[256,256]{1,0:T(8,128)(2,1)S(1)}, bf16[256,256]{1,0:T(8,128)(2,1)S(1)}, u32[]{:S(2)}, u32[]{:S(2)}) collective-permute-start(bf16[256,256]{1,0:T(8,128)(2,1)S(1)} %get-tuple-element.56), channel_id=1, source_target_pairs={{0,1},{1,0},{2,3},{3,2},{4,5},{5,4},{6,7},{7,6},{8,9},{9,8},{10,11... | collective-permute-start | bytes 393224 | tf_op jit(solution)/shard_map/ppermute | solution.py:424

commit v7 on v6

--- a/solution.py
+++ b/solution.py
@@ -98,7 +98,7 @@
     out[48:64, :] = jnp.concatenate([mine, peer], axis=0).astype(BF16)
 
 
-def far_join_kernel(sent, got, w_next, w_far, out):
+def far_join_kernel(sent, got, out):
     out[0:32, :] = got[0:32, :]
     for level in (1, 2):
         to, at = level * 32, 16 + level * 16
@@ -361,8 +361,6 @@
         compiler_params=pltpu.CompilerParams(vmem_limit_bytes=105 * 512 * 1024),
         cost_estimate=pl.CostEstimate(flops=COST, bytes_accessed=1000, transcendentals=0),
     )(tokens, wk, wv, wo)
-    w_next = lax.ppermute(to_next, "head", PAIR_NEXT)
-    w_far = lax.ppermute(to_far, "head", PAIR_FAR)
     share_other = swap(share, "swap_share")
     first = across(e1, 1, "across_one")
     state = [((WIDTH, 256), F32), ((8, 512), F32)]
@@ -387,9 +385,12 @@
         joint_kernel, (share, share_other, pay, got, own[0][1]), [rows(64)], COST, unread=1
     )
     got = hub(pay, lambda z, x: (z ^ 1, x), idle_x, "planes_one")
-    (far,) = call(far_join_kernel, (pay, got, w_next, w_far), [rows(96)], COST, unread=2)
+    (far,) = call(far_join_kernel, (pay, got), [rows(96)], COST)
     (near,) = call(plane_join_kernel, (first, second), [rows(128)], COST)
     other = swap(near, "swap_near")
+    far, to_far, to_next = lax.optimization_barrier((far, to_far, to_next))
+    w_next = lax.ppermute(to_next, "head", PAIR_NEXT)
+    w_far = lax.ppermute(to_far, "head", PAIR_FAR)
     acc0, ml0, acc1, ml1 = call(
         plane_kernel,
         (gate, qt, *own[0], *own[1], share_other, first, second, other),

time: 48.4 us -> 49.7 us (1.027)
  starting transfers between devices: 18.4 us -> 22 us
  waiting for transfers between devices: 18.8 us -> 16.4 us
    ppermute x2, waiting for transfers between devices: 4.59 us -> 1.97 us  [shards(): peer = lax.ppermute(halves[half], 'head', pairs[half])]
    ppermute x2, starting transfers between devices: 1.36 us -> 3.33 us  [shards(): out.append(keep + lax.ppermute(send, 'head', pairs[1 - half]).astype(F32))]
    ppermute x11, starting transfers between devices: 11.7 us -> 13.4 us  [move(): return lax.ppermute(array, 'seq', pairs)]
    ppermute x1, waiting for transfers between devices: 0.01 us -> 1.74 us  [shards(): w_next = lax.ppermute(to_next, 'head', PAIR_NEXT)]
    ppermute x11, waiting for transfers between devices: 9.4 us -> 7.88 us  [move(): return lax.ppermute(array, 'seq', pairs)]
  transfers between devices with their start and end apart: 17 -> 17, of which waited for: 11 -> 11; matrix products, arithmetic and copies ran while one was open for 0% -> 0% of each run, Pallas kernels for 12% -> 14%
where the time goes in v7:
time: 49.7 us; the launch traced here: 49.6 us
  starting transfers between devices  22 us (44%)
  waiting for transfers between devices  16.4 us (33%)
  Pallas kernels  10.2 us (21%)
  other arithmetic  0.77 us (2%)
    ppermute x11, starting transfers between devices, move(): return lax.ppermute(array, 'seq', pairs)  13.4 us
    ppermute x11, waiting for transfers between devices, move(): return lax.ppermute(array, 'seq', pairs)  7.88 us
    pallas_call x15, Pallas kernels, call(): pl.pallas_call(kernel, name=getattr(kernel, 'func', kernel).__name__, out...  6.98 us
    ppermute x2, waiting for transfers between devices, shards(): out.append(keep + lax.ppermute(send, 'head', pairs[1 - half]).astype(F32))  4.8 us
    ppermute x2, starting transfers between devices, shards(): out.append(keep + lax.ppermute(send, 'head', pairs[1 - half]).astype(F32))  3.33 us
    pallas_call x1, Pallas kernels, shards(): pl.pallas_call(load_kernel, name='load_kernel', out_shape=[jax.ShapeDtype...  3.21 us
    ppermute x1, starting transfers between devices, shards(): w_far = lax.ppermute(to_far, 'head', PAIR_FAR)  2.18 us
    ppermute x2, waiting for transfers between devices, shards(): peer = lax.ppermute(halves[half], 'head', pairs[half])  1.97 us
  transfers between devices with their start and end apart: 17, of which 11 were waited for; matrix products, arithmetic and copies ran while one was open for 0% of the time, Pallas kernels for 14%

profile of v7, /device:TPU:32, one launch (start us, length us, event | category | flops | bytes accessed | tf_op | source)
XLA Modules:
  0.0 49.6 jit_solution(9280983423040380812)
XLA Ops:
  0.0 3.2 %load_kernel.1 = (bf16[512,512]{1,0:T(8,128)(2,1)S(1)}, bf16[128,512]{1,0:T(8,128)(2,1)S(1)}, bf16[96,512]{1,0:T(8,128)(2,1)S(1)}, bf16[176,512]{1,0:T(8,128)(2,...) custom-call(bf16[512,1024]{1,0:T(8,128)(2,1)} %tok.3, bf16[1024,256]{1,0:T(8,128)(2,1)} %wk_hbm.1, ...), custom_call_target="tpu_custom_call" | custom-call | flops 1000000 | bytes 1000 | tf_op jit(solution)/shard_map/load_kernel/pallas_call | solution.py:345
  3.3 1.6 %collective-permute-start.1 = (bf16[96,512]{1,0:T(8,128)(2,1)S(1)}, bf16[96,512]{1,0:T(8,128)(2,1)S(1)}, u32[]{:S(2)}, u32[]{:S(2)}) collective-permute-start(bf16[96,512]{1,0:T(8,128)(2,1)S(1)} %get-tuple-element.46.sent), channel_id=1, source_target_pairs={{0,8},{4,12},{8,0},{12,4},{16,24},{20,28},{24,16},{28,20},{32,40},... | collective-permute-start | bytes 294920 | tf_op jit(solution)/shard_map/across_one/ppermute | solution.py:311
  5.1 2.2 %early_kernel.1 = (bf16[256,512]{1,0:T(8,128)(2,1)S(1)}, f32[256,256]{1,0:T(8,128)S(1)}, f32[8,512]{1,0:T(8,128)S(1)}, f32[256,256]{1,0:T(8,128)S(1)}, f32[8,512]{1,0:T(8,128)S(1)}) custom-call(f32[32,128]{1,0:T(8,128)S(1)} %bias_kernel.1.gate, bf16[512,1024]{1,0:T(8,128)(2,1)S(1)} %copy-done, bf16[1024,256]{1,0:T(8,128)(2,1)S(1)} %copy-done.2, ...), custom_call_target="tpu_custom_call" | custom-call | flops 1000000 | bytes 1000 | tf_op jit(solution)/shard_map/early_kernel/pallas_call | solution.py:298
  8.6 2.5 %collective-permute-done.4.got = bf16[16,512]{1,0:T(8,128)(2,1)S(1)} collective-permute-done((bf16[16,512]{1,0:T(8,128)(2,1)S(1)}, bf16[16,512]{1,0:T(8,128)(2,1)S(1)}, u32[]{:S(2)}, u32[]{:S(2)}) %collective-permute-start.4) | collective-permute-done | bytes 16416 | tf_op jit(solution)/shard_map/planes_mirror/ppermute | solution.py:311
  11.6 3.0 %collective-permute-start.2 = (bf16[64,512]{1,0:T(8,128)(2,1)S(1)}, bf16[64,512]{1,0:T(8,128)(2,1)S(1)}, u32[]{:S(2)}, u32[]{:S(2)}) collective-permute-start(bf16[64,512]{1,0:T(8,128)(2,1)S(1)} %near_join_kernel.1), channel_id=1, source_target_pairs={{0,16},{4,20},{8,24},{12,28},{16,0},{20,4},{24,8},{28,12},{32,48},... | collective-permute-start | bytes 196616 | tf_op jit(solution)/shard_map/across_two/ppermute | solution.py:311
  15.6 1.9 %collective-permute-done.2.second = bf16[64,512]{1,0:T(8,128)(2,1)S(1)} collective-permute-done((bf16[64,512]{1,0:T(8,128)(2,1)S(1)}, bf16[64,512]{1,0:T(8,128)(2,1)S(1)}, u32[]{:S(2)}, u32[]{:S(2)}) %collective-permute-start.2) | collective-permute-done | bytes 65568 | tf_op jit(solution)/shard_map/across_two/ppermute | solution.py:311
  17.4 2.5 %collective-permute-start.3 = (bf16[128,512]{1,0:T(8,128)(2,1)S(1)}, bf16[128,512]{1,0:T(8,128)(2,1)S(1)}, u32[]{:S(2)}, u32[]{:S(2)}) collective-permute-start(bf16[128,512]{1,0:T(8,128)(2,1)S(1)} %plane_join_kernel.1), channel_id=1, source_target_pairs={{0,4},{4,0},{8,12},{12,8},{16,20},{20,16},{24,28},{28,24},{32,36},... | collective-permute-start | bytes 393224 | tf_op jit(solution)/shard_map/swap_near/ppermute | solution.py:311
  20.3 1.7 %collective-permute-start.8 = (bf16[96,512]{1,0:T(8,128)(2,1)S(1)}, bf16[96,512]{1,0:T(8,128)(2,1)S(1)}, u32[]{:S(2)}, u32[]{:S(2)}) collective-permute-start(bf16[96,512]{1,0:T(8,128)(2,1)S(1)} %far_join_kernel.1.a), channel_id=1, source_target_pairs={{4,28},{12,4},{20,12},{28,20},{36,60},{44,36},{52,44},{60,52},{68,... | collective-permute-start | bytes 294920 | tf_op jit(solution)/shard_map/along/ppermute | solution.py:311
  22.4 1.9 %plane_kernel.1 = (f32[256,256]{1,0:T(8,128)S(1)}, f32[8,512]{1,0:T(8,128)S(1)}, f32[256,256]{1,0:T(8,128)S(1)}, f32[8,512]{1,0:T(8,128)S(1)}) custom-call(f32[32,128]{1,0:T(8,128)S(1)} %bias_kernel.1.gate, bf16[256,512]{1,0:T(8,128)(2,1)S(1)} %get-tuple-element.42.qt, f32[256,256]{1,0:T(8,128)S(1)} %get-tuple-element.43.acc0, ...), custom_call_target="tpu_custom_call" | custom-call | flops 1000000 | bytes 1000 | tf_op jit(solution)/shard_map/plane_kernel/pallas_call | solution.py:298
  24.6 1.1 %collective-permute-done.8.c = bf16[96,512]{1,0:T(8,128)(2,1)S(1)} collective-permute-done((bf16[96,512]{1,0:T(8,128)(2,1)S(1)}, bf16[96,512]{1,0:T(8,128)(2,1)S(1)}, u32[]{:S(2)}, u32[]{:S(2)}) %collective-permute-start.8) | collective-permute-done | bytes 98336 | tf_op jit(solution)/shard_map/along/ppermute | solution.py:311
  25.7 1.1 %collective-permute-done.9.d = bf16[96,512]{1,0:T(8,128)(2,1)S(1)} collective-permute-done((bf16[96,512]{1,0:T(8,128)(2,1)S(1)}, bf16[96,512]{1,0:T(8,128)(2,1)S(1)}, u32[]{:S(2)}, u32[]{:S(2)}) %collective-permute-start.9) | collective-permute-done | bytes 98336 | tf_op jit(solution)/shard_map/along/ppermute | solution.py:311
  26.8 2.1 %collective-permute-start.10 = (bf16[384,512]{1,0:T(8,128)(2,1)S(1)}, bf16[384,512]{1,0:T(8,128)(2,1)S(1)}, u32[]{:S(2)}, u32[]{:S(2)}) collective-permute-start(bf16[384,512]{1,0:T(8,128)(2,1)S(1)} %row_join_kernel.1.mine), channel_id=1, source_target_pairs={{0,4},{4,0},{8,12},{12,8},{16,20},{20,16},{24,28},{28,24},{32,36},... | collective-permute-start | bytes 1179656 | tf_op jit(solution)/shard_map/swap_far/ppermute | solution.py:311
  28.9 1.6 %collective-permute-start.12 = (bf16[256,512]{1,0:T(8,128)(2,1)S(1)}, bf16[256,512]{1,0:T(8,128)(2,1)S(1)}, u32[]{:S(2)}, u32[]{:S(2)}) collective-permute-start(bf16[256,512]{1,0:T(8,128)(2,1)S(1)} %get-tuple-element.55), channel_id=1, source_target_pairs={{0,1},{1,0},{2,3},{3,2},{4,5},{5,4},{6,7},{7,6},{8,9},{9,8},{10,11... | collective-permute-start | bytes 786440 | tf_op jit(solution)/shard_map/ppermute | solution.py:392
  30.5 2.2 %collective-permute-start.15 = (bf16[256,512]{1,0:T(8,128)(2,1)S(1)}, bf16[256,512]{1,0:T(8,128)(2,1)S(1)}, u32[]{:S(2)}, u32[]{:S(2)}) collective-permute-start(bf16[256,512]{1,0:T(8,128)(2,1)S(1)} %get-tuple-element.60), channel_id=1, source_target_pairs={{0,3},{3,0},{1,2},{2,1},{4,7},{7,4},{5,6},{6,5},{8,11},{11,8},{9,1... | collective-permute-start | bytes 786440 | tf_op jit(solution)/shard_map/ppermute | solution.py:393
  32.7 1.1 %far_kernel.2.mine_att.after = bf16[256,256]{1,0:T(8,128)(2,1)S(1)} custom-call(f32[32,128]{1,0:T(8,128)S(1)} %bias_kernel.1.gate, bf16[256,512]{1,0:T(8,128)(2,1)S(1)} %get-tuple-element.42.qt, f32[256,256]{1,0:T(8,128)S(1)} %get-tuple-element.50.acc, f32[8,512]{1,0:T(8,128)S(1)} %get-tuple-element.51.after.ml, bf16[384,512]{1,0:T(8,128)(2,1)S(1)} %row_join_kernel.1.mine, ...), custom_call_target="tpu_custom_call" | custom-call | flops 1000000 | bytes 1000 | tf_op jit(solution)/shard_map/far_kernel/pallas_call | solution.py:298
  33.7 0.8 %collective-permute-start.11 = (bf16[256,256]{1,0:T(8,128)(2,1)S(1)}, bf16[256,256]{1,0:T(8,128)(2,1)S(1)}, u32[]{:S(2)}, u32[]{:S(2)}) collective-permute-start(bf16[256,256]{1,0:T(8,128)(2,1)S(1)} %far_kernel.2.mine_att.after), channel_id=1, source_target_pairs={{0,1},{1,0},{2,3},{3,2},{4,5},{5,4},{6,7},{7,6},{8,9},{9,8},{10,11... | collective-permute-start | bytes 393224 | tf_op jit(solution)/shard_map/ppermute | solution.py:418
  34.5 1.1 %far_kernel.3.mine_att = bf16[256,256]{1,0:T(8,128)(2,1)S(1)} custom-call(f32[32,128]{1,0:T(8,128)S(1)} %bias_kernel.1.gate, bf16[256,512]{1,0:T(8,128)(2,1)S(1)} %get-tuple-element.42.qt, f32[256,256]{1,0:T(8,128)S(1)} %get-tuple-element.58.acc, f32[8,512]{1,0:T(8,128)S(1)} %get-tuple-element.59.ml, bf16[384,512]{1,0:T(8,128)(2,1)S(1)} %row_join_kernel.1.mine, ...), custom_call_target="tpu_custom_call" | custom-call | flops 1000000 | bytes 1000 | tf_op jit(solution)/shard_map/far_kernel/pallas_call | solution.py:298
  35.6 0.8 %collective-permute-start.14 = (bf16[256,256]{1,0:T(8,128)(2,1)S(1)}, bf16[256,256]{1,0:T(8,128)(2,1)S(1)}, u32[]{:S(2)}, u32[]{:S(2)}) collective-permute-start(bf16[256,256]{1,0:T(8,128)(2,1)S(1)} %far_kernel.3.mine_att), channel_id=1, source_target_pairs={{0,3},{3,0},{1,2},{2,1},{4,7},{7,4},{5,6},{6,5},{8,11},{11,8},{9,1... | collective-permute-start | bytes 393224 | tf_op jit(solution)/shard_map/ppermute | solution.py:418
  36.3 1.7 %collective-permute-done.12.peer_w = bf16[256,512]{1,0:T(8,128)(2,1)S(1)} collective-permute-done((bf16[256,512]{1,0:T(8,128)(2,1)S(1)}, bf16[256,512]{1,0:T(8,128)(2,1)S(1)}, u32[]{:S(2)}, u32[]{:S(2)}) %collective-permute-start.12) | collective-permute-done | bytes 262176 | tf_op jit(solution)/shard_map/ppermute | solution.py:392
  38.1 2.0 %collective-permute-done.11.peer_att = bf16[256,256]{1,0:T(8,128)(2,1)S(1)} collective-permute-done((bf16[256,256]{1,0:T(8,128)(2,1)S(1)}, bf16[256,256]{1,0:T(8,128)(2,1)S(1)}, u32[]{:S(2)}, u32[]{:S(2)}) %collective-permute-start.11) | collective-permute-done | bytes 131104 | tf_op jit(solution)/shard_map/ppermute | solution.py:418
  40.3 3.1 %collective-permute-start.13 = (bf16[256,256]{1,0:T(8,128)(2,1)S(1)}, bf16[256,256]{1,0:T(8,128)(2,1)S(1)}, u32[]{:S(2)}, u32[]{:S(2)}) collective-permute-start(bf16[256,256]{1,0:T(8,128)(2,1)S(1)} %get-tuple-element.57), channel_id=1, source_target_pairs={{0,3},{3,0},{1,2},{2,1},{4,7},{7,4},{5,6},{6,5},{8,11},{11,8},{9,1... | collective-permute-start | bytes 393224 | tf_op jit(solution)/shard_map/ppermute | solution.py:425
  44.0 2.6 %collective-permute-done.13 = bf16[256,256]{1,0:T(8,128)(2,1)S(1)} collective-permute-done((bf16[256,256]{1,0:T(8,128)(2,1)S(1)}, bf16[256,256]{1,0:T(8,128)(2,1)S(1)}, u32[]{:S(2)}, u32[]{:S(2)}) %collective-permute-start.13) | collective-permute-done | bytes 131104 | tf_op jit(solution)/shard_map/ppermute | solution.py:425
  46.6 2.2 %collective-permute-done.16 = bf16[256,256]{1,0:T(8,128)(2,1)S(1)} collective-permute-done((bf16[256,256]{1,0:T(8,128)(2,1)S(1)}, bf16[256,256]{1,0:T(8,128)(2,1)S(1)}, u32[]{:S(2)}, u32[]{:S(2)}) %collective-permute-start.16) | collective-permute-done | bytes 131104 | tf_op jit(solution)/shard_map/ppermute | solution.py:425
  48.8 0.7 %pad_maximum_fusion = bf16[512,256]{1,0:T(8,128)(2,1)} fusion(bf16[256,256]{1,0:T(8,128)(2,1)S(1)} %add_convert_fusion, bf16[256,256]{1,0:T(8,128)(2,1)S(1)} %add_convert_fusion.1), kind=kLoop, calls=%fused_computation | loop fusion | flops 524288 | bytes 524288 | tf_op jit(solution)/shard_map/concatenate | solution.py:426
  (37 shorter events, 5.0 us)
Async XLA Ops:
  0.0 5.0 %copy-start = (bf16[512,1024]{1,0:T(8,128)(2,1)S(1)}, bf16[512,1024]{1,0:T(8,128)(2,1)}, u32[]{:S(2)}) copy-start(bf16[512,1024]{1,0:T(8,128)(2,1)} %tok.3) | copy-start | bytes 3145732
  0.0 5.0 %copy-start.2 = (bf16[1024,256]{1,0:T(8,128)(2,1)S(1)}, bf16[1024,256]{1,0:T(8,128)(2,1)}, u32[]{:S(2)}) copy-start(bf16[1024,256]{1,0:T(8,128)(2,1)} %wq.3) | copy-start | bytes 1572868
  3.2 1.7 %copy-start.3 = (s32[4,16]{1,0:T(4,128)S(1)}, s32[4,16]{1,0:T(4,128)}, u32[]{:S(2)}) copy-start(s32[4,16]{1,0:T(4,128)} %gate.1) | copy-start | bytes 772
  3.2 4.0 %collective-permute-start = (bf16[176,512]{1,0:T(8,128)(2,1)S(1)}, bf16[176,512]{1,0:T(8,128)(2,1)S(1)}, u32[]{:S(2)}, u32[]{:S(2)}) collective-permute-start(bf16[176,512]{1,0:T(8,128)(2,1)S(1)} %get-tuple-element.41.share), channel_id=1, source_target_pairs={{0,4},{4,0},{8,12},{12,8},{16,20},{20,16},{24,28},{28,24},{32,36},... | collective-permute-start | bytes 540680 | tf_op jit(solution)/shard_map/swap_share/ppermute | solution.py:311
  3.3 5.2 %collective-permute-start.1 = (bf16[96,512]{1,0:T(8,128)(2,1)S(1)}, bf16[96,512]{1,0:T(8,128)(2,1)S(1)}, u32[]{:S(2)}, u32[]{:S(2)}) collective-permute-start(bf16[96,512]{1,0:T(8,128)(2,1)S(1)} %get-tuple-element.46.sent), channel_id=1, source_target_pairs={{0,8},{4,12},{8,0},{12,4},{16,24},{20,28},{24,16},{28,20},{32,40},... | collective-permute-start | bytes 294920 | tf_op jit(solution)/shard_map/across_one/ppermute | solution.py:311
  7.3 3.8 %collective-permute-start.4 = (bf16[16,512]{1,0:T(8,128)(2,1)S(1)}, bf16[16,512]{1,0:T(8,128)(2,1)S(1)}, u32[]{:S(2)}, u32[]{:S(2)}) collective-permute-start(bf16[16,512]{1,0:T(8,128)(2,1)S(1)} %mirror_kernel.1.refs_5_), channel_id=1, source_target_pairs={{4,196},{12,204},{20,212},{28,220},{36,228},{44,236},{52,244},{60,... | collective-permute-start | bytes 49160 | tf_op jit(solution)/shard_map/planes_mirror/ppermute | solution.py:311
  11.1 3.9 %collective-permute-start.5 = (bf16[32,512]{1,0:T(8,128)(2,1)S(1)}, bf16[32,512]{1,0:T(8,128)(2,1)S(1)}, u32[]{:S(2)}, u32[]{:S(2)}) collective-permute-start(bf16[32,512]{1,0:T(8,128)(2,1)S(1)} %two_kernel.1.sent), channel_id=1, source_target_pairs={{4,68},{12,76},{20,84},{28,92},{36,100},{44,108},{52,116},{60,124}... | collective-permute-start | bytes 98312 | tf_op jit(solution)/shard_map/planes_two/ppermute | solution.py:311
  11.6 5.8 %collective-permute-start.2 = (bf16[64,512]{1,0:T(8,128)(2,1)S(1)}, bf16[64,512]{1,0:T(8,128)(2,1)S(1)}, u32[]{:S(2)}, u32[]{:S(2)}) collective-permute-start(bf16[64,512]{1,0:T(8,128)(2,1)S(1)} %near_join_kernel.1), channel_id=1, source_target_pairs={{0,16},{4,20},{8,24},{12,28},{16,0},{20,4},{24,8},{28,12},{32,48},... | collective-permute-start | bytes 196616 | tf_op jit(solution)/shard_map/across_two/ppermute | solution.py:311
  15.0 4.9 %collective-permute-start.6 = (bf16[64,512]{1,0:T(8,128)(2,1)S(1)}, bf16[64,512]{1,0:T(8,128)(2,1)S(1)}, u32[]{:S(2)}, u32[]{:S(2)}) collective-permute-start(bf16[64,512]{1,0:T(8,128)(2,1)S(1)} %joint_kernel.1.sent), channel_id=1, source_target_pairs={{4,36},{12,44},{20,52},{28,60},{36,4},{44,12},{52,20},{60,28},{68,... | collective-permute-start | bytes 196616 | tf_op jit(solution)/shard_map/planes_one/ppermute | solution.py:311
  17.4 4.9 %collective-permute-start.3 = (bf16[128,512]{1,0:T(8,128)(2,1)S(1)}, bf16[128,512]{1,0:T(8,128)(2,1)S(1)}, u32[]{:S(2)}, u32[]{:S(2)}) collective-permute-start(bf16[128,512]{1,0:T(8,128)(2,1)S(1)} %plane_join_kernel.1), channel_id=1, source_target_pairs={{0,4},{4,0},{8,12},{12,8},{16,20},{20,16},{24,28},{28,24},{32,36},... | collective-permute-start | bytes 393224 | tf_op jit(solution)/shard_map/swap_near/ppermute | solution.py:311
  19.9 4.7 %collective-permute-start.7 = (bf16[96,512]{1,0:T(8,128)(2,1)S(1)}, bf16[96,512]{1,0:T(8,128)(2,1)S(1)}, u32[]{:S(2)}, u32[]{:S(2)}) collective-permute-start(bf16[96,512]{1,0:T(8,128)(2,1)S(1)} %far_join_kernel.1.a), channel_id=1, source_target_pairs={{4,12},{12,20},{20,28},{28,4},{36,44},{44,52},{52,60},{60,36},{68,... | collective-permute-start | bytes 294920 | tf_op jit(solution)/shard_map/along/ppermute | solution.py:311
  20.3 5.4 %collective-permute-start.8 = (bf16[96,512]{1,0:T(8,128)(2,1)S(1)}, bf16[96,512]{1,0:T(8,128)(2,1)S(1)}, u32[]{:S(2)}, u32[]{:S(2)}) collective-permute-start(bf16[96,512]{1,0:T(8,128)(2,1)S(1)} %far_join_kernel.1.a), channel_id=1, source_target_pairs={{4,28},{12,4},{20,12},{28,20},{36,60},{44,36},{52,44},{60,52},{68,... | collective-permute-start | bytes 294920 | tf_op jit(solution)/shard_map/along/ppermute | solution.py:311
  22.0 4.7 %collective-permute-start.9 = (bf16[96,512]{1,0:T(8,128)(2,1)S(1)}, bf16[96,512]{1,0:T(8,128)(2,1)S(1)}, u32[]{:S(2)}, u32[]{:S(2)}) collective-permute-start(bf16[96,512]{1,0:T(8,128)(2,1)S(1)} %far_join_kernel.1.a), channel_id=1, source_target_pairs={{4,20},{12,28},{20,4},{28,12},{36,52},{44,60},{52,36},{60,44},{68,... | collective-permute-start | bytes 294920 | tf_op jit(solution)/shard_map/along/ppermute | solution.py:311
  26.8 5.9 %collective-permute-start.10 = (bf16[384,512]{1,0:T(8,128)(2,1)S(1)}, bf16[384,512]{1,0:T(8,128)(2,1)S(1)}, u32[]{:S(2)}, u32[]{:S(2)}) collective-permute-start(bf16[384,512]{1,0:T(8,128)(2,1)S(1)} %row_join_kernel.1.mine), channel_id=1, source_target_pairs={{0,4},{4,0},{8,12},{12,8},{16,20},{20,16},{24,28},{28,24},{32,36},... | collective-permute-start | bytes 1179656 | tf_op jit(solution)/shard_map/swap_far/ppermute | solution.py:311
  28.9 9.2 %collective-permute-start.12 = (bf16[256,512]{1,0:T(8,128)(2,1)S(1)}, bf16[256,512]{1,0:T(8,128)(2,1)S(1)}, u32[]{:S(2)}, u32[]{:S(2)}) collective-permute-start(bf16[256,512]{1,0:T(8,128)(2,1)S(1)} %get-tuple-element.55), channel_id=1, source_target_pairs={{0,1},{1,0},{2,3},{3,2},{4,5},{5,4},{6,7},{7,6},{8,9},{9,8},{10,11... | collective-permute-start | bytes 786440 | tf_op jit(solution)/shard_map/ppermute | solution.py:392
  30.5 13.0 %collective-permute-start.15 = (bf16[256,512]{1,0:T(8,128)(2,1)S(1)}, bf16[256,512]{1,0:T(8,128)(2,1)S(1)}, u32[]{:S(2)}, u32[]{:S(2)}) collective-permute-start(bf16[256,512]{1,0:T(8,128)(2,1)S(1)} %get-tuple-element.60), channel_id=1, source_target_pairs={{0,3},{3,0},{1,2},{2,1},{4,7},{7,4},{5,6},{6,5},{8,11},{11,8},{9,1... | collective-permute-start | bytes 786440 | tf_op jit(solution)/shard_map/ppermute | solution.py:393
  33.7 6.3 %collective-permute-start.11 = (bf16[256,256]{1,0:T(8,128)(2,1)S(1)}, bf16[256,256]{1,0:T(8,128)(2,1)S(1)}, u32[]{:S(2)}, u32[]{:S(2)}) collective-permute-start(bf16[256,256]{1,0:T(8,128)(2,1)S(1)} %far_kernel.2.mine_att.after), channel_id=1, source_target_pairs={{0,1},{1,0},{2,3},{3,2},{4,5},{5,4},{6,7},{7,6},{8,9},{9,8},{10,11... | collective-permute-start | bytes 393224 | tf_op jit(solution)/shard_map/ppermute | solution.py:418
  34.5 5.5 %copy-start.1 = (bf16[256,1024]{1,0:T(8,128)(2,1)S(1)}, bf16[256,1024]{1,0:T(8,128)(2,1)}, u32[]{:S(2)}) copy-start(bf16[256,1024]{1,0:T(8,128)(2,1)} %mine_w.3) | copy-start | bytes 1572868
  35.6 7.9 %collective-permute-start.14 = (bf16[256,256]{1,0:T(8,128)(2,1)S(1)}, bf16[256,256]{1,0:T(8,128)(2,1)S(1)}, u32[]{:S(2)}, u32[]{:S(2)}) collective-permute-start(bf16[256,256]{1,0:T(8,128)(2,1)S(1)} %far_kernel.3.mine_att), channel_id=1, source_target_pairs={{0,3},{3,0},{1,2},{2,1},{4,7},{7,4},{5,6},{6,5},{8,11},{11,8},{9,1... | collective-permute-start | bytes 393224 | tf_op jit(solution)/shard_map/ppermute | solution.py:418
  40.3 6.3 %collective-permute-start.13 = (bf16[256,256]{1,0:T(8,128)(2,1)S(1)}, bf16[256,256]{1,0:T(8,128)(2,1)S(1)}, u32[]{:S(2)}, u32[]{:S(2)}) collective-permute-start(bf16[256,256]{1,0:T(8,128)(2,1)S(1)} %get-tuple-element.57), channel_id=1, source_target_pairs={{0,3},{3,0},{1,2},{2,1},{4,7},{7,4},{5,6},{6,5},{8,11},{11,8},{9,1... | collective-permute-start | bytes 393224 | tf_op jit(solution)/shard_map/ppermute | solution.py:425
  43.7 5.1 %collective-permute-start.16 = (bf16[256,256]{1,0:T(8,128)(2,1)S(1)}, bf16[256,256]{1,0:T(8,128)(2,1)S(1)}, u32[]{:S(2)}, u32[]{:S(2)}) collective-permute-start(bf16[256,256]{1,0:T(8,128)(2,1)S(1)} %get-tuple-element.62), channel_id=1, source_target_pairs={{0,1},{1,0},{2,3},{3,2},{4,5},{5,4},{6,7},{7,6},{8,9},{9,8},{10,11... | collective-permute-start | bytes 393224 | tf_op jit(solution)/shard_map/ppermute | solution.py:425

commit v8 on v6

--- a/solution.py
+++ b/solution.py
@@ -98,7 +98,7 @@
     out[48:64, :] = jnp.concatenate([mine, peer], axis=0).astype(BF16)
 
 
-def far_join_kernel(sent, got, w_next, w_far, out):
+def far_join_kernel(sent, got, w_next, out):
     out[0:32, :] = got[0:32, :]
     for level in (1, 2):
         to, at = level * 32, 16 + level * 16
@@ -362,7 +362,6 @@
         cost_estimate=pl.CostEstimate(flops=COST, bytes_accessed=1000, transcendentals=0),
     )(tokens, wk, wv, wo)
     w_next = lax.ppermute(to_next, "head", PAIR_NEXT)
-    w_far = lax.ppermute(to_far, "head", PAIR_FAR)
     share_other = swap(share, "swap_share")
     first = across(e1, 1, "across_one")
     state = [((WIDTH, 256), F32), ((8, 512), F32)]
@@ -387,9 +386,11 @@
         joint_kernel, (share, share_other, pay, got, own[0][1]), [rows(64)], COST, unread=1
     )
     got = hub(pay, lambda z, x: (z ^ 1, x), idle_x, "planes_one")
-    (far,) = call(far_join_kernel, (pay, got, w_next, w_far), [rows(96)], COST, unread=2)
+    (far,) = call(far_join_kernel, (pay, got, w_next), [rows(96)], COST, unread=1)
     (near,) = call(plane_join_kernel, (first, second), [rows(128)], COST)
     other = swap(near, "swap_near")
+    far, to_far = lax.optimization_barrier((far, to_far))
+    w_far = lax.ppermute(to_far, "head", PAIR_FAR)
     acc0, ml0, acc1, ml1 = call(
         plane_kernel,
         (gate, qt, *own[0], *own[1], share_other, first, second, other),

time: 48.4 us -> 48.1 us (level)
  waiting for transfers between devices: 18.8 us -> 16.7 us
  starting transfers between devices: 18.4 us -> 19.8 us
    ppermute x2, starting transfers between devices: 1.53 us -> 2.93 us  [shards(): peer = lax.ppermute(halves[half], 'head', pairs[half])]
    ppermute x11, waiting for transfers between devices: 9.4 us -> 8.29 us  [move(): return lax.ppermute(array, 'seq', pairs)]
    ppermute x2, waiting for transfers between devices: 4.59 us -> 3.51 us  [shards(): peer = lax.ppermute(halves[half], 'head', pairs[half])]
    ppermute x2, starting transfers between devices: 1.36 us -> 1.97 us  [shards(): out.append(keep + lax.ppermute(send, 'head', pairs[1 - half]).astype(F32))]
    ppermute x11, starting transfers between devices: 11.7 us -> 11.1 us  [move(): return lax.ppermute(array, 'seq', pairs)]
  transfers between devices with their start and end apart: 17 -> 17, of which waited for: 11 -> 12; matrix products, arithmetic and copies ran while one was open for 0% -> 0% of each run, Pallas kernels for 12% -> 15%
where the time goes in v8:
time: 48.1 us; the launch traced here: 47.6 us
  starting transfers between devices  19.8 us (41%)
  waiting for transfers between devices  16.7 us (35%)
  Pallas kernels  10.2 us (21%)
  other arithmetic  0.77 us (2%)
    ppermute x11, starting transfers between devices, move(): return lax.ppermute(array, 'seq', pairs)  11.1 us
    ppermute x11, waiting for transfers between devices, move(): return lax.ppermute(array, 'seq', pairs)  8.29 us
    pallas_call x15, Pallas kernels, call(): pl.pallas_call(kernel, name=getattr(kernel, 'func', kernel).__name__, out...  6.98 us
    ppermute x2, waiting for transfers between devices, shards(): out.append(keep + lax.ppermute(send, 'head', pairs[1 - half]).astype(F32))  4.88 us
    ppermute x2, waiting for transfers between devices, shards(): peer = lax.ppermute(halves[half], 'head', pairs[half])  3.51 us
    pallas_call x1, Pallas kernels, shards(): pl.pallas_call(load_kernel, name='load_kernel', out_shape=[jax.ShapeDtype...  3.21 us
    ppermute x2, starting transfers between devices, shards(): peer = lax.ppermute(halves[half], 'head', pairs[half])  2.93 us
    ppermute x1, starting transfers between devices, shards(): w_far = lax.ppermute(to_far, 'head', PAIR_FAR)  2.18 us
  transfers between devices with their start and end apart: 17, of which 12 were waited for; matrix products, arithmetic and copies ran while one was open for 0% of the time, Pallas kernels for 15%

profile of v8, /device:TPU:32, one launch (start us, length us, event | category | flops | bytes accessed | tf_op | source)
XLA Modules:
  0.0 47.6 jit_solution(740712894422264738)
XLA Ops:
  0.0 3.2 %load_kernel.1 = (bf16[512,512]{1,0:T(8,128)(2,1)S(1)}, bf16[128,512]{1,0:T(8,128)(2,1)S(1)}, bf16[96,512]{1,0:T(8,128)(2,1)S(1)}, bf16[176,512]{1,0:T(8,128)(2,...) custom-call(bf16[512,1024]{1,0:T(8,128)(2,1)} %tok.3, bf16[1024,256]{1,0:T(8,128)(2,1)} %wk_hbm.1, ...), custom_call_target="tpu_custom_call" | custom-call | flops 1000000 | bytes 1000 | tf_op jit(solution)/shard_map/load_kernel/pallas_call | solution.py:345
  3.3 1.7 %collective-permute-start.7 = (bf16[256,512]{1,0:T(8,128)(2,1)S(1)}, bf16[256,512]{1,0:T(8,128)(2,1)S(1)}, u32[]{:S(2)}, u32[]{:S(2)}) collective-permute-start(bf16[256,512]{1,0:T(8,128)(2,1)S(1)} %get-tuple-element.51), channel_id=1, source_target_pairs={{0,1},{1,0},{2,3},{3,2},{4,5},{5,4},{6,7},{7,6},{8,9},{9,8},{10,11... | collective-permute-start | bytes 786440 | tf_op jit(solution)/shard_map/ppermute | solution.py:364
  5.0 1.5 %collective-permute-start.1 = (bf16[96,512]{1,0:T(8,128)(2,1)S(1)}, bf16[96,512]{1,0:T(8,128)(2,1)S(1)}, u32[]{:S(2)}, u32[]{:S(2)}) collective-permute-start(bf16[96,512]{1,0:T(8,128)(2,1)S(1)} %get-tuple-element.45.sent), channel_id=1, source_target_pairs={{0,8},{4,12},{8,0},{12,4},{16,24},{20,28},{24,16},{28,20},{32,40},... | collective-permute-start | bytes 294920 | tf_op jit(solution)/shard_map/across_one/ppermute | solution.py:311
  6.6 2.2 %early_kernel.1 = (bf16[256,512]{1,0:T(8,128)(2,1)S(1)}, f32[256,256]{1,0:T(8,128)S(1)}, f32[8,512]{1,0:T(8,128)S(1)}, f32[256,256]{1,0:T(8,128)S(1)}, f32[8,512]{1,0:T(8,128)S(1)}) custom-call(f32[32,128]{1,0:T(8,128)S(1)} %bias_kernel.1.gate, bf16[512,1024]{1,0:T(8,128)(2,1)S(1)} %copy-done, bf16[1024,256]{1,0:T(8,128)(2,1)S(1)} %copy-done.2, ...), custom_call_target="tpu_custom_call" | custom-call | flops 1000000 | bytes 1000 | tf_op jit(solution)/shard_map/early_kernel/pallas_call | solution.py:298
  8.8 0.6 %collective-permute-start.4 = (bf16[16,512]{1,0:T(8,128)(2,1)S(1)}, bf16[16,512]{1,0:T(8,128)(2,1)S(1)}, u32[]{:S(2)}, u32[]{:S(2)}) collective-permute-start(bf16[16,512]{1,0:T(8,128)(2,1)S(1)} %mirror_kernel.1.refs_5_), channel_id=1, source_target_pairs={{4,196},{12,204},{20,212},{28,220},{36,228},{44,236},{52,244},{60,... | collective-permute-start | bytes 49160 | tf_op jit(solution)/shard_map/planes_mirror/ppermute | solution.py:311
  9.8 2.8 %collective-permute-done.4.got = bf16[16,512]{1,0:T(8,128)(2,1)S(1)} collective-permute-done((bf16[16,512]{1,0:T(8,128)(2,1)S(1)}, bf16[16,512]{1,0:T(8,128)(2,1)S(1)}, u32[]{:S(2)}, u32[]{:S(2)}) %collective-permute-start.4) | collective-permute-done | bytes 16416 | tf_op jit(solution)/shard_map/planes_mirror/ppermute | solution.py:311
  13.2 3.0 %collective-permute-start.2 = (bf16[64,512]{1,0:T(8,128)(2,1)S(1)}, bf16[64,512]{1,0:T(8,128)(2,1)S(1)}, u32[]{:S(2)}, u32[]{:S(2)}) collective-permute-start(bf16[64,512]{1,0:T(8,128)(2,1)S(1)} %near_join_kernel.1), channel_id=1, source_target_pairs={{0,16},{4,20},{8,24},{12,28},{16,0},{20,4},{24,8},{28,12},{32,48},... | collective-permute-start | bytes 196616 | tf_op jit(solution)/shard_map/across_two/ppermute | solution.py:311
  17.1 1.9 %collective-permute-done.2.second = bf16[64,512]{1,0:T(8,128)(2,1)S(1)} collective-permute-done((bf16[64,512]{1,0:T(8,128)(2,1)S(1)}, bf16[64,512]{1,0:T(8,128)(2,1)S(1)}, u32[]{:S(2)}, u32[]{:S(2)}) %collective-permute-start.2) | collective-permute-done | bytes 65568 | tf_op jit(solution)/shard_map/across_two/ppermute | solution.py:311
  19.0 2.2 %collective-permute-start.3 = (bf16[128,512]{1,0:T(8,128)(2,1)S(1)}, bf16[128,512]{1,0:T(8,128)(2,1)S(1)}, u32[]{:S(2)}, u32[]{:S(2)}) collective-permute-start(bf16[128,512]{1,0:T(8,128)(2,1)S(1)} %plane_join_kernel.1), channel_id=1, source_target_pairs={{0,4},{4,0},{8,12},{12,8},{16,20},{20,16},{24,28},{28,24},{32,36},... | collective-permute-start | bytes 393224 | tf_op jit(solution)/shard_map/swap_near/ppermute | solution.py:311
  21.6 1.9 %collective-permute-start.8 = (bf16[96,512]{1,0:T(8,128)(2,1)S(1)}, bf16[96,512]{1,0:T(8,128)(2,1)S(1)}, u32[]{:S(2)}, u32[]{:S(2)}) collective-permute-start(bf16[96,512]{1,0:T(8,128)(2,1)S(1)} %far_join_kernel.1.a), channel_id=1, source_target_pairs={{4,12},{12,20},{20,28},{28,4},{36,44},{44,52},{52,60},{60,36},{68,... | collective-permute-start | bytes 294920 | tf_op jit(solution)/shard_map/along/ppermute | solution.py:311
  23.7 1.9 %plane_kernel.1 = (f32[256,256]{1,0:T(8,128)S(1)}, f32[8,512]{1,0:T(8,128)S(1)}, f32[256,256]{1,0:T(8,128)S(1)}, f32[8,512]{1,0:T(8,128)S(1)}) custom-call(f32[32,128]{1,0:T(8,128)S(1)} %bias_kernel.1.gate, bf16[256,512]{1,0:T(8,128)(2,1)S(1)} %get-tuple-element.41.qt, f32[256,256]{1,0:T(8,128)S(1)} %get-tuple-element.42.acc0, ...), custom_call_target="tpu_custom_call" | custom-call | flops 1000000 | bytes 1000 | tf_op jit(solution)/shard_map/plane_kernel/pallas_call | solution.py:298
  26.1 1.1 %collective-permute-done.8.b = bf16[96,512]{1,0:T(8,128)(2,1)S(1)} collective-permute-done((bf16[96,512]{1,0:T(8,128)(2,1)S(1)}, bf16[96,512]{1,0:T(8,128)(2,1)S(1)}, u32[]{:S(2)}, u32[]{:S(2)}) %collective-permute-start.8) | collective-permute-done | bytes 98336 | tf_op jit(solution)/shard_map/along/ppermute | solution.py:311
  27.2 1.1 %collective-permute-done.9.c = bf16[96,512]{1,0:T(8,128)(2,1)S(1)} collective-permute-done((bf16[96,512]{1,0:T(8,128)(2,1)S(1)}, bf16[96,512]{1,0:T(8,128)(2,1)S(1)}, u32[]{:S(2)}, u32[]{:S(2)}) %collective-permute-start.9) | collective-permute-done | bytes 98336 | tf_op jit(solution)/shard_map/along/ppermute | solution.py:311
  28.6 2.2 %collective-permute-start.15 = (bf16[256,512]{1,0:T(8,128)(2,1)S(1)}, bf16[256,512]{1,0:T(8,128)(2,1)S(1)}, u32[]{:S(2)}, u32[]{:S(2)}) collective-permute-start(bf16[256,512]{1,0:T(8,128)(2,1)S(1)} %get-tuple-element.58), channel_id=1, source_target_pairs={{0,3},{3,0},{1,2},{2,1},{4,7},{7,4},{5,6},{6,5},{8,11},{11,8},{9,1... | collective-permute-start | bytes 786440 | tf_op jit(solution)/shard_map/ppermute | solution.py:393
  30.8 1.1 %far_kernel.2.mine_att.after = bf16[256,256]{1,0:T(8,128)(2,1)S(1)} custom-call(f32[32,128]{1,0:T(8,128)S(1)} %bias_kernel.1.gate, bf16[256,512]{1,0:T(8,128)(2,1)S(1)} %get-tuple-element.41.qt, f32[256,256]{1,0:T(8,128)S(1)} %get-tuple-element.49.acc, f32[8,512]{1,0:T(8,128)S(1)} %get-tuple-element.50.after.ml, bf16[384,512]{1,0:T(8,128)(2,1)S(1)} %row_join_kernel.1.mine, ...), custom_call_target="tpu_custom_call" | custom-call | flops 1000000 | bytes 1000 | tf_op jit(solution)/shard_map/far_kernel/pallas_call | solution.py:298
  31.9 0.8 %collective-permute-start.12 = (bf16[256,256]{1,0:T(8,128)(2,1)S(1)}, bf16[256,256]{1,0:T(8,128)(2,1)S(1)}, u32[]{:S(2)}, u32[]{:S(2)}) collective-permute-start(bf16[256,256]{1,0:T(8,128)(2,1)S(1)} %far_kernel.2.mine_att.after), channel_id=1, source_target_pairs={{0,1},{1,0},{2,3},{3,2},{4,5},{5,4},{6,7},{7,6},{8,9},{9,8},{10,11... | collective-permute-start | bytes 393224 | tf_op jit(solution)/shard_map/ppermute | solution.py:418
  32.6 1.1 %far_kernel.3.mine_att = bf16[256,256]{1,0:T(8,128)(2,1)S(1)} custom-call(f32[32,128]{1,0:T(8,128)S(1)} %bias_kernel.1.gate, bf16[256,512]{1,0:T(8,128)(2,1)S(1)} %get-tuple-element.41.qt, f32[256,256]{1,0:T(8,128)S(1)} %get-tuple-element.56.acc, f32[8,512]{1,0:T(8,128)S(1)} %get-tuple-element.57.ml, bf16[384,512]{1,0:T(8,128)(2,1)S(1)} %row_join_kernel.1.mine, ...), custom_call_target="tpu_custom_call" | custom-call | flops 1000000 | bytes 1000 | tf_op jit(solution)/shard_map/far_kernel/pallas_call | solution.py:298
  33.7 2.2 %collective-permute-start.14 = (bf16[256,256]{1,0:T(8,128)(2,1)S(1)}, bf16[256,256]{1,0:T(8,128)(2,1)S(1)}, u32[]{:S(2)}, u32[]{:S(2)}) collective-permute-start(bf16[256,256]{1,0:T(8,128)(2,1)S(1)} %far_kernel.3.mine_att), channel_id=1, source_target_pairs={{0,3},{3,0},{1,2},{2,1},{4,7},{7,4},{5,6},{6,5},{8,11},{11,8},{9,1... | collective-permute-start | bytes 393224 | tf_op jit(solution)/shard_map/ppermute | solution.py:418
  35.8 1.5 %collective-permute-done.12.peer_att = bf16[256,256]{1,0:T(8,128)(2,1)S(1)} collective-permute-done((bf16[256,256]{1,0:T(8,128)(2,1)S(1)}, bf16[256,256]{1,0:T(8,128)(2,1)S(1)}, u32[]{:S(2)}, u32[]{:S(2)}) %collective-permute-start.12) | collective-permute-done | bytes 131104 | tf_op jit(solution)/shard_map/ppermute | solution.py:418
  37.6 1.8 %collective-permute-start.13 = (bf16[256,256]{1,0:T(8,128)(2,1)S(1)}, bf16[256,256]{1,0:T(8,128)(2,1)S(1)}, u32[]{:S(2)}, u32[]{:S(2)}) collective-permute-start(bf16[256,256]{1,0:T(8,128)(2,1)S(1)} %get-tuple-element.55), channel_id=1, source_target_pairs={{0,3},{3,0},{1,2},{2,1},{4,7},{7,4},{5,6},{6,5},{8,11},{11,8},{9,1... | collective-permute-start | bytes 393224 | tf_op jit(solution)/shard_map/ppermute | solution.py:425
  39.5 2.0 %collective-permute-done.14.peer_att = bf16[256,256]{1,0:T(8,128)(2,1)S(1)} collective-permute-done((bf16[256,256]{1,0:T(8,128)(2,1)S(1)}, bf16[256,256]{1,0:T(8,128)(2,1)S(1)}, u32[]{:S(2)}, u32[]{:S(2)}) %collective-permute-start.14) | collective-permute-done | bytes 131104 | tf_op jit(solution)/shard_map/ppermute | solution.py:418
  41.9 2.0 %collective-permute-done.13 = bf16[256,256]{1,0:T(8,128)(2,1)S(1)} collective-permute-done((bf16[256,256]{1,0:T(8,128)(2,1)S(1)}, bf16[256,256]{1,0:T(8,128)(2,1)S(1)}, u32[]{:S(2)}, u32[]{:S(2)}) %collective-permute-start.13) | collective-permute-done | bytes 131104 | tf_op jit(solution)/shard_map/ppermute | solution.py:425
  43.9 2.9 %collective-permute-done.16 = bf16[256,256]{1,0:T(8,128)(2,1)S(1)} collective-permute-done((bf16[256,256]{1,0:T(8,128)(2,1)S(1)}, bf16[256,256]{1,0:T(8,128)(2,1)S(1)}, u32[]{:S(2)}, u32[]{:S(2)}) %collective-permute-start.16) | collective-permute-done | bytes 131104 | tf_op jit(solution)/shard_map/ppermute | solution.py:425
  46.9 0.7 %pad_maximum_fusion = bf16[512,256]{1,0:T(8,128)(2,1)} fusion(bf16[256,256]{1,0:T(8,128)(2,1)S(1)} %add_convert_fusion, bf16[256,256]{1,0:T(8,128)(2,1)S(1)} %add_convert_fusion.1), kind=kLoop, calls=%fused_computation | loop fusion | flops 524288 | bytes 524288 | tf_op jit(solution)/shard_map/concatenate | solution.py:426
  (37 shorter events, 4.3 us)
Async XLA Ops:
  0.0 6.6 %copy-start = (bf16[512,1024]{1,0:T(8,128)(2,1)S(1)}, bf16[512,1024]{1,0:T(8,128)(2,1)}, u32[]{:S(2)}) copy-start(bf16[512,1024]{1,0:T(8,128)(2,1)} %tok.3) | copy-start | bytes 3145732
  0.0 6.6 %copy-start.2 = (bf16[1024,256]{1,0:T(8,128)(2,1)S(1)}, bf16[1024,256]{1,0:T(8,128)(2,1)}, u32[]{:S(2)}) copy-start(bf16[1024,256]{1,0:T(8,128)(2,1)} %wq.3) | copy-start | bytes 1572868
  3.2 3.3 %copy-start.3 = (s32[4,16]{1,0:T(4,128)S(1)}, s32[4,16]{1,0:T(4,128)}, u32[]{:S(2)}) copy-start(s32[4,16]{1,0:T(4,128)} %gate.1) | copy-start | bytes 772
  3.2 5.6 %collective-permute-start = (bf16[176,512]{1,0:T(8,128)(2,1)S(1)}, bf16[176,512]{1,0:T(8,128)(2,1)S(1)}, u32[]{:S(2)}, u32[]{:S(2)}) collective-permute-start(bf16[176,512]{1,0:T(8,128)(2,1)S(1)} %get-tuple-element.40.share), channel_id=1, source_target_pairs={{0,4},{4,0},{8,12},{12,8},{16,20},{20,16},{24,28},{28,24},{32,36},... | collective-permute-start | bytes 540680 | tf_op jit(solution)/shard_map/swap_share/ppermute | solution.py:311
  3.3 17.9 %collective-permute-start.7 = (bf16[256,512]{1,0:T(8,128)(2,1)S(1)}, bf16[256,512]{1,0:T(8,128)(2,1)S(1)}, u32[]{:S(2)}, u32[]{:S(2)}) collective-permute-start(bf16[256,512]{1,0:T(8,128)(2,1)S(1)} %get-tuple-element.51), channel_id=1, source_target_pairs={{0,1},{1,0},{2,3},{3,2},{4,5},{5,4},{6,7},{7,6},{8,9},{9,8},{10,11... | collective-permute-start | bytes 786440 | tf_op jit(solution)/shard_map/ppermute | solution.py:364
  5.0 4.8 %collective-permute-start.1 = (bf16[96,512]{1,0:T(8,128)(2,1)S(1)}, bf16[96,512]{1,0:T(8,128)(2,1)S(1)}, u32[]{:S(2)}, u32[]{:S(2)}) collective-permute-start(bf16[96,512]{1,0:T(8,128)(2,1)S(1)} %get-tuple-element.45.sent), channel_id=1, source_target_pairs={{0,8},{4,12},{8,0},{12,4},{16,24},{20,28},{24,16},{28,20},{32,40},... | collective-permute-start | bytes 294920 | tf_op jit(solution)/shard_map/across_one/ppermute | solution.py:311
  8.8 3.8 %collective-permute-start.4 = (bf16[16,512]{1,0:T(8,128)(2,1)S(1)}, bf16[16,512]{1,0:T(8,128)(2,1)S(1)}, u32[]{:S(2)}, u32[]{:S(2)}) collective-permute-start(bf16[16,512]{1,0:T(8,128)(2,1)S(1)} %mirror_kernel.1.refs_5_), channel_id=1, source_target_pairs={{4,196},{12,204},{20,212},{28,220},{36,228},{44,236},{52,244},{60,... | collective-permute-start | bytes 49160 | tf_op jit(solution)/shard_map/planes_mirror/ppermute | solution.py:311
  12.7 3.9 %collective-permute-start.5 = (bf16[32,512]{1,0:T(8,128)(2,1)S(1)}, bf16[32,512]{1,0:T(8,128)(2,1)S(1)}, u32[]{:S(2)}, u32[]{:S(2)}) collective-permute-start(bf16[32,512]{1,0:T(8,128)(2,1)S(1)} %two_kernel.1.sent), channel_id=1, source_target_pairs={{4,68},{12,76},{20,84},{28,92},{36,100},{44,108},{52,116},{60,124}... | collective-permute-start | bytes 98312 | tf_op jit(solution)/shard_map/planes_two/ppermute | solution.py:311
  13.2 5.8 %collective-permute-start.2 = (bf16[64,512]{1,0:T(8,128)(2,1)S(1)}, bf16[64,512]{1,0:T(8,128)(2,1)S(1)}, u32[]{:S(2)}, u32[]{:S(2)}) collective-permute-start(bf16[64,512]{1,0:T(8,128)(2,1)S(1)} %near_join_kernel.1), channel_id=1, source_target_pairs={{0,16},{4,20},{8,24},{12,28},{16,0},{20,4},{24,8},{28,12},{32,48},... | collective-permute-start | bytes 196616 | tf_op jit(solution)/shard_map/across_two/ppermute | solution.py:311
  16.6 4.8 %collective-permute-start.6 = (bf16[64,512]{1,0:T(8,128)(2,1)S(1)}, bf16[64,512]{1,0:T(8,128)(2,1)S(1)}, u32[]{:S(2)}, u32[]{:S(2)}) collective-permute-start(bf16[64,512]{1,0:T(8,128)(2,1)S(1)} %joint_kernel.1.sent), channel_id=1, source_target_pairs={{4,36},{12,44},{20,52},{28,60},{36,4},{44,12},{52,20},{60,28},{68,... | collective-permute-start | bytes 196616 | tf_op jit(solution)/shard_map/planes_one/ppermute | solution.py:311
  19.0 4.7 %collective-permute-start.3 = (bf16[128,512]{1,0:T(8,128)(2,1)S(1)}, bf16[128,512]{1,0:T(8,128)(2,1)S(1)}, u32[]{:S(2)}, u32[]{:S(2)}) collective-permute-start(bf16[128,512]{1,0:T(8,128)(2,1)S(1)} %plane_join_kernel.1), channel_id=1, source_target_pairs={{0,4},{4,0},{8,12},{12,8},{16,20},{20,16},{24,28},{28,24},{32,36},... | collective-permute-start | bytes 393224 | tf_op jit(solution)/shard_map/swap_near/ppermute | solution.py:311
  21.4 4.7 %collective-permute-start.10 = (bf16[96,512]{1,0:T(8,128)(2,1)S(1)}, bf16[96,512]{1,0:T(8,128)(2,1)S(1)}, u32[]{:S(2)}, u32[]{:S(2)}) collective-permute-start(bf16[96,512]{1,0:T(8,128)(2,1)S(1)} %far_join_kernel.1.a), channel_id=1, source_target_pairs={{4,20},{12,28},{20,4},{28,12},{36,52},{44,60},{52,36},{60,44},{68,... | collective-permute-start | bytes 294920 | tf_op jit(solution)/shard_map/along/ppermute | solution.py:311
  21.6 5.6 %collective-permute-start.8 = (bf16[96,512]{1,0:T(8,128)(2,1)S(1)}, bf16[96,512]{1,0:T(8,128)(2,1)S(1)}, u32[]{:S(2)}, u32[]{:S(2)}) collective-permute-start(bf16[96,512]{1,0:T(8,128)(2,1)S(1)} %far_join_kernel.1.a), channel_id=1, source_target_pairs={{4,12},{12,20},{20,28},{28,4},{36,44},{44,52},{52,60},{60,36},{68,... | collective-permute-start | bytes 294920 | tf_op jit(solution)/shard_map/along/ppermute | solution.py:311
  23.6 4.7 %collective-permute-start.9 = (bf16[96,512]{1,0:T(8,128)(2,1)S(1)}, bf16[96,512]{1,0:T(8,128)(2,1)S(1)}, u32[]{:S(2)}, u32[]{:S(2)}) collective-permute-start(bf16[96,512]{1,0:T(8,128)(2,1)S(1)} %far_join_kernel.1.a), channel_id=1, source_target_pairs={{4,28},{12,4},{20,12},{28,20},{36,60},{44,36},{52,44},{60,52},{68,... | collective-permute-start | bytes 294920 | tf_op jit(solution)/shard_map/along/ppermute | solution.py:311
  28.3 2.5 %collective-permute-start.11 = (bf16[384,512]{1,0:T(8,128)(2,1)S(1)}, bf16[384,512]{1,0:T(8,128)(2,1)S(1)}, u32[]{:S(2)}, u32[]{:S(2)}) collective-permute-start(bf16[384,512]{1,0:T(8,128)(2,1)S(1)} %row_join_kernel.1.mine), channel_id=1, source_target_pairs={{0,4},{4,0},{8,12},{12,8},{16,20},{20,16},{24,28},{28,24},{32,36},... | collective-permute-start | bytes 1179656 | tf_op jit(solution)/shard_map/swap_far/ppermute | solution.py:311
  28.6 10.9 %collective-permute-start.15 = (bf16[256,512]{1,0:T(8,128)(2,1)S(1)}, bf16[256,512]{1,0:T(8,128)(2,1)S(1)}, u32[]{:S(2)}, u32[]{:S(2)}) collective-permute-start(bf16[256,512]{1,0:T(8,128)(2,1)S(1)} %get-tuple-element.58), channel_id=1, source_target_pairs={{0,3},{3,0},{1,2},{2,1},{4,7},{7,4},{5,6},{6,5},{8,11},{11,8},{9,1... | collective-permute-start | bytes 786440 | tf_op jit(solution)/shard_map/ppermute | solution.py:393
  31.9 5.5 %collective-permute-start.12 = (bf16[256,256]{1,0:T(8,128)(2,1)S(1)}, bf16[256,256]{1,0:T(8,128)(2,1)S(1)}, u32[]{:S(2)}, u32[]{:S(2)}) collective-permute-start(bf16[256,256]{1,0:T(8,128)(2,1)S(1)} %far_kernel.2.mine_att.after), channel_id=1, source_target_pairs={{0,1},{1,0},{2,3},{3,2},{4,5},{5,4},{6,7},{7,6},{8,9},{9,8},{10,11... | collective-permute-start | bytes 393224 | tf_op jit(solution)/shard_map/ppermute | solution.py:418
  32.6 4.7 %copy-start.1 = (bf16[256,1024]{1,0:T(8,128)(2,1)S(1)}, bf16[256,1024]{1,0:T(8,128)(2,1)}, u32[]{:S(2)}) copy-start(bf16[256,1024]{1,0:T(8,128)(2,1)} %mine_w.3) | copy-start | bytes 1572868
  33.7 7.8 %collective-permute-start.14 = (bf16[256,256]{1,0:T(8,128)(2,1)S(1)}, bf16[256,256]{1,0:T(8,128)(2,1)S(1)}, u32[]{:S(2)}, u32[]{:S(2)}) collective-permute-start(bf16[256,256]{1,0:T(8,128)(2,1)S(1)} %far_kernel.3.mine_att), channel_id=1, source_target_pairs={{0,3},{3,0},{1,2},{2,1},{4,7},{7,4},{5,6},{6,5},{8,11},{11,8},{9,1... | collective-permute-start | bytes 393224 | tf_op jit(solution)/shard_map/ppermute | solution.py:418
  37.6 6.3 %collective-permute-start.13 = (bf16[256,256]{1,0:T(8,128)(2,1)S(1)}, bf16[256,256]{1,0:T(8,128)(2,1)S(1)}, u32[]{:S(2)}, u32[]{:S(2)}) collective-permute-start(bf16[256,256]{1,0:T(8,128)(2,1)S(1)} %get-tuple-element.55), channel_id=1, source_target_pairs={{0,3},{3,0},{1,2},{2,1},{4,7},{7,4},{5,6},{6,5},{8,11},{11,8},{9,1... | collective-permute-start | bytes 393224 | tf_op jit(solution)/shard_map/ppermute | solution.py:425
  41.8 5.1 %collective-permute-start.16 = (bf16[256,256]{1,0:T(8,128)(2,1)S(1)}, bf16[256,256]{1,0:T(8,128)(2,1)S(1)}, u32[]{:S(2)}, u32[]{:S(2)}) collective-permute-start(bf16[256,256]{1,0:T(8,128)(2,1)S(1)} %get-tuple-element.60), channel_id=1, source_target_pairs={{0,1},{1,0},{2,3},{3,2},{4,5},{5,4},{6,7},{7,6},{8,9},{9,8},{10,11... | collective-permute-start | bytes 393224 | tf_op jit(solution)/shard_map/ppermute | solution.py:425
